TPU v7x, 32 devices: a whole 2x2x4 slice. The times are simulated.
32 devices in a mesh: split: 4 (over x, core), tensor: 8 (over z, y).
Axes of the slice: x: 2, y: 2, z: 4, core: 2. Of those that a mesh axis runs over, the one named last changes fastest.
Arguments:
- three_centre: bfloat16 [256, 256, 128], P('split', 'tensor'), may hold values from -6 to 6
- green_occ: bfloat16 [256, 256], P('split'), may hold values from -0.375 to 0.375
- green_virt: bfloat16 [256, 256], P('tensor'), may hold values from -0.375 to 0.375
- occ_mask: int32 [8, 8], replicated, may hold values 0 or 1
- virt_mask: int32 [8, 8], replicated, may hold values 0 or 1
Outputs:
- polar: float32 [128, 128], P('split')
All inputs are finite; a program needn't handle non-finite values.
Results may differ from a plain program's by a relative error of at most 0.008.
Values may be sent and summed in bfloat16 or wider, within the bound.
No kernel may reach another device: no remote copies, remote signals or barrier semaphores. Data moves between devices by JAX's collectives and lax.ppermute only.
A program may use at most 128 MiB of HBM per device.

v0:
```python
import jax
import jax.numpy as jnp
from jax import lax
from jax.sharding import PartitionSpec as P


def widen(mask, block):
    return jnp.repeat(jnp.repeat(mask, block, axis=0), block, axis=1)


def local(three_centre, green_occ, green_virt, occ_mask, virt_mask):
    nao = green_occ.shape[1]
    block = nao // occ_mask.shape[0]
    own_rows = three_centre.shape[0]
    own_cols = three_centre.shape[1]
    split_index = lax.axis_index("split")
    tensor_index = lax.axis_index("tensor")
    occ_rows = lax.dynamic_slice_in_dim(
        occ_mask, split_index * (own_rows // block), own_rows // block, 0
    )
    occ = jnp.where(widen(occ_rows, block) > 0, green_occ, jnp.zeros_like(green_occ))
    virt_rows = lax.dynamic_slice_in_dim(
        virt_mask, tensor_index * (own_cols // block), own_cols // block, 0
    )
    virt_local = jnp.where(widen(virt_rows, block) > 0, green_virt, jnp.zeros_like(green_virt))
    virt = lax.all_gather(virt_local, "tensor", axis=0, tiled=True)
    first = jnp.einsum("mn,mlp->nlp", occ, three_centre, preferred_element_type=jnp.float32).astype(
        jnp.bfloat16
    )
    second = jnp.einsum(
        "ls,nlp->nsp",
        virt,
        lax.all_to_all(first, "tensor", split_axis=0, concat_axis=1, tiled=True),
        preferred_element_type=jnp.float32,
    ).astype(jnp.bfloat16)
    summed = lax.psum_scatter(
        second.astype(jnp.float32).astype(jnp.bfloat16), "split", scatter_dimension=1, tiled=True
    ).astype(jnp.float32)
    upper = summed.astype(jnp.bfloat16)
    lower = (summed - upper.astype(jnp.float32)).astype(jnp.bfloat16)
    partial_value = jnp.einsum(
        "nsp,snq->pq", upper, three_centre, preferred_element_type=jnp.float32
    )
    partial_value = partial_value + jnp.einsum(
        "nsp,snq->pq", lower, three_centre, preferred_element_type=jnp.float32
    )
    whole = lax.psum(partial_value, "tensor")
    result = lax.psum_scatter(whole, "split", scatter_dimension=0, tiled=True)
    return result / nao


def solution(mesh):
    return jax.shard_map(
        local,
        mesh=mesh,
        in_specs=(P("split", "tensor", None), P("split", None), P("tensor", None), P(), P()),
        out_specs=P("split", None),
        check_vma=False,
    )
```

profile of v0, /device:TPU:0, one launch (start us, length us, event | category | flops | bytes accessed | tf_op | source)
XLA Modules:
  0.0 189.4 jit_solution(6730928338945920521)
XLA Ops:
  6.5 0.0 copy-start
  6.5 0.8 dynamic-slice_compare_fusion
  7.3 0.1 copy.43
  7.4 0.1 broadcast_in_dim.18
  7.5 0.1 gt.30
  7.6 0.9 copy.44
  8.5 0.0 copy-done
  8.5 0.7 convolution_convert_fusion
  9.2 2.7 %copy.47 = bf16[256,32,128]{2,1,0:T(8,128)(2,1)} copy(bf16[256,32,128]{2,0,1:T(8,128)(2,1)S(1)} %convolution_convert_fusion) | data formatting | bytes 4194304 | tf_op jit(solution)/shard_map/convert_element_type | solution.py:27
  11.9 0.0 copy-start.1
  11.9 7.4 %all-to-all-start = ((bf16[256,32,128]{2,1,0:T(8,128)(2,1)}), bf16[256,32,128]{2,1,0:T(8,128)(2,1)S(1)}, u32[]{:S(2)}, u32[]{:S(2)}) async-start(bf16[256,32,128]{2,1,0:T(8,128)(2,1)} %copy.47), calls=%async_computation | async-start | bytes 4194304 | tf_op jit(solution)/shard_map/all_to_all | solution.py:33
  19.3 0.0 reduce-scatter.3.cloned.1.call-start
  19.3 0.7 compare_bitcast_fusion
  20.0 0.1 broadcast_in_dim.21
  20.1 0.1 gt.35
  20.2 0.0 copy-done.1
  20.2 67.5 %all_gather.3 = bf16[256,256]{1,0:T(8,128)(2,1)S(1)} all-gather(bf16[32,256]{1,0:T(8,128)(2,1)S(1)} %broadcast_select_fusion), channel_id=1, replica_groups=mesh['split'=4,'tensor'=8] {'tensor'}, dimensions={0}, use_global_device_ids=true | all-gather | bytes 147456 | tf_op jit(solution)/shard_map/all_gather | solution.py:26
  87.7 0.0 all-to-all-done
  87.7 0.6 copy.48
  88.3 0.8 convert_bitcast_fusion
  89.1 3.1 %copy.50 = bf16[32,256,128]{2,0,1:T(8,128)(2,1)} copy(bf16[32,256,128]{1,2,0:T(8,128)(2,1)S(1)} %convert_bitcast_fusion) | data formatting | bytes 4194304 | tf_op jit(solution)/shard_map/convert_element_type | solution.py:35
  92.2 0.0 reduce-scatter.3.cloned.1.call-update
  92.2 0.0 reduce-scatter.5.cloned.1.call-start
  92.3 30.6 %reduce-scatter.3.cloned.1.call-done = bf16[32,64,128]{2,0,1:T(8,128)(2,1)} async-done(((bf16[32,256,128]{2,0,1:T(8,128)(2,1)}), bf16[32,64,128]{2,0,1:T(8,128)(2,1)}) %reduce-scatter.3.cloned.1.call-update) | async-done | bytes 524304 | tf_op jit(solution)/shard_map/reduce_scatter | solution.py:36
  122.9 0.0 copy-start.2
  122.9 1.5 convolution_bitcast_fusion
  124.3 0.0 copy-done.2
  124.4 1.0 fusion
  125.3 0.0 reduce-scatter.5.cloned.1.call-update
  125.3 19.6 %reduce-scatter.5.cloned.1.call-done = f32[32,128]{1,0:T(8,128)} async-done(((f32[128,128]{1,0:T(8,128)}), f32[32,128]{1,0:T(8,128)}) %reduce-scatter.5.cloned.1.call-update) | async-done | bytes 16400 | tf_op jit(solution)/shard_map/reduce_scatter | solution.py:48
  144.9 37.1 %psum.8 = f32[32,128]{1,0:T(8,128)S(1)} all-reduce(f32[32,128]{1,0:T(8,128)} %reduce-scatter.5.cloned.1.call-done), channel_id=1, replica_groups=mesh['split'=4,'tensor'=8] {'tensor'}, use_global_device_ids=true, to_apply=%region_1.2 | all-reduce | flops 4096 | bytes 32768 | tf_op jit(solution)/shard_map/psum | solution.py:47
  182.0 0.6 broadcast_multiply_fusion
  (2 shorter events, 0.0 us)
Async XLA Ops:
  6.5 1.9 %copy-start = (bf16[64,32,128]{2,1,0:T(8,128)(2,1)S(1)}, bf16[64,32,128]{2,1,0:T(8,128)(2,1)}, u32[]{:S(2)}) copy-start(bf16[64,32,128]{2,1,0:T(8,128)(2,1)} %param.5) | copy-start | bytes 1572868
  11.9 8.3 %copy-start.1 = (bf16[32,256]{1,0:T(8,128)(2,1)S(1)}, bf16[32,256]{1,0:T(8,128)(2,1)}, u32[]{:S(2)}) copy-start(bf16[32,256]{1,0:T(8,128)(2,1)} %param.7) | copy-start | bytes 49156
  11.9 75.8 %all-to-all-start = ((bf16[256,32,128]{2,1,0:T(8,128)(2,1)}), bf16[256,32,128]{2,1,0:T(8,128)(2,1)S(1)}, u32[]{:S(2)}, u32[]{:S(2)}) async-start(bf16[256,32,128]{2,1,0:T(8,128)(2,1)} %copy.47), calls=%async_computation | async-start | bytes 4194304 | tf_op jit(solution)/shard_map/all_to_all | solution.py:33
  19.3 103.6 %reduce-scatter.3.cloned.1.call-start = ((), (), s32[]{:S(2)}) async-start(), calls=%async_computation.3 | async-start | bytes 2621440 | tf_op jit(solution)/shard_map/reduce_scatter | solution.py:36
  92.2 52.7 %reduce-scatter.5.cloned.1.call-start = ((), (), s32[]{:S(2)}) async-start(), calls=%async_computation.4 | async-start | bytes 81920 | tf_op jit(solution)/shard_map/reduce_scatter | solution.py:48
  122.9 1.5 copy-start.2
Sparse Core Ops, SparseCore 0:
  92.3 30.4 reduce-scatter.2
  125.5 19.4 reduce-scatter.4
where the time goes:
time: 190 us; the launch traced here: 189 us
  blocking collectives  105 us (55%)
  waiting for transfers between devices  50.2 us (26%)
  between operations  13.5 us (7%)
  local copies, waits for them, and re-layouts  7.74 us (4%)
  starting transfers between devices  7.49 us (4%)
  matrix products  3.88 us (2%)
  other arithmetic  2.08 us (1%)
    all_gather x1, blocking collectives, local(): virt = lax.all_gather(virt_local, 'tensor', axis=0, tiled=True)  67.5 us
    psum x1, blocking collectives, local(): whole = lax.psum(partial_value, 'tensor')  37.1 us
    reduce_scatter x1, waiting for transfers between devices, local(): lax.psum_scatter(second.astype(jnp.float32).astype(jnp.bfloat16), 'split'...  30.6 us
    reduce_scatter x1, waiting for transfers between devices, local(): result = lax.psum_scatter(whole, 'split', scatter_dimension=0, tiled=True)  19.6 us
    all_to_all x1, starting transfers between devices, local(): lax.all_to_all(first, 'tensor', split_axis=0, concat_axis=1, tiled=True)  7.42 us
  transfers between devices with their start and end apart: 3, of which 2 were waited for; matrix products, arithmetic and copies ran while one was open for 0% of the time, Pallas kernels for 0%

commit v1 on v0

v1 whole, which is shorter than its diff:
```python
import functools

import jax
import jax.numpy as jnp
from jax import lax
from jax.experimental import pallas as pl
from jax.experimental.pallas import tpu as pltpu
from jax.sharding import PartitionSpec as P

VMEM_LIMIT = 48 * 1024 * 1024


def swap_blocks(x, width, flag):
    cols = x.shape[1]
    order = []
    for start in range(0, cols, 2 * width):
        order += [x[:, start + width:start + 2 * width], x[:, start:start + width]]
    return jnp.where(flag, jnp.concatenate(order, axis=1), x)


def xor_blocks(x, width, index):
    blocks = x.shape[1] // width
    bit = 1
    while bit < blocks:
        x = swap_blocks(x, width * bit, (index & bit) != 0)
        bit *= 2
    return x


def screened(green, mask_ref, first_row, block):
    rows, cols = green.shape
    column = lax.broadcasted_iota(jnp.int32, (block, cols), 1) // block
    parts = []
    for r in range(rows // block):
        keep = jnp.zeros((block, cols), jnp.int32)
        for c in range(cols // block):
            keep = jnp.where(column == c, mask_ref[first_row + r, c], keep)
        part = green[r * block:(r + 1) * block].astype(jnp.float32)
        parts.append(jnp.where(keep > 0, part, 0.0))
    return jnp.concatenate(parts, axis=0) if len(parts) > 1 else parts[0]


def pack_kernel(n_split, n_tensor, place, occ_mask, virt_mask, b_ref, occ_ref, virt_ref, *outs):
    s, t = place[0], place[1]
    cols, rows, naux = b_ref.shape
    width = naux // n_split
    group = cols // n_split
    block = occ_ref.shape[1] // occ_mask.shape[0]
    occ = screened(occ_ref[...], occ_mask, s * (rows // block), block)
    occ = xor_blocks(occ, cols, t).astype(jnp.bfloat16)
    virt = screened(virt_ref[...], virt_mask, t * (cols // block), block)
    outs[n_split][...] = xor_blocks(virt, rows, s).astype(jnp.bfloat16)
    for m in range(n_split):
        outs[m][:, group * naux:] = occ
    for l in range(group):
        for member in range(n_split):
            lanes = slice(member * width, (member + 1) * width)
            tile = jnp.concatenate([b_ref[j * group + l, :, lanes] for j in range(n_split)], axis=1)
            for m in range(n_split):

                @pl.when((s ^ m) == member)
                def _():
                    outs[m][:, l * naux:(l + 1) * naux] = tile


def first_kernel(n_split, n_tensor, width, *refs):
    packed, outs = refs[:n_split], refs[n_split:]
    whole = jnp.concatenate([p[...] for p in packed], axis=0)
    first = lax.dot_general(
        whole[:, width:], whole[:, :width], (((0,), (0,)), ((), ())), preferred_element_type=jnp.float32
    )
    rows = first.shape[0] // n_tensor
    for k in range(n_tensor):
        outs[k][...] = first[k * rows:(k + 1) * rows].astype(jnp.bfloat16)


def g_kernel(n_split, virt_ref, *refs):
    out = refs[n_split]
    for n in range(out.shape[0]):
        right = jnp.concatenate([r[n] for r in refs[:n_split]], axis=0)
        out[n] = jnp.dot(virt_ref[...], right, preferred_element_type=jnp.float32).astype(jnp.bfloat16)


def last_kernel(n_split, n_tensor, scale, g_ref, *refs):
    firsts, out = refs[:n_tensor], refs[n_tensor]
    rows = firsts[0].shape[0]
    naux = g_ref.shape[2]
    group = firsts[0].shape[1] // naux
    width = naux // n_split
    totals = [jnp.zeros((naux, naux), jnp.float32) for _ in range(n_split)]
    for k in range(n_tensor):
        left = jnp.concatenate([firsts[k][:, l * naux:(l + 1) * naux] for l in range(group)], axis=0)
        for j in range(n_split):
            start = (k * n_split + j) * group
            right = g_ref[start:start + group].reshape(group * rows, naux)
            totals[j] += lax.dot_general(
                left, right, (((0,), (0,)), ((), ())), preferred_element_type=jnp.float32
            )
    result = totals[0][:width]
    for j in range(1, n_split):
        result = result + totals[j][j * width:(j + 1) * width]
    out[...] = result * scale


def local(three_centre, green_occ, green_virt, occ_mask, virt_mask, *, n_split, n_tensor):
    rows, cols, naux = three_centre.shape
    nao = green_occ.shape[1]
    group = cols // n_split
    packed_width = group * naux
    count = n_split * n_tensor
    params = pltpu.CompilerParams(vmem_limit_bytes=VMEM_LIMIT)
    bf16 = jnp.bfloat16

    def exchange(x, split_bits=0, tensor_bits=0):
        bits = split_bits * n_tensor + tensor_bits
        return lax.ppermute(x, ("split", "tensor"), [(d, d ^ bits) for d in range(count)])

    place = jnp.stack([lax.axis_index("split"), lax.axis_index("tensor")]).astype(jnp.int32)
    basis = jnp.swapaxes(three_centre, 0, 1)
    smem = pl.BlockSpec(memory_space=pltpu.SMEM)
    vmem = pl.BlockSpec(memory_space=pltpu.VMEM)
    *packed, virt = pl.pallas_call(
        functools.partial(pack_kernel, n_split, n_tensor),
        out_shape=[jax.ShapeDtypeStruct((rows, packed_width + nao), bf16)] * n_split
        + [jax.ShapeDtypeStruct(green_virt.shape, bf16)],
        in_specs=[smem] * 3 + [vmem] * 3,
        out_specs=[vmem] * (n_split + 1),
        compiler_params=params,
    )(place, occ_mask, virt_mask, basis, green_occ, green_virt)
    packed = [packed[0]] + [exchange(packed[m], split_bits=m) for m in range(1, n_split)]

    held = {0: basis}
    bit = n_split // 2
    while bit:
        held.update({m | bit: exchange(x, split_bits=bit) for m, x in held.items()})
        bit //= 2

    bit = 1
    while bit < n_tensor:
        virt = jnp.concatenate([virt, exchange(virt, tensor_bits=bit)], axis=0)
        bit *= 2

    firsts = pl.pallas_call(
        functools.partial(first_kernel, n_split, n_tensor, packed_width),
        out_shape=[jax.ShapeDtypeStruct((cols, packed_width), bf16)] * n_tensor,
        in_specs=[vmem] * n_split,
        out_specs=[vmem] * n_tensor,
        compiler_params=params,
    )(*packed)
    firsts = [firsts[0]] + [exchange(firsts[k], tensor_bits=k) for k in range(1, n_tensor)]

    step = 8
    g = pl.pallas_call(
        functools.partial(g_kernel, n_split),
        grid=(cols // step,),
        out_shape=jax.ShapeDtypeStruct((cols, nao, naux), bf16),
        in_specs=[pl.BlockSpec((nao, nao), lambda i: (0, 0))]
        + [pl.BlockSpec((step, rows, naux), lambda i: (i, 0, 0))] * n_split,
        out_specs=pl.BlockSpec((step, nao, naux), lambda i: (i, 0, 0)),
        compiler_params=params,
    )(virt, *[held[m] for m in range(n_split)])
    g = jnp.swapaxes(g, 0, 1)

    total = pl.pallas_call(
        functools.partial(last_kernel, n_split, n_tensor, 1.0 / nao),
        out_shape=jax.ShapeDtypeStruct((naux // n_split, naux), jnp.float32),
        in_specs=[vmem] * (1 + n_tensor),
        out_specs=vmem,
        compiler_params=params,
    )(g, *firsts)
    bit = 1
    while bit < n_tensor:
        total = total + exchange(total, tensor_bits=bit)
        bit *= 2
    return total


def solution(mesh):
    sizes = dict(mesh.shape)
    return jax.shard_map(
        functools.partial(local, n_split=sizes["split"], n_tensor=sizes["tensor"]),
        mesh=mesh,
        in_specs=(P("split", "tensor", None), P("split", None), P("tensor", None), P(), P()),
        out_specs=P("split", None),
        check_vma=False,
    )
```

time: 190 us -> 70.2 us (0.37)
  blocking collectives: 105 us -> 0 us
  waiting for transfers between devices: 50.2 us -> 27.7 us
  starting transfers between devices: 7.49 us -> 29.7 us
  between operations: 13.5 us -> 0.11 us
  Pallas kernels: 0 us -> 6.2 us
  matrix products: 3.88 us -> 0 us
  local copies, waits for them, and re-layouts: 7.74 us -> 5.45 us
    all_gather x1 -> x0, blocking collectives: 67.5 us -> none  [local(): virt = lax.all_gather(virt_local, 'tensor', axis=0, tiled=True)]
    reduce_scatter x2 -> x0, waiting for transfers between devices: 50.2 us -> none  [the longest x1 30.6 us: local(): lax.psum_scatter(second.astype(jnp.float32).astype(jnp.bfloat16), 'split'...]
    psum x1 -> x0, blocking collectives: 37.1 us -> none  [local(): whole = lax.psum(partial_value, 'tensor')]
    ppermute x0 -> x19, starting transfers between devices: none -> 29.7 us  [exchange(): lax.ppermute(x, ('split', 'tensor'), [(d, d ^ bits) for d in range(count)])]
    ppermute x0 -> x19, waiting for transfers between devices: none -> 27.7 us  [exchange(): lax.ppermute(x, ('split', 'tensor'), [(d, d ^ bits) for d in range(count)])]
    all_to_all x1 -> x0, starting transfers between devices: 7.42 us -> none  [local(): lax.all_to_all(first, 'tensor', split_axis=0, concat_axis=1, tiled=True)]
    pallas_call x0 -> x4, Pallas kernels: none -> 6.2 us  [the longest x1 3.4 us: local(): pl.pallas_call(functools.partial(pack_kernel, n_split, n_tensor), out_sha...]
    convert_element_type x2 -> x0, local copies, waits for them, and re-layouts: 5.81 us -> none  [the longest x1 3.12 us: local(): second = jnp.einsum('ls,nlp->nsp', virt, lax.all_to_all(first, 'tensor',...]
  transfers between devices with their start and end apart: 3 -> 19, of which waited for: 2 -> 10; matrix products, arithmetic and copies ran while one was open for 0% -> 2% of each run, Pallas kernels for 0% -> 8%
where the time goes in v1:
time: 70.2 us; the launch traced here: 69.9 us
  starting transfers between devices  29.7 us (42%)
  waiting for transfers between devices  27.7 us (39%)
  Pallas kernels  6.2 us (9%)
  local copies, waits for them, and re-layouts  5.45 us (8%)
  other arithmetic  0.71 us (1%)
    ppermute x19, starting transfers between devices, exchange(): lax.ppermute(x, ('split', 'tensor'), [(d, d ^ bits) for d in range(count)])  29.7 us
    ppermute x19, waiting for transfers between devices, exchange(): lax.ppermute(x, ('split', 'tensor'), [(d, d ^ bits) for d in range(count)])  27.7 us
    unnamed x9, local copies, waits for them, and re-layouts  4.09 us
    pallas_call x1, Pallas kernels, local(): pl.pallas_call(functools.partial(pack_kernel, n_split, n_tensor), out_sha...  3.4 us
    pallas_call x1, Pallas kernels, local(): pl.pallas_call(functools.partial(g_kernel, n_split), grid=(cols // step,)...  1.75 us
  transfers between devices with their start and end apart: 19, of which 10 were waited for; matrix products, arithmetic and copies ran while one was open for 2% of the time, Pallas kernels for 8%

profile of v1, /device:TPU:0, one launch (start us, length us, event | category | flops | bytes accessed | tf_op | source)
XLA Modules:
  0.0 69.9 jit_solution(4928613773087809118)
XLA Ops:
  0.0 1.2 %copy.11 = bf16[64,32,128]{2,0,1:T(8,128)(2,1)S(1)} copy(bf16[64,32,128]{2,1,0:T(8,128)(2,1)} %param.5) | data formatting | bytes 1048576 | tf_op args[0]
  1.2 3.0 %collective-permute-start.4 = (bf16[32,64,128]{2,1,0:T(8,128)(2,1)S(1)}, bf16[32,64,128]{2,1,0:T(8,128)(2,1)S(1)}, u32[]{:S(2)}, u32[]{:S(2)}) collective-permute-start(bf16[32,64,128]{2,1,0:T(8,128)(2,1)S(1)} %bitcast.9), channel_id=1, source_target_pairs={{0,16},{1,17},{2,18},{3,19},{4,20},{5,21},{6,22},{7,23},{8,24},{9,... | collective-permute-start | bytes 1572872 | tf_op jit(solution)/shard_map/ppermute | solution.py:116
  4.3 11.9 %collective-permute-done.4.refs_2_ = bf16[32,64,128]{2,1,0:T(8,128)(2,1)S(1)} collective-permute-done((bf16[32,64,128]{2,1,0:T(8,128)(2,1)S(1)}, bf16[32,64,128]{2,1,0:T(8,128)(2,1)S(1)}, u32[]{:S(2)}, u32[]{:S(2)}) %collective-permute-start.4) | collective-permute-done | bytes 524320 | tf_op jit(solution)/shard_map/ppermute | solution.py:116
  16.3 0.8 %copy-done = bf16[64,256]{1,0:T(8,128)(2,1)S(1)} copy-done((bf16[64,256]{1,0:T(8,128)(2,1)S(1)}, bf16[64,256]{1,0:T(8,128)(2,1)}, u32[]{:S(2)}) %copy-start) | copy-done | bytes 32792
  17.0 0.7 %copy-done.1 = bf16[32,256]{1,0:T(8,128)(2,1)S(1)} copy-done((bf16[32,256]{1,0:T(8,128)(2,1)S(1)}, bf16[32,256]{1,0:T(8,128)(2,1)}, u32[]{:S(2)}) %copy-start.1) | copy-done | bytes 16408
  17.7 0.7 copy-done.2
  18.4 0.7 copy-done.3
  19.1 3.4 %shard_map.55 = (bf16[64,1280]{1,0:T(8,128)(2,1)S(1)}, bf16[64,1280]{1,0:T(8,128)(2,1)S(1)}, bf16[64,1280]{1,0:T(8,128)(2,1)S(1)}, bf16[64,1280]{1,0:T(8,128)(2,1)S(1)}, bf16[32,256]{1,0:T(8,128)(2,1)S(1)}) custom-call(s32[2]{0:T(128)S(1)} %pad_add_fusion.place, s32[8,8]{1,0:T(8,128)S(1)} %copy-done.2, s32[8,8]{1,0:T(8,128)S(1)} %copy-done.3, ...), custom_call_target="tpu_custom_call" | custom-call | tf_op jit(solution)/shard_map/pallas_call | solution.py:122
  22.5 1.8 %collective-permute-start = (bf16[32,256]{1,0:T(8,128)(2,1)S(1)}, bf16[32,256]{1,0:T(8,128)(2,1)S(1)}, u32[]{:S(2)}, u32[]{:S(2)}) collective-permute-start(bf16[32,256]{1,0:T(8,128)(2,1)S(1)} %get-tuple-element.18), channel_id=1, source_target_pairs={{0,1},{1,0},{2,3},{3,2},{4,5},{5,4},{6,7},{7,6},{8,9},{9,8},{10,11... | collective-permute-start | bytes 49160 | tf_op jit(solution)/shard_map/ppermute | solution.py:116
  24.3 2.0 %collective-permute-done = bf16[32,256]{1,0:T(8,128)(2,1)S(1)} collective-permute-done((bf16[32,256]{1,0:T(8,128)(2,1)S(1)}, bf16[32,256]{1,0:T(8,128)(2,1)S(1)}, u32[]{:S(2)}, u32[]{:S(2)}) %collective-permute-start) | collective-permute-done | bytes 16416 | tf_op jit(solution)/shard_map/ppermute | solution.py:116
  26.3 1.8 %collective-permute-start.1 = (bf16[64,256]{1,0:T(8,128)(2,1)S(1)}, bf16[64,256]{1,0:T(8,128)(2,1)S(1)}, u32[]{:S(2)}, u32[]{:S(2)}) collective-permute-start(bf16[64,256]{1,0:T(8,128)(2,1)S(1)} %pad_maximum_fusion.2), channel_id=1, source_target_pairs={{0,2},{1,3},{2,0},{3,1},{4,6},{5,7},{6,4},{7,5},{8,10},{9,11},{10,... | collective-permute-start | bytes 98312 | tf_op jit(solution)/shard_map/ppermute | solution.py:116
  28.1 1.5 %collective-permute-start.7 = (bf16[64,1280]{1,0:T(8,128)(2,1)S(1)}, bf16[64,1280]{1,0:T(8,128)(2,1)S(1)}, u32[]{:S(2)}, u32[]{:S(2)}) collective-permute-start(bf16[64,1280]{1,0:T(8,128)(2,1)S(1)} %get-tuple-element.21), channel_id=1, source_target_pairs={{0,16},{1,17},{2,18},{3,19},{4,20},{5,21},{6,22},{7,23},{8,24},{9,... | collective-permute-start | bytes 491528 | tf_op jit(solution)/shard_map/ppermute | solution.py:116
  30.3 2.9 %collective-permute-start.2 = (bf16[128,256]{1,0:T(8,128)(2,1)S(1)}, bf16[128,256]{1,0:T(8,128)(2,1)S(1)}, u32[]{:S(2)}, u32[]{:S(2)}) collective-permute-start(bf16[128,256]{1,0:T(8,128)(2,1)S(1)} %pad_maximum_fusion.1), channel_id=1, source_target_pairs={{0,4},{1,5},{2,6},{3,7},{4,0},{5,1},{6,2},{7,3},{8,12},{9,13},{10,... | collective-permute-start | bytes 196616 | tf_op jit(solution)/shard_map/ppermute | solution.py:116
  33.2 2.0 %collective-permute-done.7.refs_2_ = bf16[64,1280]{1,0:T(8,128)(2,1)S(1)} collective-permute-done((bf16[64,1280]{1,0:T(8,128)(2,1)S(1)}, bf16[64,1280]{1,0:T(8,128)(2,1)S(1)}, u32[]{:S(2)}, u32[]{:S(2)}) %collective-permute-start.7) | collective-permute-done | bytes 163872 | tf_op jit(solution)/shard_map/ppermute | solution.py:116
  35.1 2.7 %collective-permute-done.8.refs_3_ = bf16[64,1280]{1,0:T(8,128)(2,1)S(1)} collective-permute-done((bf16[64,1280]{1,0:T(8,128)(2,1)S(1)}, bf16[64,1280]{1,0:T(8,128)(2,1)S(1)}, u32[]{:S(2)}, u32[]{:S(2)}) %collective-permute-start.8) | collective-permute-done | bytes 163872 | tf_op jit(solution)/shard_map/ppermute | solution.py:116
  38.2 1.6 %collective-permute-start.9 = (bf16[32,1024]{1,0:T(8,128)(2,1)S(1)}, bf16[32,1024]{1,0:T(8,128)(2,1)S(1)}, u32[]{:S(2)}, u32[]{:S(2)}) collective-permute-start(bf16[32,1024]{1,0:T(8,128)(2,1)S(1)} %get-tuple-element.24), channel_id=1, source_target_pairs={{0,1},{1,0},{2,3},{3,2},{4,5},{5,4},{6,7},{7,6},{8,9},{9,8},{10,11... | collective-permute-start | bytes 196616 | tf_op jit(solution)/shard_map/ppermute | solution.py:116
  39.8 0.7 %collective-permute-start.10 = (bf16[32,1024]{1,0:T(8,128)(2,1)S(1)}, bf16[32,1024]{1,0:T(8,128)(2,1)S(1)}, u32[]{:S(2)}, u32[]{:S(2)}) collective-permute-start(bf16[32,1024]{1,0:T(8,128)(2,1)S(1)} %get-tuple-element.25), channel_id=1, source_target_pairs={{0,2},{1,3},{2,0},{3,1},{4,6},{5,7},{6,4},{7,5},{8,10},{9,11},{10,... | collective-permute-start | bytes 196616 | tf_op jit(solution)/shard_map/ppermute | solution.py:116
  40.5 1.2 %collective-permute-start.11 = (bf16[32,1024]{1,0:T(8,128)(2,1)S(1)}, bf16[32,1024]{1,0:T(8,128)(2,1)S(1)}, u32[]{:S(2)}, u32[]{:S(2)}) collective-permute-start(bf16[32,1024]{1,0:T(8,128)(2,1)S(1)} %get-tuple-element.26), channel_id=1, source_target_pairs={{0,3},{1,2},{2,1},{3,0},{4,7},{5,6},{6,5},{7,4},{8,11},{9,10},{10,... | collective-permute-start | bytes 196616 | tf_op jit(solution)/shard_map/ppermute | solution.py:116
  41.8 0.8 %collective-permute-done.9.refs_1_ = bf16[32,1024]{1,0:T(8,128)(2,1)S(1)} collective-permute-done((bf16[32,1024]{1,0:T(8,128)(2,1)S(1)}, bf16[32,1024]{1,0:T(8,128)(2,1)S(1)}, u32[]{:S(2)}, u32[]{:S(2)}) %collective-permute-start.9) | collective-permute-done | bytes 65568 | tf_op jit(solution)/shard_map/ppermute | solution.py:116
  42.5 2.6 %collective-permute-start.12 = (bf16[32,1024]{1,0:T(8,128)(2,1)S(1)}, bf16[32,1024]{1,0:T(8,128)(2,1)S(1)}, u32[]{:S(2)}, u32[]{:S(2)}) collective-permute-start(bf16[32,1024]{1,0:T(8,128)(2,1)S(1)} %get-tuple-element.27), channel_id=1, source_target_pairs={{0,4},{1,5},{2,6},{3,7},{4,0},{5,1},{6,2},{7,3},{8,12},{9,13},{10,... | collective-permute-start | bytes 196616 | tf_op jit(solution)/shard_map/ppermute | solution.py:116
  45.1 1.9 %collective-permute-start.13 = (bf16[32,1024]{1,0:T(8,128)(2,1)S(1)}, bf16[32,1024]{1,0:T(8,128)(2,1)S(1)}, u32[]{:S(2)}, u32[]{:S(2)}) collective-permute-start(bf16[32,1024]{1,0:T(8,128)(2,1)S(1)} %get-tuple-element.28), channel_id=1, source_target_pairs={{0,5},{1,4},{2,7},{3,6},{4,1},{5,0},{6,3},{7,2},{8,13},{9,12},{10,... | collective-permute-start | bytes 196616 | tf_op jit(solution)/shard_map/ppermute | solution.py:116
  47.0 2.2 %collective-permute-start.14 = (bf16[32,1024]{1,0:T(8,128)(2,1)S(1)}, bf16[32,1024]{1,0:T(8,128)(2,1)S(1)}, u32[]{:S(2)}, u32[]{:S(2)}) collective-permute-start(bf16[32,1024]{1,0:T(8,128)(2,1)S(1)} %get-tuple-element.29), channel_id=1, source_target_pairs={{0,6},{1,7},{2,4},{3,5},{4,2},{5,3},{6,0},{7,1},{8,14},{9,15},{10,... | collective-permute-start | bytes 196616 | tf_op jit(solution)/shard_map/ppermute | solution.py:116
  49.2 2.9 %collective-permute-start.15 = (bf16[32,1024]{1,0:T(8,128)(2,1)S(1)}, bf16[32,1024]{1,0:T(8,128)(2,1)S(1)}, u32[]{:S(2)}, u32[]{:S(2)}) collective-permute-start(bf16[32,1024]{1,0:T(8,128)(2,1)S(1)} %get-tuple-element.30), channel_id=1, source_target_pairs={{0,7},{1,6},{2,5},{3,4},{4,3},{5,2},{6,1},{7,0},{8,15},{9,14},{10,... | collective-permute-start | bytes 196616 | tf_op jit(solution)/shard_map/ppermute | solution.py:116
  52.1 1.7 %shard_map.56 = bf16[32,256,128]{2,1,0:T(8,128)(2,1)S(1)} custom-call(bf16[256,256]{1,0:T(8,128)(2,1)S(1)} %pad_maximum_fusion.virt_ref, bf16[32,64,128]{2,1,0:T(8,128)(2,1)S(1)} %bitcast.12, bf16[32,64,128]{2,1,0:T(8,128)(2,1)S(1)} %collective-permute-done.3.refs_1_, bf16[32,64,128]{2,1,0:T(8,128)(2,1)S(1)} %collective-permute-done.4.refs_2_, ...), custom_call_target="tpu_custom_call" | custom-call | tf_op jit(solution)/shard_map/pallas_call | solution.py:153
  53.9 1.4 %copy.10 = bf16[32,256,128]{2,0,1:T(8,128)(2,1)S(1)} copy(bf16[32,256,128]{2,1,0:T(8,128)(2,1)S(1)} %shard_map.56) | data formatting | bytes 4194304 | tf_op jit(solution)/shard_map/pallas_call | solution.py:153
  55.3 1.0 %collective-permute-done.15.refs_7_ = bf16[32,1024]{1,0:T(8,128)(2,1)S(1)} collective-permute-done((bf16[32,1024]{1,0:T(8,128)(2,1)S(1)}, bf16[32,1024]{1,0:T(8,128)(2,1)S(1)}, u32[]{:S(2)}, u32[]{:S(2)}) %collective-permute-start.15) | collective-permute-done | bytes 65568 | tf_op jit(solution)/shard_map/ppermute | solution.py:116
  56.3 0.7 %shard_map.58 = f32[32,128]{1,0:T(8,128)S(1)} custom-call(bf16[256,32,128]{2,1,0:T(8,128)(2,1)S(1)} %bitcast.8, bf16[32,1024]{1,0:T(8,128)(2,1)S(1)} %get-tuple-element.23.refs_0_, bf16[32,1024]{1,0:T(8,128)(2,1)S(1)} %collective-permute-done.9.refs_1_, bf16[32,1024]{1,0:T(8,128)(2,1)S(1)} %collective-permute-done.10.refs_2_, ...), custom_call_target="tpu_custom_call" | custom-call | tf_op jit(solution)/shard_map/pallas_call | solution.py:164
  57.6 3.2 %collective-permute-done.16 = f32[32,128]{1,0:T(8,128)S(1)} collective-permute-done((f32[32,128]{1,0:T(8,128)S(1)}, f32[32,128]{1,0:T(8,128)S(1)}, u32[]{:S(2)}, u32[]{:S(2)}) %collective-permute-start.16) | collective-permute-done | bytes 16416 | tf_op jit(solution)/shard_map/ppermute | solution.py:116
  60.8 2.1 %collective-permute-start.17 = (f32[32,128]{1,0:T(8,128)S(1)}, f32[32,128]{1,0:T(8,128)S(1)}, u32[]{:S(2)}, u32[]{:S(2)}) collective-permute-start(f32[32,128]{1,0:T(8,128)S(1)} %add.9), channel_id=1, source_target_pairs={{0,2},{1,3},{2,0},{3,1},{4,6},{5,7},{6,4},{7,5},{8,10},{9,11},{10,... | collective-permute-start | bytes 49160 | tf_op jit(solution)/shard_map/ppermute | solution.py:116
  62.9 1.7 %collective-permute-done.17 = f32[32,128]{1,0:T(8,128)S(1)} collective-permute-done((f32[32,128]{1,0:T(8,128)S(1)}, f32[32,128]{1,0:T(8,128)S(1)}, u32[]{:S(2)}, u32[]{:S(2)}) %collective-permute-start.17) | collective-permute-done | bytes 16416 | tf_op jit(solution)/shard_map/ppermute | solution.py:116
  64.6 2.9 %collective-permute-start.18 = (f32[32,128]{1,0:T(8,128)S(1)}, f32[32,128]{1,0:T(8,128)S(1)}, u32[]{:S(2)}, u32[]{:S(2)}) collective-permute-start(f32[32,128]{1,0:T(8,128)S(1)} %add.10), channel_id=1, source_target_pairs={{0,4},{1,5},{2,6},{3,7},{4,0},{5,1},{6,2},{7,3},{8,12},{9,13},{10,... | collective-permute-start | bytes 49160 | tf_op jit(solution)/shard_map/ppermute | solution.py:116
  67.5 1.8 %collective-permute-done.18 = f32[32,128]{1,0:T(8,128)S(1)} collective-permute-done((f32[32,128]{1,0:T(8,128)S(1)}, f32[32,128]{1,0:T(8,128)S(1)}, u32[]{:S(2)}, u32[]{:S(2)}) %collective-permute-start.18) | collective-permute-done | bytes 16416 | tf_op jit(solution)/shard_map/ppermute | solution.py:116
  (27 shorter events, 2.2 us)
Async XLA Ops:
  1.2 14.9 %collective-permute-start.4 = (bf16[32,64,128]{2,1,0:T(8,128)(2,1)S(1)}, bf16[32,64,128]{2,1,0:T(8,128)(2,1)S(1)}, u32[]{:S(2)}, u32[]{:S(2)}) collective-permute-start(bf16[32,64,128]{2,1,0:T(8,128)(2,1)S(1)} %bitcast.9), channel_id=1, source_target_pairs={{0,16},{1,17},{2,18},{3,19},{4,20},{5,21},{6,22},{7,23},{8,24},{9,... | collective-permute-start | bytes 1572872 | tf_op jit(solution)/shard_map/ppermute | solution.py:116
  4.3 42.7 %collective-permute-start.3 = (bf16[32,64,128]{2,1,0:T(8,128)(2,1)S(1)}, bf16[32,64,128]{2,1,0:T(8,128)(2,1)S(1)}, u32[]{:S(2)}, u32[]{:S(2)}) collective-permute-start(bf16[32,64,128]{2,1,0:T(8,128)(2,1)S(1)} %bitcast.10), channel_id=1, source_target_pairs={{0,8},{1,9},{2,10},{3,11},{4,12},{5,13},{6,14},{7,15},{8,0},{9,1},... | collective-permute-start | bytes 1572872 | tf_op jit(solution)/shard_map/ppermute | solution.py:116
  16.2 33.0 %collective-permute-start.5 = (bf16[32,64,128]{2,1,0:T(8,128)(2,1)S(1)}, bf16[32,64,128]{2,1,0:T(8,128)(2,1)S(1)}, u32[]{:S(2)}, u32[]{:S(2)}) collective-permute-start(bf16[32,64,128]{2,1,0:T(8,128)(2,1)S(1)} %collective-permute-done.4.refs_2_), channel_id=1, source_target_pairs={{0,8},{1,9},{2,10},{3,11},{4,12},{5,13},{6,14},{7,15},{8,0},{9,1},... | collective-permute-start | bytes 1572872 | tf_op jit(solution)/shard_map/ppermute | solution.py:116
  16.3 0.8 %copy-start = (bf16[64,256]{1,0:T(8,128)(2,1)S(1)}, bf16[64,256]{1,0:T(8,128)(2,1)}, u32[]{:S(2)}) copy-start(bf16[64,256]{1,0:T(8,128)(2,1)} %occ_ref.1) | copy-start | bytes 98308
  17.0 0.7 %copy-start.1 = (bf16[32,256]{1,0:T(8,128)(2,1)S(1)}, bf16[32,256]{1,0:T(8,128)(2,1)}, u32[]{:S(2)}) copy-start(bf16[32,256]{1,0:T(8,128)(2,1)} %virt_ref.1) | copy-start | bytes 49156
  17.7 0.7 copy-start.2
  18.4 0.7 copy-start.3
  22.5 3.8 %collective-permute-start = (bf16[32,256]{1,0:T(8,128)(2,1)S(1)}, bf16[32,256]{1,0:T(8,128)(2,1)S(1)}, u32[]{:S(2)}, u32[]{:S(2)}) collective-permute-start(bf16[32,256]{1,0:T(8,128)(2,1)S(1)} %get-tuple-element.18), channel_id=1, source_target_pairs={{0,1},{1,0},{2,3},{3,2},{4,5},{5,4},{6,7},{7,6},{8,9},{9,8},{10,11... | collective-permute-start | bytes 49160 | tf_op jit(solution)/shard_map/ppermute | solution.py:116
  26.3 3.9 %collective-permute-start.1 = (bf16[64,256]{1,0:T(8,128)(2,1)S(1)}, bf16[64,256]{1,0:T(8,128)(2,1)S(1)}, u32[]{:S(2)}, u32[]{:S(2)}) collective-permute-start(bf16[64,256]{1,0:T(8,128)(2,1)S(1)} %pad_maximum_fusion.2), channel_id=1, source_target_pairs={{0,2},{1,3},{2,0},{3,1},{4,6},{5,7},{6,4},{7,5},{8,10},{9,11},{10,... | collective-permute-start | bytes 98312 | tf_op jit(solution)/shard_map/ppermute | solution.py:116
  28.1 2.1 %collective-permute-start.6 = (bf16[64,1280]{1,0:T(8,128)(2,1)S(1)}, bf16[64,1280]{1,0:T(8,128)(2,1)S(1)}, u32[]{:S(2)}, u32[]{:S(2)}) collective-permute-start(bf16[64,1280]{1,0:T(8,128)(2,1)S(1)} %get-tuple-element.20), channel_id=1, source_target_pairs={{0,8},{1,9},{2,10},{3,11},{4,12},{5,13},{6,14},{7,15},{8,0},{9,1},... | collective-permute-start | bytes 491528 | tf_op jit(solution)/shard_map/ppermute | solution.py:116
  28.1 7.0 %collective-permute-start.7 = (bf16[64,1280]{1,0:T(8,128)(2,1)S(1)}, bf16[64,1280]{1,0:T(8,128)(2,1)S(1)}, u32[]{:S(2)}, u32[]{:S(2)}) collective-permute-start(bf16[64,1280]{1,0:T(8,128)(2,1)S(1)} %get-tuple-element.21), channel_id=1, source_target_pairs={{0,16},{1,17},{2,18},{3,19},{4,20},{5,21},{6,22},{7,23},{8,24},{9,... | collective-permute-start | bytes 491528 | tf_op jit(solution)/shard_map/ppermute | solution.py:116
  30.2 7.6 %collective-permute-start.8 = (bf16[64,1280]{1,0:T(8,128)(2,1)S(1)}, bf16[64,1280]{1,0:T(8,128)(2,1)S(1)}, u32[]{:S(2)}, u32[]{:S(2)}) collective-permute-start(bf16[64,1280]{1,0:T(8,128)(2,1)S(1)} %get-tuple-element.22), channel_id=1, source_target_pairs={{0,24},{1,25},{2,26},{3,27},{4,28},{5,29},{6,30},{7,31},{8,16},{9,... | collective-permute-start | bytes 491528 | tf_op jit(solution)/shard_map/ppermute | solution.py:116
  30.3 10.3 %collective-permute-start.2 = (bf16[128,256]{1,0:T(8,128)(2,1)S(1)}, bf16[128,256]{1,0:T(8,128)(2,1)S(1)}, u32[]{:S(2)}, u32[]{:S(2)}) collective-permute-start(bf16[128,256]{1,0:T(8,128)(2,1)S(1)} %pad_maximum_fusion.1), channel_id=1, source_target_pairs={{0,4},{1,5},{2,6},{3,7},{4,0},{5,1},{6,2},{7,3},{8,12},{9,13},{10,... | collective-permute-start | bytes 196616 | tf_op jit(solution)/shard_map/ppermute | solution.py:116
  38.2 4.3 %collective-permute-start.9 = (bf16[32,1024]{1,0:T(8,128)(2,1)S(1)}, bf16[32,1024]{1,0:T(8,128)(2,1)S(1)}, u32[]{:S(2)}, u32[]{:S(2)}) collective-permute-start(bf16[32,1024]{1,0:T(8,128)(2,1)S(1)} %get-tuple-element.24), channel_id=1, source_target_pairs={{0,1},{1,0},{2,3},{3,2},{4,5},{5,4},{6,7},{7,6},{8,9},{9,8},{10,11... | collective-permute-start | bytes 196616 | tf_op jit(solution)/shard_map/ppermute | solution.py:116
  39.8 5.3 %collective-permute-start.10 = (bf16[32,1024]{1,0:T(8,128)(2,1)S(1)}, bf16[32,1024]{1,0:T(8,128)(2,1)S(1)}, u32[]{:S(2)}, u32[]{:S(2)}) collective-permute-start(bf16[32,1024]{1,0:T(8,128)(2,1)S(1)} %get-tuple-element.25), channel_id=1, source_target_pairs={{0,2},{1,3},{2,0},{3,1},{4,6},{5,7},{6,4},{7,5},{8,10},{9,11},{10,... | collective-permute-start | bytes 196616 | tf_op jit(solution)/shard_map/ppermute | solution.py:116
  40.5 14.7 %collective-permute-start.11 = (bf16[32,1024]{1,0:T(8,128)(2,1)S(1)}, bf16[32,1024]{1,0:T(8,128)(2,1)S(1)}, u32[]{:S(2)}, u32[]{:S(2)}) collective-permute-start(bf16[32,1024]{1,0:T(8,128)(2,1)S(1)} %get-tuple-element.26), channel_id=1, source_target_pairs={{0,3},{1,2},{2,1},{3,0},{4,7},{5,6},{6,5},{7,4},{8,11},{9,10},{10,... | collective-permute-start | bytes 196616 | tf_op jit(solution)/shard_map/ppermute | solution.py:116
  42.5 12.7 %collective-permute-start.12 = (bf16[32,1024]{1,0:T(8,128)(2,1)S(1)}, bf16[32,1024]{1,0:T(8,128)(2,1)S(1)}, u32[]{:S(2)}, u32[]{:S(2)}) collective-permute-start(bf16[32,1024]{1,0:T(8,128)(2,1)S(1)} %get-tuple-element.27), channel_id=1, source_target_pairs={{0,4},{1,5},{2,6},{3,7},{4,0},{5,1},{6,2},{7,3},{8,12},{9,13},{10,... | collective-permute-start | bytes 196616 | tf_op jit(solution)/shard_map/ppermute | solution.py:116
  45.1 10.1 %collective-permute-start.13 = (bf16[32,1024]{1,0:T(8,128)(2,1)S(1)}, bf16[32,1024]{1,0:T(8,128)(2,1)S(1)}, u32[]{:S(2)}, u32[]{:S(2)}) collective-permute-start(bf16[32,1024]{1,0:T(8,128)(2,1)S(1)} %get-tuple-element.28), channel_id=1, source_target_pairs={{0,5},{1,4},{2,7},{3,6},{4,1},{5,0},{6,3},{7,2},{8,13},{9,12},{10,... | collective-permute-start | bytes 196616 | tf_op jit(solution)/shard_map/ppermute | solution.py:116
  47.0 8.3 %collective-permute-start.14 = (bf16[32,1024]{1,0:T(8,128)(2,1)S(1)}, bf16[32,1024]{1,0:T(8,128)(2,1)S(1)}, u32[]{:S(2)}, u32[]{:S(2)}) collective-permute-start(bf16[32,1024]{1,0:T(8,128)(2,1)S(1)} %get-tuple-element.29), channel_id=1, source_target_pairs={{0,6},{1,7},{2,4},{3,5},{4,2},{5,3},{6,0},{7,1},{8,14},{9,15},{10,... | collective-permute-start | bytes 196616 | tf_op jit(solution)/shard_map/ppermute | solution.py:116
  49.2 7.1 %collective-permute-start.15 = (bf16[32,1024]{1,0:T(8,128)(2,1)S(1)}, bf16[32,1024]{1,0:T(8,128)(2,1)S(1)}, u32[]{:S(2)}, u32[]{:S(2)}) collective-permute-start(bf16[32,1024]{1,0:T(8,128)(2,1)S(1)} %get-tuple-element.30), channel_id=1, source_target_pairs={{0,7},{1,6},{2,5},{3,4},{4,3},{5,2},{6,1},{7,0},{8,15},{9,14},{10,... | collective-permute-start | bytes 196616 | tf_op jit(solution)/shard_map/ppermute | solution.py:116
  57.0 3.8 %collective-permute-start.16 = (f32[32,128]{1,0:T(8,128)S(1)}, f32[32,128]{1,0:T(8,128)S(1)}, u32[]{:S(2)}, u32[]{:S(2)}) collective-permute-start(f32[32,128]{1,0:T(8,128)S(1)} %shard_map.58), channel_id=1, source_target_pairs={{0,1},{1,0},{2,3},{3,2},{4,5},{5,4},{6,7},{7,6},{8,9},{9,8},{10,11... | collective-permute-start | bytes 49160 | tf_op jit(solution)/shard_map/ppermute | solution.py:116
  60.8 3.8 %collective-permute-start.17 = (f32[32,128]{1,0:T(8,128)S(1)}, f32[32,128]{1,0:T(8,128)S(1)}, u32[]{:S(2)}, u32[]{:S(2)}) collective-permute-start(f32[32,128]{1,0:T(8,128)S(1)} %add.9), channel_id=1, source_target_pairs={{0,2},{1,3},{2,0},{3,1},{4,6},{5,7},{6,4},{7,5},{8,10},{9,11},{10,... | collective-permute-start | bytes 49160 | tf_op jit(solution)/shard_map/ppermute | solution.py:116
  64.6 4.6 %collective-permute-start.18 = (f32[32,128]{1,0:T(8,128)S(1)}, f32[32,128]{1,0:T(8,128)S(1)}, u32[]{:S(2)}, u32[]{:S(2)}) collective-permute-start(f32[32,128]{1,0:T(8,128)S(1)} %add.10), channel_id=1, source_target_pairs={{0,4},{1,5},{2,6},{3,7},{4,0},{5,1},{6,2},{7,3},{8,12},{9,13},{10,... | collective-permute-start | bytes 49160 | tf_op jit(solution)/shard_map/ppermute | solution.py:116

commit v2 on v1

v2 whole, which is shorter than its diff:
```python
import functools

import jax
import jax.numpy as jnp
from jax import lax
from jax.experimental import pallas as pl
from jax.experimental.pallas import tpu as pltpu
from jax.sharding import PartitionSpec as P

VMEM_LIMIT = 24 * 1024 * 1024
PACK_VMEM_LIMIT = 56 * 1024 * 1024
BF16 = jnp.bfloat16
F32 = jnp.float32


def xor_blocks(x, width, index):
    cols = x.shape[1]
    bit = 1
    while width * bit < cols:
        span = width * bit
        order = []
        for start in range(0, cols, 2 * span):
            order += [x[:, start + span:start + 2 * span], x[:, start:start + span]]
        x = jnp.where((index & bit) != 0, jnp.concatenate(order, axis=1), x)
        bit *= 2
    return x


def screened(green, mask_ref, first_row, block):
    rows, cols = green.shape
    column = lax.broadcasted_iota(jnp.int32, (1, cols), 1) // block
    parts = []
    for r in range(rows // block):
        keep = jnp.zeros((1, cols), jnp.int32)
        for c in range(cols // block):
            keep = jnp.where(column == c, mask_ref[first_row + r, c], keep)
        part = green[r * block:(r + 1) * block].astype(F32)
        parts.append(jnp.where(keep > 0, part, 0.0))
    return jnp.concatenate(parts, axis=0) if len(parts) > 1 else parts[0]


def swap_lane_blocks(tiles, width):
    tiles = list(tiles)
    count = len(tiles)
    lanes = tiles[0].shape[1]
    lane = lax.broadcasted_iota(jnp.int32, tiles[0].shape, 1)
    half = count // 2
    while half:
        span = half * width
        low = (lane // span) % 2 == 0
        for j in range(count):
            if j & half:
                continue
            a, b = tiles[j], tiles[j | half]
            tiles[j] = jnp.where(low, a, pltpu.roll(b, span, 1))
            tiles[j | half] = jnp.where(low, pltpu.roll(a, lanes - span, 1), b)
        half //= 2
    return tiles


def xor_list(items, index):
    bit = 1
    while bit < len(items):
        flag = (index & bit) != 0
        items = [jnp.where(flag, items[m ^ bit], items[m]) for m in range(len(items))]
        bit *= 2
    return items


def pack_kernel(n_split, mask_hbm, b_hbm, occ_hbm, basis_ref, *rest):
    outs, (mask, b, green, sems) = rest[:n_split], rest[n_split:]
    copies = [
        pltpu.make_async_copy(src, dst, sems.at[i])
        for i, (src, dst) in enumerate(((b_hbm, b), (occ_hbm, green), (mask_hbm, mask)))
    ]
    for copy in copies:
        copy.start()
    s, t = lax.axis_index("split"), lax.axis_index("tensor")
    rows, cols, naux = b.shape
    group = cols // n_split
    block = green.shape[1] // mask.shape[0]
    for copy in copies[1:]:
        copy.wait()
    occ = screened(green[...], mask, s * (rows // block), block)
    occ = xor_blocks(occ, cols, t).astype(BF16)
    for m in range(n_split):
        outs[m][:, group * naux:] = occ
    copies[0].wait()
    basis_ref[...] = jnp.swapaxes(b[...], 0, 1)
    for l in range(group):
        tiles = swap_lane_blocks([basis_ref[j * group + l] for j in range(n_split)], naux // n_split)
        tiles = xor_list(tiles, s)
        for m in range(n_split):
            outs[m][:, l * naux:(l + 1) * naux] = tiles[m]


def first_kernel(n_split, n_tensor, width, *refs):
    packed, outs = refs[:n_split], refs[n_split:]
    whole = jnp.concatenate([p[...] for p in packed], axis=0)
    first = lax.dot_general(
        whole[:, width:], whole[:, :width], (((0,), (0,)), ((), ())), preferred_element_type=F32
    )
    rows = first.shape[0] // n_tensor
    for k in range(n_tensor):
        outs[k][...] = first[k * rows:(k + 1) * rows].astype(BF16)


def g_kernel(n_split, n_tensor, mask, virt_ref, *refs):
    out, virt = refs[n_split], refs[n_split + 1]
    part, step = out.shape[0], out.shape[1]
    nao = virt.shape[0]
    cols = nao // n_tensor
    rows = nao // n_split
    block = nao // mask.shape[0]
    s, t = lax.axis_index("split"), lax.axis_index("tensor")

    @pl.when((pl.program_id(0) == 0) & (pl.program_id(1) == 0))
    def _():
        for k in range(n_tensor):
            piece = slice(k * cols, (k + 1) * cols)
            kept = screened(virt_ref[piece, :], mask, (t ^ k) * (cols // block), block)
            virt[piece, :] = xor_blocks(kept, rows, s).astype(BF16)

    left = virt[pl.ds(pl.multiple_of(pl.program_id(1) * part, part), part), :]
    made = []
    for n in range(step):
        right = jnp.concatenate([r[n] for r in refs[:n_split]], axis=0)
        made.append(jnp.dot(left, right, preferred_element_type=F32).astype(BF16))
    out[...] = jnp.swapaxes(jnp.stack(made), 0, 1)


def last_kernel(n_split, n_tensor, scale, g_ref, *refs):
    firsts, out = refs[:n_tensor], refs[n_tensor]
    rows = firsts[0].shape[0]
    naux = g_ref.shape[2]
    group = firsts[0].shape[1] // naux
    width = naux // n_split
    totals = [jnp.zeros((naux, naux), F32) for _ in range(n_split)]
    for k in range(n_tensor):
        left = jnp.concatenate([firsts[k][:, l * naux:(l + 1) * naux] for l in range(group)], axis=0)
        for j in range(n_split):
            start = (k * n_split + j) * group
            right = g_ref[start:start + group].reshape(group * rows, naux)
            totals[j] += lax.dot_general(left, right, (((0,), (0,)), ((), ())), preferred_element_type=F32)
    result = totals[0][:width]
    for j in range(1, n_split):
        result = result + totals[j][j * width:(j + 1) * width]
    out[...] = result * scale


def stages(count):
    bit, found = 1, []
    while bit < count:
        found.append([bit, 2 * bit, 3 * bit] if 2 * bit < count else [bit])
        bit *= 4
    return found


def local(three_centre, green_occ, green_virt, occ_mask, virt_mask, *, n_split, n_tensor):
    rows, cols, naux = three_centre.shape
    nao = green_occ.shape[1]
    packed_width = cols // n_split * naux
    count = n_split * n_tensor
    params = pltpu.CompilerParams(vmem_limit_bytes=VMEM_LIMIT)
    smem = pl.BlockSpec(memory_space=pltpu.SMEM)
    vmem = pl.BlockSpec(memory_space=pltpu.VMEM)
    hbm = pl.BlockSpec(memory_space=pltpu.HBM)

    def exchange(x, split_bits=0, tensor_bits=0):
        bits = split_bits * n_tensor + tensor_bits
        return lax.ppermute(x, ("split", "tensor"), [(d, d ^ bits) for d in range(count)])

    basis, *packed = pl.pallas_call(
        functools.partial(pack_kernel, n_split),
        out_shape=[jax.ShapeDtypeStruct((cols, rows, naux), BF16)]
        + [jax.ShapeDtypeStruct((rows, packed_width + nao), BF16)] * n_split,
        in_specs=[hbm] * 3,
        out_specs=[vmem] * (n_split + 1),
        scratch_shapes=[
            pltpu.SMEM(occ_mask.shape, jnp.int32),
            pltpu.VMEM(three_centre.shape, BF16),
            pltpu.VMEM(green_occ.shape, BF16),
            pltpu.SemaphoreType.DMA((3,)),
        ],
        compiler_params=pltpu.CompilerParams(vmem_limit_bytes=PACK_VMEM_LIMIT),
    )(occ_mask, three_centre, green_occ)
    virt, *packed = lax.optimization_barrier((green_virt, *packed))
    packed = [packed[0]] + [exchange(packed[m], split_bits=m) for m in range(1, n_split)]

    for near in stages(n_tensor):
        virt = jnp.concatenate([virt] + [exchange(virt, tensor_bits=k) for k in near], axis=0)

    virt, *packed = lax.optimization_barrier((virt, *packed))

    firsts = pl.pallas_call(
        functools.partial(first_kernel, n_split, n_tensor, packed_width),
        out_shape=[jax.ShapeDtypeStruct((cols, packed_width), BF16)] * n_tensor,
        in_specs=[vmem] * n_split,
        out_specs=[vmem] * n_tensor,
        compiler_params=params,
    )(*packed)
    basis, *firsts = lax.optimization_barrier((basis, *firsts))

    held = {0: basis}
    bit = n_split // 2
    held[bit] = exchange(basis, split_bits=bit)
    half = n_tensor // 2
    far = [exchange(firsts[k], tensor_bits=k) for k in reversed(range(half, n_tensor))]
    held[bit], *far = lax.optimization_barrier((held[bit], *far))
    near = [exchange(firsts[k], tensor_bits=k) for k in reversed(range(1, half))]
    firsts = [firsts[0], *near[::-1], *far[::-1]]
    while bit > 1:
        bit //= 2
        held.update({m | bit: exchange(x, split_bits=bit) for m, x in held.items()})

    step, part = 16, min(nao, 256)
    g = pl.pallas_call(
        functools.partial(g_kernel, n_split, n_tensor),
        grid=(cols // step, nao // part),
        out_shape=jax.ShapeDtypeStruct((nao, cols, naux), BF16),
        in_specs=[smem, pl.BlockSpec((nao, nao), lambda i, j: (0, 0))]
        + [pl.BlockSpec((step, rows, naux), lambda i, j: (i, 0, 0))] * n_split,
        out_specs=pl.BlockSpec((part, step, naux), lambda i, j: (j, i, 0)),
        scratch_shapes=[pltpu.VMEM((nao, nao), BF16)],
        compiler_params=params,
    )(virt_mask, virt, *[held[m] for m in range(n_split)])

    total = pl.pallas_call(
        functools.partial(last_kernel, n_split, n_tensor, 1.0 / nao),
        out_shape=jax.ShapeDtypeStruct((naux // n_split, naux), F32),
        in_specs=[vmem] * (1 + n_tensor),
        out_specs=vmem,
        compiler_params=params,
    )(g, *firsts)
    for near in stages(n_tensor):
        got = [exchange(total, tensor_bits=k) for k in near]
        for x in got:
            total = total + x
    return total


def solution(mesh):
    sizes = dict(mesh.shape)
    return jax.shard_map(
        functools.partial(local, n_split=sizes["split"], n_tensor=sizes["tensor"]),
        mesh=mesh,
        in_specs=(P("split", "tensor", None), P("split", None), P("tensor", None), P(), P()),
        out_specs=P("split", None),
        check_vma=False,
    )
```

time: 70.2 us -> 56.4 us (0.80)
  waiting for transfers between devices: 27.7 us -> 17.7 us
  starting transfers between devices: 29.7 us -> 27.3 us
  local copies, waits for them, and re-layouts: 5.45 us -> 3.37 us
    ppermute x19 -> x21, waiting for transfers between devices: 27.7 us -> 17.7 us  [exchange(): lax.ppermute(x, ('split', 'tensor'), [(d, d ^ bits) for d in range(count)])]
    ppermute x19 -> x21, starting transfers between devices: 29.7 us -> 27.3 us  [exchange(): lax.ppermute(x, ('split', 'tensor'), [(d, d ^ bits) for d in range(count)])]
    pallas_call x1 -> x0, local copies, waits for them, and re-layouts: 1.35 us -> none  [local(): pl.pallas_call(functools.partial(g_kernel, n_split), grid=(cols // step,)...]
    unnamed x9 -> x10, local copies, waits for them, and re-layouts: 4.09 us -> 3.37 us
    concatenate x3 -> x1, other arithmetic: 0.02 us -> 0.72 us  [local(): jnp.concatenate([virt] + [exchange(virt, tensor_bits=k) for k in near], a...]
  transfers between devices with their start and end apart: 19 -> 21, of which waited for: 10 -> 11; matrix products, arithmetic and copies ran while one was open for 2% -> 3% of each run, Pallas kernels for 8% -> 4%
where the time goes in v2:
time: 56.4 us; the launch traced here: 56 us
  starting transfers between devices  27.3 us (48%)
  waiting for transfers between devices  17.7 us (31%)
  Pallas kernels  6.13 us (11%)
  local copies, waits for them, and re-layouts  3.37 us (6%)
  other arithmetic  1.34 us (2%)
    ppermute x21, starting transfers between devices, exchange(): lax.ppermute(x, ('split', 'tensor'), [(d, d ^ bits) for d in range(count)])  27.3 us
    ppermute x21, waiting for transfers between devices, exchange(): lax.ppermute(x, ('split', 'tensor'), [(d, d ^ bits) for d in range(count)])  17.7 us
    unnamed x10, local copies, waits for them, and re-layouts  3.37 us
    pallas_call x1, Pallas kernels, local(): pl.pallas_call(functools.partial(pack_kernel, n_split), out_shape=[jax.Sh...  2.7 us
    pallas_call x1, Pallas kernels, local(): pl.pallas_call(functools.partial(g_kernel, n_split, n_tensor), grid=(cols...  2.36 us
  transfers between devices with their start and end apart: 21, of which 11 were waited for; matrix products, arithmetic and copies ran while one was open for 3% of the time, Pallas kernels for 4%

profile of v2, /device:TPU:0, one launch (start us, length us, event | category | flops | bytes accessed | tf_op | source)
XLA Modules:
  0.0 56.0 jit_solution(8500735955786854985)
XLA Ops:
  0.0 2.7 %shard_map.55 = (bf16[32,64,128]{2,1,0:T(8,128)(2,1)}, bf16[64,1280]{1,0:T(8,128)(2,1)}, bf16[64,1280]{1,0:T(8,128)(2,1)}, bf16[64,1280]{1,0:T(8,128)(2,1)}, bf16[64,1280]{1,0:T(8,128)(2,1)}) custom-call(s32[8,8]{1,0:T(8,128)} %mask_hbm.1, bf16[64,32,128]{2,1,0:T(8,128)(2,1)} %b_hbm.1, bf16[64,256]{1,0:T(8,128)(2,1)} %occ_hbm.1), custom_call_target="tpu_custom_call" | custom-call | tf_op jit(solution)/shard_map/pallas_call | solution.py:173
  2.7 4.0 %collective-permute-start.2 = (bf16[32,256]{1,0:T(8,128)(2,1)}, bf16[32,256]{1,0:T(8,128)(2,1)S(1)}, u32[]{:S(2)}, u32[]{:S(2)}) collective-permute-start(bf16[32,256]{1,0:T(8,128)(2,1)} %param.7), channel_id=1, source_target_pairs={{0,3},{1,2},{2,1},{3,0},{4,7},{5,6},{6,5},{7,4},{8,11},{9,10},{10,... | collective-permute-start | bytes 49160 | tf_op jit(solution)/shard_map/ppermute | solution.py:171
  6.8 0.4 collective-permute-start.1
  7.4 1.8 %collective-permute-start.5 = (bf16[64,1280]{1,0:T(8,128)(2,1)}, bf16[64,1280]{1,0:T(8,128)(2,1)S(1)}, u32[]{:S(2)}, u32[]{:S(2)}) collective-permute-start(bf16[64,1280]{1,0:T(8,128)(2,1)} %get-tuple-element.49), channel_id=1, source_target_pairs={{0,16},{1,17},{2,18},{3,19},{4,20},{5,21},{6,22},{7,23},{8,24},{9,... | collective-permute-start | bytes 491528 | tf_op jit(solution)/shard_map/ppermute | solution.py:171
  9.2 0.7 %constant_dynamic-update-slice_fusion.4 = bf16[256,256]{1,0:T(8,128)(2,1)S(1)} fusion(bf16[32,256]{1,0:T(8,128)(2,1)} %param.7), kind=kLoop, calls=%fused_computation.6 | loop fusion | bytes 32768
  10.0 0.7 %collective-permute-done.1 = bf16[32,256]{1,0:T(8,128)(2,1)S(1)} collective-permute-done((bf16[32,256]{1,0:T(8,128)(2,1)}, bf16[32,256]{1,0:T(8,128)(2,1)S(1)}, u32[]{:S(2)}, u32[]{:S(2)}) %collective-permute-start.1) | collective-permute-done | bytes 16416 | tf_op jit(solution)/shard_map/ppermute | solution.py:171
  10.7 0.4 collective-permute-done
  11.2 0.7 %pad_maximum_fusion = bf16[128,256]{1,0:T(8,128)(2,1)S(1)} fusion(bf16[32,256]{1,0:T(8,128)(2,1)S(1)} %collective-permute-done.2, bf16[32,256]{1,0:T(8,128)(2,1)S(1)} %collective-permute-done.1, bf16[32,256]{1,0:T(8,128)(2,1)S(1)} %collective-permute-done, bf16[32,256]{1,0:T(8,128)(2,1)} %param.7), kind=kLoop, calls=%fused_computation | loop fusion | flops 262144 | bytes 131072 | tf_op jit(solution)/shard_map/concatenate | solution.py:191
  11.9 2.6 %collective-permute-start.3 = (bf16[128,256]{1,0:T(8,128)(2,1)S(1)}, bf16[128,256]{1,0:T(8,128)(2,1)S(1)}, u32[]{:S(2)}, u32[]{:S(2)}) collective-permute-start(bf16[128,256]{1,0:T(8,128)(2,1)S(1)} %pad_maximum_fusion), channel_id=1, source_target_pairs={{0,4},{1,5},{2,6},{3,7},{4,0},{5,1},{6,2},{7,3},{8,12},{9,13},{10,... | collective-permute-start | bytes 196616 | tf_op jit(solution)/shard_map/ppermute | solution.py:171
  14.5 2.8 %collective-permute-done.3 = bf16[128,256]{1,0:T(8,128)(2,1)S(1)} collective-permute-done((bf16[128,256]{1,0:T(8,128)(2,1)S(1)}, bf16[128,256]{1,0:T(8,128)(2,1)S(1)}, u32[]{:S(2)}, u32[]{:S(2)}) %collective-permute-start.3) | collective-permute-done | bytes 65568 | tf_op jit(solution)/shard_map/ppermute | solution.py:171
  17.5 0.9 %copy-done.1 = bf16[64,1280]{1,0:T(8,128)(2,1)S(1)} copy-done((bf16[64,1280]{1,0:T(8,128)(2,1)S(1)}, bf16[64,1280]{1,0:T(8,128)(2,1)}, u32[]{:S(2)}) %copy-start.1) | copy-done | bytes 163864
  18.7 1.7 %collective-permute-start.8 = (bf16[32,64,128]{2,1,0:T(8,128)(2,1)}, bf16[32,64,128]{2,1,0:T(8,128)(2,1)S(1)}, u32[]{:S(2)}, u32[]{:S(2)}) collective-permute-start(bf16[32,64,128]{2,1,0:T(8,128)(2,1)} %get-tuple-element.65.refs_0_), channel_id=1, source_target_pairs={{0,16},{1,17},{2,18},{3,19},{4,20},{5,21},{6,22},{7,23},{8,24},{9,... | collective-permute-start | bytes 1572872 | tf_op jit(solution)/shard_map/ppermute | solution.py:171
  20.5 4.6 %collective-permute-start.9 = (bf16[32,1024]{1,0:T(8,128)(2,1)S(1)}, bf16[32,1024]{1,0:T(8,128)(2,1)S(1)}, u32[]{:S(2)}, u32[]{:S(2)}) collective-permute-start(bf16[32,1024]{1,0:T(8,128)(2,1)S(1)} %get-tuple-element.66), channel_id=1, source_target_pairs={{0,7},{1,6},{2,5},{3,4},{4,3},{5,2},{6,1},{7,0},{8,15},{9,14},{10,... | collective-permute-start | bytes 196616 | tf_op jit(solution)/shard_map/ppermute | solution.py:171
  25.2 0.7 %collective-permute-start.11 = (bf16[32,1024]{1,0:T(8,128)(2,1)S(1)}, bf16[32,1024]{1,0:T(8,128)(2,1)S(1)}, u32[]{:S(2)}, u32[]{:S(2)}) collective-permute-start(bf16[32,1024]{1,0:T(8,128)(2,1)S(1)} %get-tuple-element.68), channel_id=1, source_target_pairs={{0,5},{1,4},{2,7},{3,6},{4,1},{5,0},{6,3},{7,2},{8,13},{9,12},{10,... | collective-permute-start | bytes 196616 | tf_op jit(solution)/shard_map/ppermute | solution.py:171
  26.0 2.1 %collective-permute-start.12 = (bf16[32,1024]{1,0:T(8,128)(2,1)S(1)}, bf16[32,1024]{1,0:T(8,128)(2,1)S(1)}, u32[]{:S(2)}, u32[]{:S(2)}) collective-permute-start(bf16[32,1024]{1,0:T(8,128)(2,1)S(1)} %get-tuple-element.69), channel_id=1, source_target_pairs={{0,4},{1,5},{2,6},{3,7},{4,0},{5,1},{6,2},{7,3},{8,12},{9,13},{10,... | collective-permute-start | bytes 196616 | tf_op jit(solution)/shard_map/ppermute | solution.py:171
  28.1 3.2 %collective-permute-done.10.refs_6_ = bf16[32,1024]{1,0:T(8,128)(2,1)S(1)} collective-permute-done((bf16[32,1024]{1,0:T(8,128)(2,1)S(1)}, bf16[32,1024]{1,0:T(8,128)(2,1)S(1)}, u32[]{:S(2)}, u32[]{:S(2)}) %collective-permute-start.10) | collective-permute-done | bytes 65568 | tf_op jit(solution)/shard_map/ppermute | solution.py:171
  31.3 3.8 %collective-permute-done.11.refs_5_ = bf16[32,1024]{1,0:T(8,128)(2,1)S(1)} collective-permute-done((bf16[32,1024]{1,0:T(8,128)(2,1)S(1)}, bf16[32,1024]{1,0:T(8,128)(2,1)S(1)}, u32[]{:S(2)}, u32[]{:S(2)}) %collective-permute-start.11) | collective-permute-done | bytes 65568 | tf_op jit(solution)/shard_map/ppermute | solution.py:171
  35.1 1.2 %collective-permute-done.12.refs_4_ = bf16[32,1024]{1,0:T(8,128)(2,1)S(1)} collective-permute-done((bf16[32,1024]{1,0:T(8,128)(2,1)S(1)}, bf16[32,1024]{1,0:T(8,128)(2,1)S(1)}, u32[]{:S(2)}, u32[]{:S(2)}) %collective-permute-start.12) | collective-permute-done | bytes 65568 | tf_op jit(solution)/shard_map/ppermute | solution.py:171
  36.3 0.8 %collective-permute-start.14 = (bf16[32,1024]{1,0:T(8,128)(2,1)S(1)}, bf16[32,1024]{1,0:T(8,128)(2,1)S(1)}, u32[]{:S(2)}, u32[]{:S(2)}) collective-permute-start(bf16[32,1024]{1,0:T(8,128)(2,1)S(1)} %get-tuple-element.72), channel_id=1, source_target_pairs={{0,1},{1,0},{2,3},{3,2},{4,5},{5,4},{6,7},{7,6},{8,9},{9,8},{10,11... | collective-permute-start | bytes 196616 | tf_op jit(solution)/shard_map/ppermute | solution.py:171
  37.1 2.7 %collective-permute-start.16 = (bf16[32,1024]{1,0:T(8,128)(2,1)S(1)}, bf16[32,1024]{1,0:T(8,128)(2,1)S(1)}, u32[]{:S(2)}, u32[]{:S(2)}) collective-permute-start(bf16[32,1024]{1,0:T(8,128)(2,1)S(1)} %get-tuple-element.74), channel_id=1, source_target_pairs={{0,3},{1,2},{2,1},{3,0},{4,7},{5,6},{6,5},{7,4},{8,11},{9,10},{10,... | collective-permute-start | bytes 196616 | tf_op jit(solution)/shard_map/ppermute | solution.py:171
  39.8 1.0 %copy-done = bf16[32,64,128]{2,1,0:T(8,128)(2,1)S(1)} copy-done((bf16[32,64,128]{2,1,0:T(8,128)(2,1)S(1)}, bf16[32,64,128]{2,1,0:T(8,128)(2,1)}, u32[]{:S(2)}) %copy-start) | copy-done | bytes 524312
  40.8 0.7 %copy-done.2 = s32[8,8]{1,0:T(8,128)S(1)} copy-done((s32[8,8]{1,0:T(8,128)S(1)}, s32[8,8]{1,0:T(8,128)}, u32[]{:S(2)}) %copy-start.2) | copy-done | bytes 280
  41.5 2.4 %shard_map.57.g_ref = bf16[256,32,128]{2,1,0:T(8,128)(2,1)S(1)} custom-call(s32[8,8]{1,0:T(8,128)S(1)} %copy-done.2, bf16[256,256]{1,0:T(8,128)(2,1)S(1)} %constant_dynamic-update-slice_fusion.virt_ref, bf16[32,64,128]{2,1,0:T(8,128)(2,1)S(1)} %copy-done, bf16[32,64,128]{2,1,0:T(8,128)(2,1)S(1)} %collective-permute-done.7.refs_1_, ...), custom_call_target="tpu_custom_call" | custom-call | tf_op jit(solution)/shard_map/pallas_call | solution.py:217
  43.9 0.8 %shard_map.58 = f32[32,128]{1,0:T(8,128)S(1)} custom-call(bf16[256,32,128]{2,1,0:T(8,128)(2,1)S(1)} %shard_map.57.g_ref, bf16[32,1024]{1,0:T(8,128)(2,1)S(1)} %get-tuple-element.71.refs_0_, bf16[32,1024]{1,0:T(8,128)(2,1)S(1)} %collective-permute-done.14.refs_1_, bf16[32,1024]{1,0:T(8,128)(2,1)S(1)} %collective-permute-done.15.refs_2_, ...), custom_call_target="tpu_custom_call" | custom-call | tf_op jit(solution)/shard_map/pallas_call | solution.py:228
  44.7 1.1 %collective-permute-start.19 = (f32[32,128]{1,0:T(8,128)S(1)}, f32[32,128]{1,0:T(8,128)S(1)}, u32[]{:S(2)}, u32[]{:S(2)}) collective-permute-start(f32[32,128]{1,0:T(8,128)S(1)} %shard_map.58), channel_id=1, source_target_pairs={{0,3},{1,2},{2,1},{3,0},{4,7},{5,6},{6,5},{7,4},{8,11},{9,10},{10,... | collective-permute-start | bytes 49160 | tf_op jit(solution)/shard_map/ppermute | solution.py:171
  45.7 1.2 %collective-permute-start.18 = (f32[32,128]{1,0:T(8,128)S(1)}, f32[32,128]{1,0:T(8,128)S(1)}, u32[]{:S(2)}, u32[]{:S(2)}) collective-permute-start(f32[32,128]{1,0:T(8,128)S(1)} %shard_map.58), channel_id=1, source_target_pairs={{0,2},{1,3},{2,0},{3,1},{4,6},{5,7},{6,4},{7,5},{8,10},{9,11},{10,... | collective-permute-start | bytes 49160 | tf_op jit(solution)/shard_map/ppermute | solution.py:171
  47.0 1.2 %collective-permute-start.17 = (f32[32,128]{1,0:T(8,128)S(1)}, f32[32,128]{1,0:T(8,128)S(1)}, u32[]{:S(2)}, u32[]{:S(2)}) collective-permute-start(f32[32,128]{1,0:T(8,128)S(1)} %shard_map.58), channel_id=1, source_target_pairs={{0,1},{1,0},{2,3},{3,2},{4,5},{5,4},{6,7},{7,6},{8,9},{9,8},{10,11... | collective-permute-start | bytes 49160 | tf_op jit(solution)/shard_map/ppermute | solution.py:171
  48.2 1.1 %collective-permute-done.19 = f32[32,128]{1,0:T(8,128)S(1)} collective-permute-done((f32[32,128]{1,0:T(8,128)S(1)}, f32[32,128]{1,0:T(8,128)S(1)}, u32[]{:S(2)}, u32[]{:S(2)}) %collective-permute-start.19) | collective-permute-done | bytes 16416 | tf_op jit(solution)/shard_map/ppermute | solution.py:171
  49.5 1.2 %collective-permute-done.17 = f32[32,128]{1,0:T(8,128)S(1)} collective-permute-done((f32[32,128]{1,0:T(8,128)S(1)}, f32[32,128]{1,0:T(8,128)S(1)}, u32[]{:S(2)}, u32[]{:S(2)}) %collective-permute-start.17) | collective-permute-done | bytes 16416 | tf_op jit(solution)/shard_map/ppermute | solution.py:171
  50.7 1.7 %collective-permute-start.20 = (f32[32,128]{1,0:T(8,128)S(1)}, f32[32,128]{1,0:T(8,128)S(1)}, u32[]{:S(2)}, u32[]{:S(2)}) collective-permute-start(f32[32,128]{1,0:T(8,128)S(1)} %add_add_fusion), channel_id=1, source_target_pairs={{0,4},{1,5},{2,6},{3,7},{4,0},{5,1},{6,2},{7,3},{8,12},{9,13},{10,... | collective-permute-start | bytes 49160 | tf_op jit(solution)/shard_map/ppermute | solution.py:171
  52.5 2.9 %collective-permute-done.20 = f32[32,128]{1,0:T(8,128)S(1)} collective-permute-done((f32[32,128]{1,0:T(8,128)S(1)}, f32[32,128]{1,0:T(8,128)S(1)}, u32[]{:S(2)}, u32[]{:S(2)}) %collective-permute-start.20) | collective-permute-done | bytes 16416 | tf_op jit(solution)/shard_map/ppermute | solution.py:171
  55.4 0.6 %add.15 = f32[32,128]{1,0:T(8,128)} add(f32[32,128]{1,0:T(8,128)S(1)} %add_add_fusion, f32[32,128]{1,0:T(8,128)S(1)} %collective-permute-done.20) | non-fusion elementwise | flops 4096 | bytes 49152 | tf_op jit(solution)/shard_map/add | solution.py:238
  (28 shorter events, 1.2 us)
Async XLA Ops:
  2.7 7.2 %collective-permute-start.2 = (bf16[32,256]{1,0:T(8,128)(2,1)}, bf16[32,256]{1,0:T(8,128)(2,1)S(1)}, u32[]{:S(2)}, u32[]{:S(2)}) collective-permute-start(bf16[32,256]{1,0:T(8,128)(2,1)} %param.7), channel_id=1, source_target_pairs={{0,3},{1,2},{2,1},{3,0},{4,7},{5,6},{6,5},{7,4},{8,11},{9,10},{10,... | collective-permute-start | bytes 49160 | tf_op jit(solution)/shard_map/ppermute | solution.py:171
  6.8 3.9 %collective-permute-start.1 = (bf16[32,256]{1,0:T(8,128)(2,1)}, bf16[32,256]{1,0:T(8,128)(2,1)S(1)}, u32[]{:S(2)}, u32[]{:S(2)}) collective-permute-start(bf16[32,256]{1,0:T(8,128)(2,1)} %param.7), channel_id=1, source_target_pairs={{0,2},{1,3},{2,0},{3,1},{4,6},{5,7},{6,4},{7,5},{8,10},{9,11},{10,... | collective-permute-start | bytes 49160 | tf_op jit(solution)/shard_map/ppermute | solution.py:171
  7.2 3.9 %collective-permute-start = (bf16[32,256]{1,0:T(8,128)(2,1)}, bf16[32,256]{1,0:T(8,128)(2,1)S(1)}, u32[]{:S(2)}, u32[]{:S(2)}) collective-permute-start(bf16[32,256]{1,0:T(8,128)(2,1)} %param.7), channel_id=1, source_target_pairs={{0,1},{1,0},{2,3},{3,2},{4,5},{5,4},{6,7},{7,6},{8,9},{9,8},{10,11... | collective-permute-start | bytes 49160 | tf_op jit(solution)/shard_map/ppermute | solution.py:171
  7.4 9.9 %collective-permute-start.4 = (bf16[64,1280]{1,0:T(8,128)(2,1)}, bf16[64,1280]{1,0:T(8,128)(2,1)S(1)}, u32[]{:S(2)}, u32[]{:S(2)}) collective-permute-start(bf16[64,1280]{1,0:T(8,128)(2,1)} %get-tuple-element.48), channel_id=1, source_target_pairs={{0,8},{1,9},{2,10},{3,11},{4,12},{5,13},{6,14},{7,15},{8,0},{9,1},... | collective-permute-start | bytes 491528 | tf_op jit(solution)/shard_map/ppermute | solution.py:171
  7.4 9.9 %collective-permute-start.5 = (bf16[64,1280]{1,0:T(8,128)(2,1)}, bf16[64,1280]{1,0:T(8,128)(2,1)S(1)}, u32[]{:S(2)}, u32[]{:S(2)}) collective-permute-start(bf16[64,1280]{1,0:T(8,128)(2,1)} %get-tuple-element.49), channel_id=1, source_target_pairs={{0,16},{1,17},{2,18},{3,19},{4,20},{5,21},{6,22},{7,23},{8,24},{9,... | collective-permute-start | bytes 491528 | tf_op jit(solution)/shard_map/ppermute | solution.py:171
  9.9 7.5 %collective-permute-start.6 = (bf16[64,1280]{1,0:T(8,128)(2,1)}, bf16[64,1280]{1,0:T(8,128)(2,1)S(1)}, u32[]{:S(2)}, u32[]{:S(2)}) collective-permute-start(bf16[64,1280]{1,0:T(8,128)(2,1)} %get-tuple-element.50), channel_id=1, source_target_pairs={{0,24},{1,25},{2,26},{3,27},{4,28},{5,29},{6,30},{7,31},{8,16},{9,... | collective-permute-start | bytes 491528 | tf_op jit(solution)/shard_map/ppermute | solution.py:171
  11.9 5.4 %collective-permute-start.3 = (bf16[128,256]{1,0:T(8,128)(2,1)S(1)}, bf16[128,256]{1,0:T(8,128)(2,1)S(1)}, u32[]{:S(2)}, u32[]{:S(2)}) collective-permute-start(bf16[128,256]{1,0:T(8,128)(2,1)S(1)} %pad_maximum_fusion), channel_id=1, source_target_pairs={{0,4},{1,5},{2,6},{3,7},{4,0},{5,1},{6,2},{7,3},{8,12},{9,13},{10,... | collective-permute-start | bytes 196616 | tf_op jit(solution)/shard_map/ppermute | solution.py:171
  17.5 0.9 %copy-start.1 = (bf16[64,1280]{1,0:T(8,128)(2,1)S(1)}, bf16[64,1280]{1,0:T(8,128)(2,1)}, u32[]{:S(2)}) copy-start(bf16[64,1280]{1,0:T(8,128)(2,1)} %get-tuple-element.53.refs_0_) | copy-start | bytes 491524
  18.7 17.6 %collective-permute-start.8 = (bf16[32,64,128]{2,1,0:T(8,128)(2,1)}, bf16[32,64,128]{2,1,0:T(8,128)(2,1)S(1)}, u32[]{:S(2)}, u32[]{:S(2)}) collective-permute-start(bf16[32,64,128]{2,1,0:T(8,128)(2,1)} %get-tuple-element.65.refs_0_), channel_id=1, source_target_pairs={{0,16},{1,17},{2,18},{3,19},{4,20},{5,21},{6,22},{7,23},{8,24},{9,... | collective-permute-start | bytes 1572872 | tf_op jit(solution)/shard_map/ppermute | solution.py:171
  20.5 7.7 %collective-permute-start.9 = (bf16[32,1024]{1,0:T(8,128)(2,1)S(1)}, bf16[32,1024]{1,0:T(8,128)(2,1)S(1)}, u32[]{:S(2)}, u32[]{:S(2)}) collective-permute-start(bf16[32,1024]{1,0:T(8,128)(2,1)S(1)} %get-tuple-element.66), channel_id=1, source_target_pairs={{0,7},{1,6},{2,5},{3,4},{4,3},{5,2},{6,1},{7,0},{8,15},{9,14},{10,... | collective-permute-start | bytes 196616 | tf_op jit(solution)/shard_map/ppermute | solution.py:171
  25.0 6.2 %collective-permute-start.10 = (bf16[32,1024]{1,0:T(8,128)(2,1)S(1)}, bf16[32,1024]{1,0:T(8,128)(2,1)S(1)}, u32[]{:S(2)}, u32[]{:S(2)}) collective-permute-start(bf16[32,1024]{1,0:T(8,128)(2,1)S(1)} %get-tuple-element.67), channel_id=1, source_target_pairs={{0,6},{1,7},{2,4},{3,5},{4,2},{5,3},{6,0},{7,1},{8,14},{9,15},{10,... | collective-permute-start | bytes 196616 | tf_op jit(solution)/shard_map/ppermute | solution.py:171
  25.2 9.9 %collective-permute-start.11 = (bf16[32,1024]{1,0:T(8,128)(2,1)S(1)}, bf16[32,1024]{1,0:T(8,128)(2,1)S(1)}, u32[]{:S(2)}, u32[]{:S(2)}) collective-permute-start(bf16[32,1024]{1,0:T(8,128)(2,1)S(1)} %get-tuple-element.68), channel_id=1, source_target_pairs={{0,5},{1,4},{2,7},{3,6},{4,1},{5,0},{6,3},{7,2},{8,13},{9,12},{10,... | collective-permute-start | bytes 196616 | tf_op jit(solution)/shard_map/ppermute | solution.py:171
  26.0 10.3 %collective-permute-start.12 = (bf16[32,1024]{1,0:T(8,128)(2,1)S(1)}, bf16[32,1024]{1,0:T(8,128)(2,1)S(1)}, u32[]{:S(2)}, u32[]{:S(2)}) collective-permute-start(bf16[32,1024]{1,0:T(8,128)(2,1)S(1)} %get-tuple-element.69), channel_id=1, source_target_pairs={{0,4},{1,5},{2,6},{3,7},{4,0},{5,1},{6,2},{7,3},{8,12},{9,13},{10,... | collective-permute-start | bytes 196616 | tf_op jit(solution)/shard_map/ppermute | solution.py:171
  28.1 11.7 %collective-permute-start.7 = (bf16[32,64,128]{2,1,0:T(8,128)(2,1)}, bf16[32,64,128]{2,1,0:T(8,128)(2,1)S(1)}, u32[]{:S(2)}, u32[]{:S(2)}) collective-permute-start(bf16[32,64,128]{2,1,0:T(8,128)(2,1)} %get-tuple-element.65.refs_0_), channel_id=1, source_target_pairs={{0,8},{1,9},{2,10},{3,11},{4,12},{5,13},{6,14},{7,15},{8,0},{9,1},... | collective-permute-start | bytes 1572872 | tf_op jit(solution)/shard_map/ppermute | solution.py:171
  36.3 3.5 %collective-permute-start.13 = (bf16[32,64,128]{2,1,0:T(8,128)(2,1)S(1)}, bf16[32,64,128]{2,1,0:T(8,128)(2,1)S(1)}, u32[]{:S(2)}, u32[]{:S(2)}) collective-permute-start(bf16[32,64,128]{2,1,0:T(8,128)(2,1)S(1)} %collective-permute-done.8.refs_2_), channel_id=1, source_target_pairs={{0,8},{1,9},{2,10},{3,11},{4,12},{5,13},{6,14},{7,15},{8,0},{9,1},... | collective-permute-start | bytes 1572872 | tf_op jit(solution)/shard_map/ppermute | solution.py:171
  36.3 7.6 %collective-permute-start.14 = (bf16[32,1024]{1,0:T(8,128)(2,1)S(1)}, bf16[32,1024]{1,0:T(8,128)(2,1)S(1)}, u32[]{:S(2)}, u32[]{:S(2)}) collective-permute-start(bf16[32,1024]{1,0:T(8,128)(2,1)S(1)} %get-tuple-element.72), channel_id=1, source_target_pairs={{0,1},{1,0},{2,3},{3,2},{4,5},{5,4},{6,7},{7,6},{8,9},{9,8},{10,11... | collective-permute-start | bytes 196616 | tf_op jit(solution)/shard_map/ppermute | solution.py:171
  37.1 6.8 %collective-permute-start.15 = (bf16[32,1024]{1,0:T(8,128)(2,1)S(1)}, bf16[32,1024]{1,0:T(8,128)(2,1)S(1)}, u32[]{:S(2)}, u32[]{:S(2)}) collective-permute-start(bf16[32,1024]{1,0:T(8,128)(2,1)S(1)} %get-tuple-element.73), channel_id=1, source_target_pairs={{0,2},{1,3},{2,0},{3,1},{4,6},{5,7},{6,4},{7,5},{8,10},{9,11},{10,... | collective-permute-start | bytes 196616 | tf_op jit(solution)/shard_map/ppermute | solution.py:171
  37.1 6.8 %collective-permute-start.16 = (bf16[32,1024]{1,0:T(8,128)(2,1)S(1)}, bf16[32,1024]{1,0:T(8,128)(2,1)S(1)}, u32[]{:S(2)}, u32[]{:S(2)}) collective-permute-start(bf16[32,1024]{1,0:T(8,128)(2,1)S(1)} %get-tuple-element.74), channel_id=1, source_target_pairs={{0,3},{1,2},{2,1},{3,0},{4,7},{5,6},{6,5},{7,4},{8,11},{9,10},{10,... | collective-permute-start | bytes 196616 | tf_op jit(solution)/shard_map/ppermute | solution.py:171
  39.8 1.0 %copy-start = (bf16[32,64,128]{2,1,0:T(8,128)(2,1)S(1)}, bf16[32,64,128]{2,1,0:T(8,128)(2,1)}, u32[]{:S(2)}) copy-start(bf16[32,64,128]{2,1,0:T(8,128)(2,1)} %get-tuple-element.65.refs_0_) | copy-start | bytes 1572868
  40.8 0.7 %copy-start.2 = (s32[8,8]{1,0:T(8,128)S(1)}, s32[8,8]{1,0:T(8,128)}, u32[]{:S(2)}) copy-start(s32[8,8]{1,0:T(8,128)} %mask.1) | copy-start | bytes 772
  44.7 4.7 %collective-permute-start.19 = (f32[32,128]{1,0:T(8,128)S(1)}, f32[32,128]{1,0:T(8,128)S(1)}, u32[]{:S(2)}, u32[]{:S(2)}) collective-permute-start(f32[32,128]{1,0:T(8,128)S(1)} %shard_map.58), channel_id=1, source_target_pairs={{0,3},{1,2},{2,1},{3,0},{4,7},{5,6},{6,5},{7,4},{8,11},{9,10},{10,... | collective-permute-start | bytes 49160 | tf_op jit(solution)/shard_map/ppermute | solution.py:171
  45.7 3.7 %collective-permute-start.18 = (f32[32,128]{1,0:T(8,128)S(1)}, f32[32,128]{1,0:T(8,128)S(1)}, u32[]{:S(2)}, u32[]{:S(2)}) collective-permute-start(f32[32,128]{1,0:T(8,128)S(1)} %shard_map.58), channel_id=1, source_target_pairs={{0,2},{1,3},{2,0},{3,1},{4,6},{5,7},{6,4},{7,5},{8,10},{9,11},{10,... | collective-permute-start | bytes 49160 | tf_op jit(solution)/shard_map/ppermute | solution.py:171
  47.0 3.7 %collective-permute-start.17 = (f32[32,128]{1,0:T(8,128)S(1)}, f32[32,128]{1,0:T(8,128)S(1)}, u32[]{:S(2)}, u32[]{:S(2)}) collective-permute-start(f32[32,128]{1,0:T(8,128)S(1)} %shard_map.58), channel_id=1, source_target_pairs={{0,1},{1,0},{2,3},{3,2},{4,5},{5,4},{6,7},{7,6},{8,9},{9,8},{10,11... | collective-permute-start | bytes 49160 | tf_op jit(solution)/shard_map/ppermute | solution.py:171
  50.7 4.6 %collective-permute-start.20 = (f32[32,128]{1,0:T(8,128)S(1)}, f32[32,128]{1,0:T(8,128)S(1)}, u32[]{:S(2)}, u32[]{:S(2)}) collective-permute-start(f32[32,128]{1,0:T(8,128)S(1)} %add_add_fusion), channel_id=1, source_target_pairs={{0,4},{1,5},{2,6},{3,7},{4,0},{5,1},{6,2},{7,3},{8,12},{9,13},{10,... | collective-permute-start | bytes 49160 | tf_op jit(solution)/shard_map/ppermute | solution.py:171

commit v3 on v2

--- a/solution.py
+++ b/solution.py
@@ -8,7 +8,7 @@
 from jax.sharding import PartitionSpec as P
 
 VMEM_LIMIT = 24 * 1024 * 1024
-PACK_VMEM_LIMIT = 56 * 1024 * 1024
+NEAR = 3
 BF16 = jnp.bfloat16
 F32 = jnp.float32
 
@@ -67,21 +67,23 @@
     return items
 
 
-def pack_kernel(n_split, mask_hbm, b_hbm, occ_hbm, basis_ref, *rest):
-    outs, (mask, b, green, sems) = rest[:n_split], rest[n_split:]
-    copies = [
-        pltpu.make_async_copy(src, dst, sems.at[i])
-        for i, (src, dst) in enumerate(((b_hbm, b), (occ_hbm, green), (mask_hbm, mask)))
-    ]
+def pack_kernel(n_split, occ_mask_hbm, virt_mask_hbm, b_hbm, occ_hbm, virt_hbm, basis_ref, virt_ref, *rest):
+    outs, (occ_mask, virt_mask, b, occ_green, virt_green, sems) = rest[:n_split], rest[n_split:]
+    pairs = (
+        (b_hbm, b), (occ_hbm, occ_green), (virt_hbm, virt_green), (occ_mask_hbm, occ_mask), (virt_mask_hbm, virt_mask)
+    )
+    copies = [pltpu.make_async_copy(src, dst, sems.at[i]) for i, (src, dst) in enumerate(pairs)]
     for copy in copies:
         copy.start()
     s, t = lax.axis_index("split"), lax.axis_index("tensor")
     rows, cols, naux = b.shape
     group = cols // n_split
-    block = green.shape[1] // mask.shape[0]
+    block = occ_green.shape[1] // occ_mask.shape[0]
     for copy in copies[1:]:
         copy.wait()
-    occ = screened(green[...], mask, s * (rows // block), block)
+    virt = screened(virt_green[...], virt_mask, t * (cols // block), block)
+    virt_ref[...] = virt.astype(BF16)
+    occ = screened(occ_green[...], occ_mask, s * (rows // block), block)
     occ = xor_blocks(occ, cols, t).astype(BF16)
     for m in range(n_split):
         outs[m][:, group * naux:] = occ
@@ -94,39 +96,53 @@
             outs[m][:, l * naux:(l + 1) * naux] = tiles[m]
 
 
-def first_kernel(n_split, n_tensor, width, *refs):
-    packed, outs = refs[:n_split], refs[n_split:]
+def first_kernel(n_split, n_tensor, width, basis_ref, own_ref, *refs):
+    packed, fetched, outs = refs[:n_split], refs[n_split:-n_tensor - 1], refs[-n_tensor - 1:]
     whole = jnp.concatenate([p[...] for p in packed], axis=0)
     first = lax.dot_general(
         whole[:, width:], whole[:, :width], (((0,), (0,)), ((), ())), preferred_element_type=F32
     )
-    rows = first.shape[0] // n_tensor
+    cols, rows, naux = basis_ref.shape
     for k in range(n_tensor):
-        outs[k][...] = first[k * rows:(k + 1) * rows].astype(BF16)
-
-
-def g_kernel(n_split, n_tensor, mask, virt_ref, *refs):
-    out, virt = refs[n_split], refs[n_split + 1]
-    part, step = out.shape[0], out.shape[1]
-    nao = virt.shape[0]
-    cols = nao // n_tensor
-    rows = nao // n_split
-    block = nao // mask.shape[0]
-    s, t = lax.axis_index("split"), lax.axis_index("tensor")
-
-    @pl.when((pl.program_id(0) == 0) & (pl.program_id(1) == 0))
-    def _():
-        for k in range(n_tensor):
-            piece = slice(k * cols, (k + 1) * cols)
-            kept = screened(virt_ref[piece, :], mask, (t ^ k) * (cols // block), block)
-            virt[piece, :] = xor_blocks(kept, rows, s).astype(BF16)
-
-    left = virt[pl.ds(pl.multiple_of(pl.program_id(1) * part, part), part), :]
-    made = []
-    for n in range(step):
-        right = jnp.concatenate([r[n] for r in refs[:n_split]], axis=0)
-        made.append(jnp.dot(left, right, preferred_element_type=F32).astype(BF16))
-    out[...] = jnp.swapaxes(jnp.stack(made), 0, 1)
+        outs[k][...] = first[k * cols:(k + 1) * cols].astype(BF16)
+    raw = outs[n_tensor]
+    raw[:cols] = basis_ref[...]
+    at = cols * rows
+    for j, ref in enumerate(fetched):
+        block = ref[...]
+        if j == 0:
+            block = jnp.where(lax.axis_index("split") == 0, own_ref[...], block)
+        for c in range(block.shape[1] // naux):
+            raw[at // rows, at % rows:at % rows + cols, :] = block[:, c * naux:(c + 1) * naux]
+            at += cols
+
+
+def g_kernel(n_split, n_tensor, *refs):
+    raws, out, virt = refs[:n_split], refs[n_split], refs[n_split + 1]
+    nao, cols, naux = out.shape
+    rows = raws[0].shape[1]
+    s = lax.axis_index("split")
+    at = cols * rows
+    for j in range(n_tensor // n_split):
+        for c in range(nao // naux):
+            tiles = xor_list([r[at // rows, at % rows:at % rows + cols, :] for r in raws], s)
+            for m, tile in enumerate(tiles):
+                k = j * n_split + m
+                virt[k * cols:(k + 1) * cols, c * naux:(c + 1) * naux] = tile
+            at += cols
+    virt[...] = xor_blocks(virt[...], rows, s)
+    part, step = min(nao, 256), 16
+
+    @pl.loop(0, nao // part)
+    def _(i):
+        band = pl.ds(pl.multiple_of(i * part, part), part)
+        left = virt[band, :]
+        for start in range(0, cols, step):
+            made = []
+            for n in range(start, start + step):
+                right = jnp.concatenate([r[n] for r in raws], axis=0)
+                made.append(jnp.dot(left, right, preferred_element_type=F32).astype(BF16))
+            out[band, start:start + step, :] = jnp.swapaxes(jnp.stack(made), 0, 1)
 
 
 def last_kernel(n_split, n_tensor, scale, g_ref, *refs):
@@ -162,7 +178,6 @@
     packed_width = cols // n_split * naux
     count = n_split * n_tensor
     params = pltpu.CompilerParams(vmem_limit_bytes=VMEM_LIMIT)
-    smem = pl.BlockSpec(memory_space=pltpu.SMEM)
     vmem = pl.BlockSpec(memory_space=pltpu.VMEM)
     hbm = pl.BlockSpec(memory_space=pltpu.HBM)
 
@@ -170,60 +185,63 @@
         bits = split_bits * n_tensor + tensor_bits
         return lax.ppermute(x, ("split", "tensor"), [(d, d ^ bits) for d in range(count)])
 
-    basis, *packed = pl.pallas_call(
+    def fetch(x, j):
+        pairs = [(s * n_tensor + t, s * n_tensor + (t ^ (j * n_split + s))) for s in range(n_split) for t in range(n_tensor)]
+        return lax.ppermute(x, ("split", "tensor"), [(a, b) for a, b in pairs if a != b])
+
+    arguments = [occ_mask, virt_mask, three_centre, green_occ, green_virt]
+    basis, virt, *packed = pl.pallas_call(
         functools.partial(pack_kernel, n_split),
-        out_shape=[jax.ShapeDtypeStruct((cols, rows, naux), BF16)]
+        out_shape=[jax.ShapeDtypeStruct((cols, rows, naux), BF16), jax.ShapeDtypeStruct(green_virt.shape, BF16)]
         + [jax.ShapeDtypeStruct((rows, packed_width + nao), BF16)] * n_split,
-        in_specs=[hbm] * 3,
-        out_specs=[vmem] * (n_split + 1),
+        in_specs=[hbm] * 5,
+        out_specs=[vmem] * (n_split + 2),
         scratch_shapes=[
             pltpu.SMEM(occ_mask.shape, jnp.int32),
+            pltpu.SMEM(virt_mask.shape, jnp.int32),
             pltpu.VMEM(three_centre.shape, BF16),
             pltpu.VMEM(green_occ.shape, BF16),
-            pltpu.SemaphoreType.DMA((3,)),
+            pltpu.VMEM(green_virt.shape, BF16),
+            pltpu.SemaphoreType.DMA((5,)),
         ],
-        compiler_params=pltpu.CompilerParams(vmem_limit_bytes=PACK_VMEM_LIMIT),
-    )(occ_mask, three_centre, green_occ)
-    virt, *packed = lax.optimization_barrier((green_virt, *packed))
+        compiler_params=params,
+    )(*[pltpu.with_memory_space_constraint(x, pltpu.HBM) for x in arguments])
     packed = [packed[0]] + [exchange(packed[m], split_bits=m) for m in range(1, n_split)]
 
-    for near in stages(n_tensor):
-        virt = jnp.concatenate([virt] + [exchange(virt, tensor_bits=k) for k in near], axis=0)
-
-    virt, *packed = lax.optimization_barrier((virt, *packed))
-
-    firsts = pl.pallas_call(
+    own = virt
+    virt, packed[1] = lax.optimization_barrier((virt, packed[1]))
+    fetched = [fetch(virt, j) for j in range(n_tensor // n_split)]
+
+    slots = n_tensor // n_split * nao // rows * cols // naux
+    *firsts, raw = pl.pallas_call(
         functools.partial(first_kernel, n_split, n_tensor, packed_width),
-        out_shape=[jax.ShapeDtypeStruct((cols, packed_width), BF16)] * n_tensor,
-        in_specs=[vmem] * n_split,
-        out_specs=[vmem] * n_tensor,
-        compiler_params=params,
-    )(*packed)
-    basis, *firsts = lax.optimization_barrier((basis, *firsts))
-
-    held = {0: basis}
+        out_shape=[jax.ShapeDtypeStruct((cols, packed_width), BF16)] * n_tensor
+        + [jax.ShapeDtypeStruct((cols + slots, rows, naux), BF16)],
+        in_specs=[vmem] * (2 + n_split + len(fetched)),
+        out_specs=[vmem] * (n_tensor + 1),
+        compiler_params=params,
+    )(basis, own, *packed, *fetched)
+
+    held = {0: raw}
     bit = n_split // 2
-    held[bit] = exchange(basis, split_bits=bit)
-    half = n_tensor // 2
-    far = [exchange(firsts[k], tensor_bits=k) for k in reversed(range(half, n_tensor))]
-    held[bit], *far = lax.optimization_barrier((held[bit], *far))
-    near = [exchange(firsts[k], tensor_bits=k) for k in reversed(range(1, half))]
-    firsts = [firsts[0], *near[::-1], *far[::-1]]
+    held[bit] = exchange(raw, split_bits=bit)
+    got = {0: firsts[0]}
+    got.update({k: exchange(firsts[k], tensor_bits=k) for k in range(n_tensor - 1, 0, -1)})
+    together = range(NEAR, n_tensor)
+    held[bit], *tied = lax.optimization_barrier((held[bit], *[got[k] for k in together]))
+    got.update(zip(together, tied))
     while bit > 1:
         bit //= 2
         held.update({m | bit: exchange(x, split_bits=bit) for m, x in held.items()})
 
-    step, part = 16, min(nao, 256)
     g = pl.pallas_call(
         functools.partial(g_kernel, n_split, n_tensor),
-        grid=(cols // step, nao // part),
         out_shape=jax.ShapeDtypeStruct((nao, cols, naux), BF16),
-        in_specs=[smem, pl.BlockSpec((nao, nao), lambda i, j: (0, 0))]
-        + [pl.BlockSpec((step, rows, naux), lambda i, j: (i, 0, 0))] * n_split,
-        out_specs=pl.BlockSpec((part, step, naux), lambda i, j: (j, i, 0)),
+        in_specs=[vmem] * n_split,
+        out_specs=vmem,
         scratch_shapes=[pltpu.VMEM((nao, nao), BF16)],
         compiler_params=params,
-    )(virt_mask, virt, *[held[m] for m in range(n_split)])
+    )(*[held[m] for m in range(n_split)])
 
     total = pl.pallas_call(
         functools.partial(last_kernel, n_split, n_tensor, 1.0 / nao),
@@ -231,7 +249,7 @@
         in_specs=[vmem] * (1 + n_tensor),
         out_specs=vmem,
         compiler_params=params,
-    )(g, *firsts)
+    )(g, *[got[k] for k in range(n_tensor)])
     for near in stages(n_tensor):
         got = [exchange(total, tensor_bits=k) for k in near]
         for x in got:

time: 56.4 us -> 49.1 us (0.87)
  local copies, waits for them, and re-layouts: 3.37 us -> 0 us
  waiting for transfers between devices: 17.7 us -> 15.2 us
  Pallas kernels: 6.13 us -> 4.74 us
  starting transfers between devices: 27.3 us -> 28.2 us
  other arithmetic: 1.34 us -> 0.62 us
    ppermute x0 -> x2, starting transfers between devices: none -> 3.48 us  [fetch(): lax.ppermute(x, ('split', 'tensor'), [(a, b) for a, b in pairs if a != b])]
    unnamed x10 -> x0, local copies, waits for them, and re-layouts: 3.37 us -> none
    ppermute x21 -> x17, starting transfers between devices: 27.3 us -> 24.8 us  [exchange(): lax.ppermute(x, ('split', 'tensor'), [(d, d ^ bits) for d in range(count)])]
    ppermute x21 -> x17, waiting for transfers between devices: 17.7 us -> 15.2 us  [exchange(): lax.ppermute(x, ('split', 'tensor'), [(d, d ^ bits) for d in range(count)])]
    pallas_call x1, Pallas kernels: 2.7 us -> 1.88 us  [local(): pl.pallas_call(functools.partial(pack_kernel, n_split), out_shape=[jax.Sh...]
    concatenate x1 -> x0, other arithmetic: 0.72 us -> none  [local(): jnp.concatenate([virt] + [exchange(virt, tensor_bits=k) for k in near], a...]
  transfers between devices with their start and end apart: 21 -> 19, of which waited for: 11 -> 11; matrix products, arithmetic and copies ran while one was open for 3% -> 0% of each run, Pallas kernels for 4% -> 4%
where the time goes in v3:
time: 49.1 us; the launch traced here: 48.9 us
  starting transfers between devices  28.2 us (57%)
  waiting for transfers between devices  15.2 us (31%)
  Pallas kernels  4.74 us (10%)
  other arithmetic  0.62 us (1%)
    ppermute x17, starting transfers between devices, exchange(): lax.ppermute(x, ('split', 'tensor'), [(d, d ^ bits) for d in range(count)])  24.8 us
    ppermute x17, waiting for transfers between devices, exchange(): lax.ppermute(x, ('split', 'tensor'), [(d, d ^ bits) for d in range(count)])  15.2 us
    ppermute x2, starting transfers between devices, fetch(): lax.ppermute(x, ('split', 'tensor'), [(a, b) for a, b in pairs if a != b])  3.48 us
    pallas_call x1, Pallas kernels, local(): pl.pallas_call(functools.partial(pack_kernel, n_split), out_shape=[jax.Sh...  1.88 us
    pallas_call x1, Pallas kernels, local(): pl.pallas_call(functools.partial(g_kernel, n_split, n_tensor), out_shape=...  1.8 us
  transfers between devices with their start and end apart: 19, of which 11 were waited for; matrix products, arithmetic and copies ran while one was open for 0% of the time, Pallas kernels for 4%

profile of v3, /device:TPU:0, one launch (start us, length us, event | category | flops | bytes accessed | tf_op | source)
XLA Modules:
  0.0 48.9 jit_solution(3005897380344465505)
XLA Ops:
  0.0 1.9 %shard_map.55 = (bf16[32,64,128]{2,1,0:T(8,128)(2,1)S(1)}, bf16[32,256]{1,0:T(8,128)(2,1)S(1)}, bf16[64,1280]{1,0:T(8,128)(2,1)S(1)}, bf16[64,1280]{1,0:T(8,128)...) custom-call(s32[8,8]{1,0:T(8,128)} %occ_mask_hbm.1, s32[8,8]{1,0:T(8,128)} %virt_mask_hbm.1, ...), custom_call_target="tpu_custom_call" | custom-call | tf_op jit(solution)/shard_map/pallas_call | solution.py:193
  1.9 0.5 %collective-permute-start = (bf16[64,1280]{1,0:T(8,128)(2,1)S(1)}, bf16[64,1280]{1,0:T(8,128)(2,1)S(1)}, u32[]{:S(2)}, u32[]{:S(2)}) collective-permute-start(bf16[64,1280]{1,0:T(8,128)(2,1)S(1)} %get-tuple-element.31), channel_id=1, source_target_pairs={{0,8},{1,9},{2,10},{3,11},{4,12},{5,13},{6,14},{7,15},{8,0},{9,1},... | collective-permute-start | bytes 491528 | tf_op jit(solution)/shard_map/ppermute | solution.py:186
  2.4 2.6 %collective-permute-start.1 = (bf16[64,1280]{1,0:T(8,128)(2,1)S(1)}, bf16[64,1280]{1,0:T(8,128)(2,1)S(1)}, u32[]{:S(2)}, u32[]{:S(2)}) collective-permute-start(bf16[64,1280]{1,0:T(8,128)(2,1)S(1)} %get-tuple-element.33), channel_id=1, source_target_pairs={{0,16},{1,17},{2,18},{3,19},{4,20},{5,21},{6,22},{7,23},{8,24},{9,... | collective-permute-start | bytes 491528 | tf_op jit(solution)/shard_map/ppermute | solution.py:186
  5.0 2.8 %collective-permute-start.4 = (bf16[32,256]{1,0:T(8,128)(2,1)S(1)}, bf16[32,256]{1,0:T(8,128)(2,1)S(1)}, u32[]{:S(2)}, u32[]{:S(2)}) collective-permute-start(bf16[32,256]{1,0:T(8,128)(2,1)S(1)} %get-tuple-element.35.own_ref), channel_id=1, source_target_pairs={{0,4},{1,5},{2,6},{3,7},{4,0},{5,1},{6,2},{7,3},{8,13},{9,12},{10,... | collective-permute-start | bytes 49160 | tf_op jit(solution)/shard_map/ppermute | solution.py:190
  7.9 0.7 %collective-permute-start.3 = (bf16[32,256]{1,0:T(8,128)(2,1)S(1)}, bf16[32,256]{1,0:T(8,128)(2,1)S(1)}, u32[]{:S(2)}, u32[]{:S(2)}) collective-permute-start(bf16[32,256]{1,0:T(8,128)(2,1)S(1)} %get-tuple-element.35.own_ref), channel_id=1, source_target_pairs={{8,9},{9,8},{10,11},{11,10},{12,13},{13,12},{14,15},{15,14},{16,18... | collective-permute-start | bytes 49160 | tf_op jit(solution)/shard_map/ppermute | solution.py:190
  8.5 1.5 %collective-permute-done.1.refs_2_ = bf16[64,1280]{1,0:T(8,128)(2,1)S(1)} collective-permute-done((bf16[64,1280]{1,0:T(8,128)(2,1)S(1)}, bf16[64,1280]{1,0:T(8,128)(2,1)S(1)}, u32[]{:S(2)}, u32[]{:S(2)}) %collective-permute-start.1) | collective-permute-done | bytes 163872 | tf_op jit(solution)/shard_map/ppermute | solution.py:186
  10.0 3.0 %collective-permute-done.2.refs_3_ = bf16[64,1280]{1,0:T(8,128)(2,1)S(1)} collective-permute-done((bf16[64,1280]{1,0:T(8,128)(2,1)S(1)}, bf16[64,1280]{1,0:T(8,128)(2,1)S(1)}, u32[]{:S(2)}, u32[]{:S(2)}) %collective-permute-start.2) | collective-permute-done | bytes 163872 | tf_op jit(solution)/shard_map/ppermute | solution.py:186
  13.0 0.3 shard_map.56
  13.3 3.2 %collective-permute-start.6 = (bf16[34,64,128]{2,1,0:T(8,128)(2,1)S(1)}, bf16[34,64,128]{2,1,0:T(8,128)(2,1)S(1)}, u32[]{:S(2)}, u32[]{:S(2)}) collective-permute-start(bf16[34,64,128]{2,1,0:T(8,128)(2,1)S(1)} %get-tuple-element.36.refs_0_), channel_id=1, source_target_pairs={{0,16},{1,17},{2,18},{3,19},{4,20},{5,21},{6,22},{7,23},{8,24},{9,... | collective-permute-start | bytes 1671176 | tf_op jit(solution)/shard_map/ppermute | solution.py:186
  16.6 1.0 %collective-permute-start.7 = (bf16[32,1024]{1,0:T(8,128)(2,1)S(1)}, bf16[32,1024]{1,0:T(8,128)(2,1)S(1)}, u32[]{:S(2)}, u32[]{:S(2)}) collective-permute-start(bf16[32,1024]{1,0:T(8,128)(2,1)S(1)} %get-tuple-element.37), channel_id=1, source_target_pairs={{0,3},{1,2},{2,1},{3,0},{4,7},{5,6},{6,5},{7,4},{8,11},{9,10},{10,... | collective-permute-start | bytes 196616 | tf_op jit(solution)/shard_map/ppermute | solution.py:186
  17.5 2.6 %collective-permute-start.8 = (bf16[32,1024]{1,0:T(8,128)(2,1)S(1)}, bf16[32,1024]{1,0:T(8,128)(2,1)S(1)}, u32[]{:S(2)}, u32[]{:S(2)}) collective-permute-start(bf16[32,1024]{1,0:T(8,128)(2,1)S(1)} %get-tuple-element.38), channel_id=1, source_target_pairs={{0,4},{1,5},{2,6},{3,7},{4,0},{5,1},{6,2},{7,3},{8,12},{9,13},{10,... | collective-permute-start | bytes 196616 | tf_op jit(solution)/shard_map/ppermute | solution.py:186
  20.1 0.3 collective-permute-start.9
  20.4 2.4 %collective-permute-start.10 = (bf16[32,1024]{1,0:T(8,128)(2,1)S(1)}, bf16[32,1024]{1,0:T(8,128)(2,1)S(1)}, u32[]{:S(2)}, u32[]{:S(2)}) collective-permute-start(bf16[32,1024]{1,0:T(8,128)(2,1)S(1)} %get-tuple-element.40), channel_id=1, source_target_pairs={{0,6},{1,7},{2,4},{3,5},{4,2},{5,3},{6,0},{7,1},{8,14},{9,15},{10,... | collective-permute-start | bytes 196616 | tf_op jit(solution)/shard_map/ppermute | solution.py:186
  22.9 0.5 collective-permute-done.7.refs_3_
  23.3 2.1 %collective-permute-start.11 = (bf16[32,1024]{1,0:T(8,128)(2,1)S(1)}, bf16[32,1024]{1,0:T(8,128)(2,1)S(1)}, u32[]{:S(2)}, u32[]{:S(2)}) collective-permute-start(bf16[32,1024]{1,0:T(8,128)(2,1)S(1)} %get-tuple-element.41), channel_id=1, source_target_pairs={{0,7},{1,6},{2,5},{3,4},{4,3},{5,2},{6,1},{7,0},{8,15},{9,14},{10,... | collective-permute-start | bytes 196616 | tf_op jit(solution)/shard_map/ppermute | solution.py:186
  25.4 1.5 %collective-permute-done.8.refs_4_ = bf16[32,1024]{1,0:T(8,128)(2,1)S(1)} collective-permute-done((bf16[32,1024]{1,0:T(8,128)(2,1)S(1)}, bf16[32,1024]{1,0:T(8,128)(2,1)S(1)}, u32[]{:S(2)}, u32[]{:S(2)}) %collective-permute-start.8) | collective-permute-done | bytes 65568 | tf_op jit(solution)/shard_map/ppermute | solution.py:186
  26.9 1.5 %collective-permute-done.9.refs_5_ = bf16[32,1024]{1,0:T(8,128)(2,1)S(1)} collective-permute-done((bf16[32,1024]{1,0:T(8,128)(2,1)S(1)}, bf16[32,1024]{1,0:T(8,128)(2,1)S(1)}, u32[]{:S(2)}, u32[]{:S(2)}) %collective-permute-start.9) | collective-permute-done | bytes 65568 | tf_op jit(solution)/shard_map/ppermute | solution.py:186
  28.4 2.0 %collective-permute-done.11.refs_7_ = bf16[32,1024]{1,0:T(8,128)(2,1)S(1)} collective-permute-done((bf16[32,1024]{1,0:T(8,128)(2,1)S(1)}, bf16[32,1024]{1,0:T(8,128)(2,1)S(1)}, u32[]{:S(2)}, u32[]{:S(2)}) %collective-permute-start.11) | collective-permute-done | bytes 65568 | tf_op jit(solution)/shard_map/ppermute | solution.py:186
  30.4 1.1 %collective-permute-start.13 = (bf16[32,1024]{1,0:T(8,128)(2,1)S(1)}, bf16[32,1024]{1,0:T(8,128)(2,1)S(1)}, u32[]{:S(2)}, u32[]{:S(2)}) collective-permute-start(bf16[32,1024]{1,0:T(8,128)(2,1)S(1)} %get-tuple-element.44), channel_id=1, source_target_pairs={{0,1},{1,0},{2,3},{3,2},{4,5},{5,4},{6,7},{7,6},{8,9},{9,8},{10,11... | collective-permute-start | bytes 196616 | tf_op jit(solution)/shard_map/ppermute | solution.py:186
  31.5 2.9 %collective-permute-start.14 = (bf16[32,1024]{1,0:T(8,128)(2,1)S(1)}, bf16[32,1024]{1,0:T(8,128)(2,1)S(1)}, u32[]{:S(2)}, u32[]{:S(2)}) collective-permute-start(bf16[32,1024]{1,0:T(8,128)(2,1)S(1)} %get-tuple-element.45), channel_id=1, source_target_pairs={{0,2},{1,3},{2,0},{3,1},{4,6},{5,7},{6,4},{7,5},{8,10},{9,11},{10,... | collective-permute-start | bytes 196616 | tf_op jit(solution)/shard_map/ppermute | solution.py:186
  34.4 1.8 %shard_map.57.g_ref = bf16[256,32,128]{2,1,0:T(8,128)(2,1)S(1)} custom-call(bf16[34,64,128]{2,1,0:T(8,128)(2,1)S(1)} %get-tuple-element.36.refs_0_, bf16[34,64,128]{2,1,0:T(8,128)(2,1)S(1)} %collective-permute-done.5.refs_1_, bf16[34,64,128]{2,1,0:T(8,128)(2,1)S(1)} %collective-permute-done.6.refs_2_, bf16[34,64,128]{2,1,0:T(8,128)(2,1)S(1)} %collective-permute-done.12.refs_3_), custom_call_target="tpu_custom_call" | custom-call | tf_op jit(solution)/shard_map/pallas_call | solution.py:237
  36.2 0.7 %collective-permute-done.14.refs_2_ = bf16[32,1024]{1,0:T(8,128)(2,1)S(1)} collective-permute-done((bf16[32,1024]{1,0:T(8,128)(2,1)S(1)}, bf16[32,1024]{1,0:T(8,128)(2,1)S(1)}, u32[]{:S(2)}, u32[]{:S(2)}) %collective-permute-start.14) | collective-permute-done | bytes 65568 | tf_op jit(solution)/shard_map/ppermute | solution.py:186
  36.9 0.7 %shard_map.58 = f32[32,128]{1,0:T(8,128)S(1)} custom-call(bf16[256,32,128]{2,1,0:T(8,128)(2,1)S(1)} %shard_map.57.g_ref, bf16[32,1024]{1,0:T(8,128)(2,1)S(1)} %get-tuple-element.43.refs_0_, bf16[32,1024]{1,0:T(8,128)(2,1)S(1)} %collective-permute-done.13.refs_1_, bf16[32,1024]{1,0:T(8,128)(2,1)S(1)} %collective-permute-done.14.refs_2_, ...), custom_call_target="tpu_custom_call" | custom-call | tf_op jit(solution)/shard_map/pallas_call | solution.py:246
  37.6 2.0 %collective-permute-start.17 = (f32[32,128]{1,0:T(8,128)S(1)}, f32[32,128]{1,0:T(8,128)S(1)}, u32[]{:S(2)}, u32[]{:S(2)}) collective-permute-start(f32[32,128]{1,0:T(8,128)S(1)} %shard_map.58), channel_id=1, source_target_pairs={{0,3},{1,2},{2,1},{3,0},{4,7},{5,6},{6,5},{7,4},{8,11},{9,10},{10,... | collective-permute-start | bytes 49160 | tf_op jit(solution)/shard_map/ppermute | solution.py:186
  39.6 0.2 collective-permute-start.16
  39.9 1.3 %collective-permute-start.15 = (f32[32,128]{1,0:T(8,128)S(1)}, f32[32,128]{1,0:T(8,128)S(1)}, u32[]{:S(2)}, u32[]{:S(2)}) collective-permute-start(f32[32,128]{1,0:T(8,128)S(1)} %shard_map.58), channel_id=1, source_target_pairs={{0,1},{1,0},{2,3},{3,2},{4,5},{5,4},{6,7},{7,6},{8,9},{9,8},{10,11... | collective-permute-start | bytes 49160 | tf_op jit(solution)/shard_map/ppermute | solution.py:186
  41.2 1.1 %collective-permute-done.17 = f32[32,128]{1,0:T(8,128)S(1)} collective-permute-done((f32[32,128]{1,0:T(8,128)S(1)}, f32[32,128]{1,0:T(8,128)S(1)}, u32[]{:S(2)}, u32[]{:S(2)}) %collective-permute-start.17) | collective-permute-done | bytes 16416 | tf_op jit(solution)/shard_map/ppermute | solution.py:186
  42.3 1.1 %collective-permute-done.16 = f32[32,128]{1,0:T(8,128)S(1)} collective-permute-done((f32[32,128]{1,0:T(8,128)S(1)}, f32[32,128]{1,0:T(8,128)S(1)}, u32[]{:S(2)}, u32[]{:S(2)}) %collective-permute-start.16) | collective-permute-done | bytes 16416 | tf_op jit(solution)/shard_map/ppermute | solution.py:186
  43.4 0.2 collective-permute-done.15
  43.6 2.5 %collective-permute-start.18 = (f32[32,128]{1,0:T(8,128)S(1)}, f32[32,128]{1,0:T(8,128)S(1)}, u32[]{:S(2)}, u32[]{:S(2)}) collective-permute-start(f32[32,128]{1,0:T(8,128)S(1)} %add_add_fusion), channel_id=1, source_target_pairs={{0,4},{1,5},{2,6},{3,7},{4,0},{5,1},{6,2},{7,3},{8,12},{9,13},{10,... | collective-permute-start | bytes 49160 | tf_op jit(solution)/shard_map/ppermute | solution.py:186
  46.1 2.2 %collective-permute-done.18 = f32[32,128]{1,0:T(8,128)S(1)} collective-permute-done((f32[32,128]{1,0:T(8,128)S(1)}, f32[32,128]{1,0:T(8,128)S(1)}, u32[]{:S(2)}, u32[]{:S(2)}) %collective-permute-start.18) | collective-permute-done | bytes 16416 | tf_op jit(solution)/shard_map/ppermute | solution.py:186
  48.3 0.6 %add.15 = f32[32,128]{1,0:T(8,128)} add(f32[32,128]{1,0:T(8,128)S(1)} %add_add_fusion, f32[32,128]{1,0:T(8,128)S(1)} %collective-permute-done.18) | non-fusion elementwise | flops 4096 | bytes 49152 | tf_op jit(solution)/shard_map/add | solution.py:256
  (12 shorter events, 0.1 us)
Async XLA Ops:
  1.9 3.2 %collective-permute-start = (bf16[64,1280]{1,0:T(8,128)(2,1)S(1)}, bf16[64,1280]{1,0:T(8,128)(2,1)S(1)}, u32[]{:S(2)}, u32[]{:S(2)}) collective-permute-start(bf16[64,1280]{1,0:T(8,128)(2,1)S(1)} %get-tuple-element.31), channel_id=1, source_target_pairs={{0,8},{1,9},{2,10},{3,11},{4,12},{5,13},{6,14},{7,15},{8,0},{9,1},... | collective-permute-start | bytes 491528 | tf_op jit(solution)/shard_map/ppermute | solution.py:186
  2.4 7.6 %collective-permute-start.1 = (bf16[64,1280]{1,0:T(8,128)(2,1)S(1)}, bf16[64,1280]{1,0:T(8,128)(2,1)S(1)}, u32[]{:S(2)}, u32[]{:S(2)}) collective-permute-start(bf16[64,1280]{1,0:T(8,128)(2,1)S(1)} %get-tuple-element.33), channel_id=1, source_target_pairs={{0,16},{1,17},{2,18},{3,19},{4,20},{5,21},{6,22},{7,23},{8,24},{9,... | collective-permute-start | bytes 491528 | tf_op jit(solution)/shard_map/ppermute | solution.py:186
  5.0 8.0 %collective-permute-start.2 = (bf16[64,1280]{1,0:T(8,128)(2,1)S(1)}, bf16[64,1280]{1,0:T(8,128)(2,1)S(1)}, u32[]{:S(2)}, u32[]{:S(2)}) collective-permute-start(bf16[64,1280]{1,0:T(8,128)(2,1)S(1)} %get-tuple-element.34), channel_id=1, source_target_pairs={{0,24},{1,25},{2,26},{3,27},{4,28},{5,29},{6,30},{7,31},{8,16},{9,... | collective-permute-start | bytes 491528 | tf_op jit(solution)/shard_map/ppermute | solution.py:186
  5.0 8.0 %collective-permute-start.4 = (bf16[32,256]{1,0:T(8,128)(2,1)S(1)}, bf16[32,256]{1,0:T(8,128)(2,1)S(1)}, u32[]{:S(2)}, u32[]{:S(2)}) collective-permute-start(bf16[32,256]{1,0:T(8,128)(2,1)S(1)} %get-tuple-element.35.own_ref), channel_id=1, source_target_pairs={{0,4},{1,5},{2,6},{3,7},{4,0},{5,1},{6,2},{7,3},{8,13},{9,12},{10,... | collective-permute-start | bytes 49160 | tf_op jit(solution)/shard_map/ppermute | solution.py:190
  7.9 5.1 %collective-permute-start.3 = (bf16[32,256]{1,0:T(8,128)(2,1)S(1)}, bf16[32,256]{1,0:T(8,128)(2,1)S(1)}, u32[]{:S(2)}, u32[]{:S(2)}) collective-permute-start(bf16[32,256]{1,0:T(8,128)(2,1)S(1)} %get-tuple-element.35.own_ref), channel_id=1, source_target_pairs={{8,9},{9,8},{10,11},{11,10},{12,13},{13,12},{14,15},{15,14},{16,18... | collective-permute-start | bytes 49160 | tf_op jit(solution)/shard_map/ppermute | solution.py:190
  13.3 17.0 %collective-permute-start.6 = (bf16[34,64,128]{2,1,0:T(8,128)(2,1)S(1)}, bf16[34,64,128]{2,1,0:T(8,128)(2,1)S(1)}, u32[]{:S(2)}, u32[]{:S(2)}) collective-permute-start(bf16[34,64,128]{2,1,0:T(8,128)(2,1)S(1)} %get-tuple-element.36.refs_0_), channel_id=1, source_target_pairs={{0,16},{1,17},{2,18},{3,19},{4,20},{5,21},{6,22},{7,23},{8,24},{9,... | collective-permute-start | bytes 1671176 | tf_op jit(solution)/shard_map/ppermute | solution.py:186
  16.6 6.8 %collective-permute-start.7 = (bf16[32,1024]{1,0:T(8,128)(2,1)S(1)}, bf16[32,1024]{1,0:T(8,128)(2,1)S(1)}, u32[]{:S(2)}, u32[]{:S(2)}) collective-permute-start(bf16[32,1024]{1,0:T(8,128)(2,1)S(1)} %get-tuple-element.37), channel_id=1, source_target_pairs={{0,3},{1,2},{2,1},{3,0},{4,7},{5,6},{6,5},{7,4},{8,11},{9,10},{10,... | collective-permute-start | bytes 196616 | tf_op jit(solution)/shard_map/ppermute | solution.py:186
  17.5 9.4 %collective-permute-start.8 = (bf16[32,1024]{1,0:T(8,128)(2,1)S(1)}, bf16[32,1024]{1,0:T(8,128)(2,1)S(1)}, u32[]{:S(2)}, u32[]{:S(2)}) collective-permute-start(bf16[32,1024]{1,0:T(8,128)(2,1)S(1)} %get-tuple-element.38), channel_id=1, source_target_pairs={{0,4},{1,5},{2,6},{3,7},{4,0},{5,1},{6,2},{7,3},{8,12},{9,13},{10,... | collective-permute-start | bytes 196616 | tf_op jit(solution)/shard_map/ppermute | solution.py:186
  20.1 8.3 %collective-permute-start.9 = (bf16[32,1024]{1,0:T(8,128)(2,1)S(1)}, bf16[32,1024]{1,0:T(8,128)(2,1)S(1)}, u32[]{:S(2)}, u32[]{:S(2)}) collective-permute-start(bf16[32,1024]{1,0:T(8,128)(2,1)S(1)} %get-tuple-element.39), channel_id=1, source_target_pairs={{0,5},{1,4},{2,7},{3,6},{4,1},{5,0},{6,3},{7,2},{8,13},{9,12},{10,... | collective-permute-start | bytes 196616 | tf_op jit(solution)/shard_map/ppermute | solution.py:186
  20.4 8.0 %collective-permute-start.10 = (bf16[32,1024]{1,0:T(8,128)(2,1)S(1)}, bf16[32,1024]{1,0:T(8,128)(2,1)S(1)}, u32[]{:S(2)}, u32[]{:S(2)}) collective-permute-start(bf16[32,1024]{1,0:T(8,128)(2,1)S(1)} %get-tuple-element.40), channel_id=1, source_target_pairs={{0,6},{1,7},{2,4},{3,5},{4,2},{5,3},{6,0},{7,1},{8,14},{9,15},{10,... | collective-permute-start | bytes 196616 | tf_op jit(solution)/shard_map/ppermute | solution.py:186
  23.3 7.0 %collective-permute-start.11 = (bf16[32,1024]{1,0:T(8,128)(2,1)S(1)}, bf16[32,1024]{1,0:T(8,128)(2,1)S(1)}, u32[]{:S(2)}, u32[]{:S(2)}) collective-permute-start(bf16[32,1024]{1,0:T(8,128)(2,1)S(1)} %get-tuple-element.41), channel_id=1, source_target_pairs={{0,7},{1,6},{2,5},{3,4},{4,3},{5,2},{6,1},{7,0},{8,15},{9,14},{10,... | collective-permute-start | bytes 196616 | tf_op jit(solution)/shard_map/ppermute | solution.py:186
  26.9 7.5 %collective-permute-start.5 = (bf16[34,64,128]{2,1,0:T(8,128)(2,1)S(1)}, bf16[34,64,128]{2,1,0:T(8,128)(2,1)S(1)}, u32[]{:S(2)}, u32[]{:S(2)}) collective-permute-start(bf16[34,64,128]{2,1,0:T(8,128)(2,1)S(1)} %get-tuple-element.36.refs_0_), channel_id=1, source_target_pairs={{0,8},{1,9},{2,10},{3,11},{4,12},{5,13},{6,14},{7,15},{8,0},{9,1},... | collective-permute-start | bytes 1671176 | tf_op jit(solution)/shard_map/ppermute | solution.py:186
  30.4 4.0 %collective-permute-start.12 = (bf16[34,64,128]{2,1,0:T(8,128)(2,1)S(1)}, bf16[34,64,128]{2,1,0:T(8,128)(2,1)S(1)}, u32[]{:S(2)}, u32[]{:S(2)}) collective-permute-start(bf16[34,64,128]{2,1,0:T(8,128)(2,1)S(1)} %collective-permute-done.6.refs_2_), channel_id=1, source_target_pairs={{0,8},{1,9},{2,10},{3,11},{4,12},{5,13},{6,14},{7,15},{8,0},{9,1},... | collective-permute-start | bytes 1671176 | tf_op jit(solution)/shard_map/ppermute | solution.py:186
  30.4 5.8 %collective-permute-start.13 = (bf16[32,1024]{1,0:T(8,128)(2,1)S(1)}, bf16[32,1024]{1,0:T(8,128)(2,1)S(1)}, u32[]{:S(2)}, u32[]{:S(2)}) collective-permute-start(bf16[32,1024]{1,0:T(8,128)(2,1)S(1)} %get-tuple-element.44), channel_id=1, source_target_pairs={{0,1},{1,0},{2,3},{3,2},{4,5},{5,4},{6,7},{7,6},{8,9},{9,8},{10,11... | collective-permute-start | bytes 196616 | tf_op jit(solution)/shard_map/ppermute | solution.py:186
  31.5 5.4 %collective-permute-start.14 = (bf16[32,1024]{1,0:T(8,128)(2,1)S(1)}, bf16[32,1024]{1,0:T(8,128)(2,1)S(1)}, u32[]{:S(2)}, u32[]{:S(2)}) collective-permute-start(bf16[32,1024]{1,0:T(8,128)(2,1)S(1)} %get-tuple-element.45), channel_id=1, source_target_pairs={{0,2},{1,3},{2,0},{3,1},{4,6},{5,7},{6,4},{7,5},{8,10},{9,11},{10,... | collective-permute-start | bytes 196616 | tf_op jit(solution)/shard_map/ppermute | solution.py:186
  37.6 4.7 %collective-permute-start.17 = (f32[32,128]{1,0:T(8,128)S(1)}, f32[32,128]{1,0:T(8,128)S(1)}, u32[]{:S(2)}, u32[]{:S(2)}) collective-permute-start(f32[32,128]{1,0:T(8,128)S(1)} %shard_map.58), channel_id=1, source_target_pairs={{0,3},{1,2},{2,1},{3,0},{4,7},{5,6},{6,5},{7,4},{8,11},{9,10},{10,... | collective-permute-start | bytes 49160 | tf_op jit(solution)/shard_map/ppermute | solution.py:186
  39.6 3.7 %collective-permute-start.16 = (f32[32,128]{1,0:T(8,128)S(1)}, f32[32,128]{1,0:T(8,128)S(1)}, u32[]{:S(2)}, u32[]{:S(2)}) collective-permute-start(f32[32,128]{1,0:T(8,128)S(1)} %shard_map.58), channel_id=1, source_target_pairs={{0,2},{1,3},{2,0},{3,1},{4,6},{5,7},{6,4},{7,5},{8,10},{9,11},{10,... | collective-permute-start | bytes 49160 | tf_op jit(solution)/shard_map/ppermute | solution.py:186
  39.9 3.7 %collective-permute-start.15 = (f32[32,128]{1,0:T(8,128)S(1)}, f32[32,128]{1,0:T(8,128)S(1)}, u32[]{:S(2)}, u32[]{:S(2)}) collective-permute-start(f32[32,128]{1,0:T(8,128)S(1)} %shard_map.58), channel_id=1, source_target_pairs={{0,1},{1,0},{2,3},{3,2},{4,5},{5,4},{6,7},{7,6},{8,9},{9,8},{10,11... | collective-permute-start | bytes 49160 | tf_op jit(solution)/shard_map/ppermute | solution.py:186
  43.6 4.6 %collective-permute-start.18 = (f32[32,128]{1,0:T(8,128)S(1)}, f32[32,128]{1,0:T(8,128)S(1)}, u32[]{:S(2)}, u32[]{:S(2)}) collective-permute-start(f32[32,128]{1,0:T(8,128)S(1)} %add_add_fusion), channel_id=1, source_target_pairs={{0,4},{1,5},{2,6},{3,7},{4,0},{5,1},{6,2},{7,3},{8,12},{9,13},{10,... | collective-permute-start | bytes 49160 | tf_op jit(solution)/shard_map/ppermute | solution.py:186

commit v4 on v3

v4 whole, which is shorter than its diff:
```python
import functools

import jax
import jax.numpy as jnp
from jax import lax
from jax.experimental import pallas as pl
from jax.experimental.pallas import tpu as pltpu
from jax.sharding import PartitionSpec as P

VMEM_LIMIT = 40 * 1024 * 1024
BF16 = jnp.bfloat16
F32 = jnp.float32


def xor_blocks(x, width, index):
    cols = x.shape[1]
    bit = 1
    while width * bit < cols:
        span = width * bit
        order = []
        for start in range(0, cols, 2 * span):
            order += [x[:, start + span:start + 2 * span], x[:, start:start + span]]
        x = jnp.where((index & bit) != 0, jnp.concatenate(order, axis=1), x)
        bit *= 2
    return x


def screened(green, mask_ref, first_row, block):
    rows, cols = green.shape
    column = lax.broadcasted_iota(jnp.int32, (1, cols), 1) // block
    parts = []
    for r in range(rows // block):
        keep = jnp.zeros((1, cols), jnp.int32)
        for c in range(cols // block):
            keep = jnp.where(column == c, mask_ref[first_row + r, c], keep)
        part = green[r * block:(r + 1) * block].astype(F32)
        parts.append(jnp.where(keep > 0, part, 0.0))
    return jnp.concatenate(parts, axis=0) if len(parts) > 1 else parts[0]


def swap_lane_blocks(tiles, width):
    tiles = list(tiles)
    count = len(tiles)
    lanes = tiles[0].shape[1]
    lane = lax.broadcasted_iota(jnp.int32, tiles[0].shape, 1)
    half = count // 2
    while half:
        span = half * width
        low = (lane // span) % 2 == 0
        for j in range(count):
            if j & half:
                continue
            a, b = tiles[j], tiles[j | half]
            tiles[j] = jnp.where(low, a, pltpu.roll(b, span, 1))
            tiles[j | half] = jnp.where(low, pltpu.roll(a, lanes - span, 1), b)
        half //= 2
    return tiles


def xor_list(items, index):
    bit = 1
    while bit < len(items):
        flag = (index & bit) != 0
        items = [jnp.where(flag, items[m ^ bit], items[m]) for m in range(len(items))]
        bit *= 2
    return items


def pack_kernel(n_split, occ_mask_hbm, virt_mask_hbm, b_hbm, occ_hbm, virt_hbm, virt_ref, *rest):
    outs, (occ_mask, virt_mask, b, occ_green, virt_green, sems) = rest[:n_split], rest[n_split:]
    pairs = (
        (b_hbm, b), (occ_hbm, occ_green), (virt_hbm, virt_green), (occ_mask_hbm, occ_mask), (virt_mask_hbm, virt_mask)
    )
    copies = [pltpu.make_async_copy(src, dst, sems.at[i]) for i, (src, dst) in enumerate(pairs)]
    for copy in copies:
        copy.start()
    s, t = lax.axis_index("split"), lax.axis_index("tensor")
    rows, cols, naux = b.shape
    group = cols // n_split
    block = occ_green.shape[1] // occ_mask.shape[0]
    for copy in copies[1:]:
        copy.wait()
    virt = screened(virt_green[...], virt_mask, t * (cols // block), block)
    virt_ref[...] = virt.astype(BF16)
    occ = screened(occ_green[...], occ_mask, s * (rows // block), block)
    occ = xor_blocks(occ, cols, t).astype(BF16)
    for m in range(n_split):
        outs[m][:, group * naux:] = occ
    copies[0].wait()
    basis = jnp.swapaxes(b[...], 0, 1)
    for l in range(group):
        tiles = swap_lane_blocks([basis[j * group + l] for j in range(n_split)], naux // n_split)
        tiles = xor_list(tiles, s)
        for m in range(n_split):
            outs[m][:, l * naux:(l + 1) * naux] = tiles[m]


def others(n_split, m):
    return [i for i in range(n_split) if i // 2 != m // 2]


def write_rows(out, start, blocks):
    rows, at = out.shape[0], 0
    for block in blocks:
        height = block.shape[0]
        for c in range(0, block.shape[1], 128):
            column = start + at // rows * 128
            out[at % rows:at % rows + height, column:column + 128] = block[:, c:c + 128]
            at += height


def read_rows(ref, start, count, height, width):
    rows, at, blocks = ref.shape[0], 0, []
    for _ in range(count):
        tiles = []
        for c in range(0, width, 128):
            column = start + at // rows * 128
            tiles.append(ref[at % rows:at % rows + height, column:column + 128])
            at += height
        blocks.append(jnp.concatenate(tiles, axis=1))
    return blocks


def first_kernel(n_split, n_tensor, width, own_virt, *refs):
    own, got, rest = refs[:n_split], refs[n_split:2 * n_split - 1], refs[2 * n_split - 1:]
    shares = n_tensor // n_split
    fetched, firsts, raws = rest[:shares], rest[shares:shares + n_tensor], rest[shares + n_tensor:]
    whole = jnp.concatenate([p[...] for p in (own[0], *got)], axis=0)
    first = lax.dot_general(
        whole[:, width:], whole[:, :width], (((0,), (0,)), ((), ())), preferred_element_type=F32
    )
    cols = first.shape[0] // n_tensor
    for k in range(n_tensor):
        firsts[k][...] = first[k * cols:(k + 1) * cols].astype(BF16)
    blocks = [f[...] for f in fetched]
    blocks[0] = jnp.where(lax.axis_index("split") == 0, own_virt[...], blocks[0])
    for p in range(1, n_split // 2):
        for n, i in enumerate(others(n_split, 2 * p)):
            raws[p - 1][:, n * width:(n + 1) * width] = own[i][:, :width]
        write_rows(raws[p - 1], (n_split - 2) * width, blocks)
    pieces = [own[i] for i in range(n_split) if i != 1] + list(got[1:])
    for n, piece in enumerate(pieces):
        raws[-1][:, n * width:(n + 1) * width] = piece[:, :width]
    write_rows(raws[-1], len(pieces) * width, blocks)


def g_kernel(n_split, n_tensor, width, *refs):
    own, got, refs = refs[:n_split], refs[n_split:2 * n_split - 1], refs[2 * n_split - 1:]
    raws, core, own_core, out, virt = refs[:n_split - 2], *refs[n_split - 2:]
    cols, nao, naux = out.shape
    rows = core.shape[0]
    group = cols // n_split
    shares = n_tensor // n_split
    s = lax.axis_index("split")

    def piece(m, q):
        if m == 0:
            return own[q], 0
        if q == 0:
            return got[m - 1], 0
        if m == 1:
            return core, [i for i in range(n_split) if i != 1].index(q ^ 1)
        if q == 1:
            return core, n_split - 1 + (m ^ 1) - 2
        return raws[m - 2], others(n_split, m).index(m ^ q)

    core_start = (2 * n_split - 3) * width
    found = [read_rows(own_core, core_start, shares, cols, nao), read_rows(core, core_start, shares, cols, nao)]
    found += [read_rows(r, (n_split - 2) * width, shares, cols, nao) for r in raws]
    blocks = [tile for i in range(shares) for tile in xor_list([f[i] for f in found], s)]
    ordered = xor_blocks(jnp.concatenate(blocks, axis=0), rows, s)
    row = lax.broadcasted_iota(jnp.int32, (nao, nao), 0)
    column = lax.broadcasted_iota(jnp.int32, (nao, nao), 1)
    j, k, l = row // (n_tensor * group), row // group % n_tensor, row % group
    place = jnp.where(column == k * cols + j * group + l, 1.0, 0.0).astype(BF16)
    virt[...] = jnp.dot(place, ordered, preferred_element_type=F32).astype(BF16)
    part = min(nao, 256)

    @pl.loop(0, nao // part)
    def _(i):
        band = pl.ds(pl.multiple_of(i * part, part), part)
        left = virt[band, :]
        for l in range(group):
            right = []
            for q in range(n_split):
                tiles = []
                for m in range(n_split):
                    ref, n = piece(m, q)
                    tiles.append(ref[:, n * width + l * naux:n * width + (l + 1) * naux])
                right.append(jnp.concatenate(tiles, axis=0))
            made = jnp.dot(left, jnp.concatenate(right, axis=1), preferred_element_type=F32).astype(BF16)
            tiles = swap_lane_blocks([made[:, q * naux:(q + 1) * naux] for q in range(n_split)], naux // n_split)
            for j, tile in enumerate(tiles):
                out[j * group + l, band, :] = tile


def last_kernel(n_split, n_tensor, scale, g_ref, *refs):
    firsts, out = refs[:n_tensor][::-1], refs[n_tensor]
    naux = g_ref.shape[2]
    group = firsts[0].shape[1] // naux
    width = naux // n_split
    depth = n_tensor * group
    left = jnp.stack([f[:, l * naux:(l + 1) * naux] for f in firsts for l in range(group)])
    left = jnp.swapaxes(left, 0, 1).reshape(-1, naux)
    right = [g_ref[:, j * depth:(j + 1) * depth, :].reshape(-1, naux) for j in range(n_split)]
    total = lax.dot_general(
        left, jnp.concatenate(right, axis=1), (((0,), (0,)), ((), ())), preferred_element_type=F32
    )
    result = total[:width, :naux]
    for j in range(1, n_split):
        result = result + total[j * width:(j + 1) * width, j * naux:(j + 1) * naux]
    out[...] = xor_blocks(result * scale, width, lax.axis_index("split"))


def stages(count):
    bit, found = 1, []
    while bit < count:
        found.append([bit, 2 * bit, 3 * bit] if 2 * bit < count else [bit])
        bit *= 4
    return found


def local(three_centre, green_occ, green_virt, occ_mask, virt_mask, *, n_split, n_tensor):
    rows, cols, naux = three_centre.shape
    nao = green_occ.shape[1]
    packed_width = cols // n_split * naux
    count = n_split * n_tensor
    params = pltpu.CompilerParams(vmem_limit_bytes=VMEM_LIMIT)
    vmem = pl.BlockSpec(memory_space=pltpu.VMEM)
    hbm = pl.BlockSpec(memory_space=pltpu.HBM)

    def exchange(x, split_bits=0, tensor_bits=0):
        bits = split_bits * n_tensor + tensor_bits
        return lax.ppermute(x, ("split", "tensor"), [(d, d ^ bits) for d in range(count)])

    def fetch(x, j):
        pairs = [(s * n_tensor + t, s * n_tensor + (t ^ (j * n_split + s))) for s in range(n_split) for t in range(n_tensor)]
        return lax.ppermute(x, ("split", "tensor"), [(a, b) for a, b in pairs if a != b])

    arguments = [occ_mask, virt_mask, three_centre, green_occ, green_virt]
    virt, *packed = pl.pallas_call(
        functools.partial(pack_kernel, n_split),
        out_shape=[jax.ShapeDtypeStruct(green_virt.shape, BF16)]
        + [jax.ShapeDtypeStruct((rows, packed_width + nao), BF16)] * n_split,
        in_specs=[hbm] * 5,
        out_specs=[vmem] * (n_split + 1),
        scratch_shapes=[
            pltpu.SMEM(occ_mask.shape, jnp.int32),
            pltpu.SMEM(virt_mask.shape, jnp.int32),
            pltpu.VMEM(three_centre.shape, BF16),
            pltpu.VMEM(green_occ.shape, BF16),
            pltpu.VMEM(green_virt.shape, BF16),
            pltpu.SemaphoreType.DMA((5,)),
        ],
        compiler_params=params,
    )(*[pltpu.with_memory_space_constraint(x, pltpu.HBM) for x in arguments])
    received = [exchange(packed[m], split_bits=m) for m in range(1, n_split)]

    own = virt
    virt, received[0] = lax.optimization_barrier((virt, received[0]))
    shares = n_tensor // n_split
    fetched = [fetch(virt, j) for j in range(shares)]

    virt_width = shares * nao * cols // rows
    widths = [(n_split - 2) * packed_width + virt_width] * (n_split // 2 - 1) + [(2 * n_split - 3) * packed_width + virt_width]
    made = pl.pallas_call(
        functools.partial(first_kernel, n_split, n_tensor, packed_width),
        out_shape=[jax.ShapeDtypeStruct((cols, packed_width), BF16)] * n_tensor
        + [jax.ShapeDtypeStruct((rows, w), BF16) for w in widths],
        in_specs=[vmem] * (2 * n_split + shares),
        out_specs=[vmem] * (n_tensor + len(widths)),
        compiler_params=params,
    )(own, *packed, *received, *fetched)
    firsts, raws = made[:n_tensor], made[n_tensor:]

    moved = {}
    moved.update({m: exchange(raws[m // 2 - 1], split_bits=m) for m in range(2, n_split, 2)})
    got = {0: firsts[0]}
    ahead = [n_tensor - 1, n_tensor - 2]
    got.update({k: exchange(firsts[k], tensor_bits=k) for k in ahead})
    later = [k for k in range(n_tensor - 1, 0, -1) if k not in ahead]
    evens = list(range(2, n_split, 2))
    tied = list(lax.optimization_barrier((*[got[k] for k in ahead], *[moved[m] for m in evens], raws[-1], *[firsts[k] for k in later])))
    got.update(zip(ahead, tied))
    moved.update(zip(evens, tied[len(ahead):]))
    moved[1] = exchange(tied.pop(len(ahead) + len(evens)), split_bits=1)
    firsts = dict(enumerate(firsts))
    firsts.update(zip(later, tied[len(ahead) + len(evens):]))
    got.update({k: exchange(firsts[k], tensor_bits=k) for k in later})
    got = [got[k] for k in range(n_tensor)]
    moved.update({m + 1: exchange(moved[m], split_bits=1) for m in range(2, n_split, 2)})
    moved = [moved[m] for m in range(2, n_split)] + [moved[1]]

    g = pl.pallas_call(
        functools.partial(g_kernel, n_split, n_tensor, packed_width),
        out_shape=jax.ShapeDtypeStruct((cols, nao, naux), BF16),
        in_specs=[vmem] * (3 * n_split - 1),
        out_specs=vmem,
        scratch_shapes=[pltpu.VMEM((nao, nao), BF16)],
        compiler_params=params,
    )(*packed, *received, *moved, raws[-1])

    total = pl.pallas_call(
        functools.partial(last_kernel, n_split, n_tensor, 1.0 / nao),
        out_shape=jax.ShapeDtypeStruct((naux // n_split, naux), F32),
        in_specs=[vmem] * (1 + n_tensor),
        out_specs=vmem,
        compiler_params=params,
    )(g, *got[::-1])
    for near in stages(n_tensor):
        got = [exchange(total, tensor_bits=k) for k in near]
        for x in got:
            total = total + x
    return total


def solution(mesh):
    sizes = dict(mesh.shape)
    return jax.shard_map(
        functools.partial(local, n_split=sizes["split"], n_tensor=sizes["tensor"]),
        mesh=mesh,
        in_specs=(P("split", "tensor", None), P("split", None), P("tensor", None), P(), P()),
        out_specs=P("split", None),
        check_vma=False,
    )
```

time: 49.1 us -> 48.7 us (level)
  starting transfers between devices: 28.2 us -> 26 us
  waiting for transfers between devices: 15.2 us -> 17.4 us
    ppermute x17, starting transfers between devices: 24.8 us -> 22.5 us  [exchange(): lax.ppermute(x, ('split', 'tensor'), [(d, d ^ bits) for d in range(count)])]
    ppermute x17, waiting for transfers between devices: 15.2 us -> 17.4 us  [exchange(): lax.ppermute(x, ('split', 'tensor'), [(d, d ^ bits) for d in range(count)])]
  transfers between devices with their start and end apart: 19 -> 19, of which waited for: 11 -> 10; matrix products, arithmetic and copies ran while one was open for 0% -> 0% of each run, Pallas kernels for 4% -> 3%
where the time goes in v4:
time: 48.7 us; the launch traced here: 48.6 us
  starting transfers between devices  26 us (53%)
  waiting for transfers between devices  17.4 us (36%)
  Pallas kernels  4.54 us (9%)
  other arithmetic  0.62 us (1%)
    ppermute x17, starting transfers between devices, exchange(): lax.ppermute(x, ('split', 'tensor'), [(d, d ^ bits) for d in range(count)])  22.5 us
    ppermute x17, waiting for transfers between devices, exchange(): lax.ppermute(x, ('split', 'tensor'), [(d, d ^ bits) for d in range(count)])  17.4 us
    ppermute x2, starting transfers between devices, fetch(): lax.ppermute(x, ('split', 'tensor'), [(a, b) for a, b in pairs if a != b])  3.48 us
    pallas_call x1, Pallas kernels, local(): pl.pallas_call(functools.partial(pack_kernel, n_split), out_shape=[jax.Sh...  1.9 us
    pallas_call x1, Pallas kernels, local(): pl.pallas_call(functools.partial(g_kernel, n_split, n_tensor, packed_widt...  1.65 us
  transfers between devices with their start and end apart: 19, of which 10 were waited for; matrix products, arithmetic and copies ran while one was open for 0% of the time, Pallas kernels for 3%

profile of v4, /device:TPU:0, one launch (start us, length us, event | category | flops | bytes accessed | tf_op | source)
XLA Modules:
  0.0 48.6 jit_solution(11461318245772921330)
XLA Ops:
  0.0 1.9 %shard_map.55 = (bf16[32,256]{1,0:T(8,128)(2,1)S(1)}, bf16[64,1280]{1,0:T(8,128)(2,1)S(1)}, bf16[64,1280]{1,0:T(8,128)(2,1)S(1)}, bf16[64,1280]{1,0:T(8,128)(2,1)S(1)}, bf16[64,1280]{1,0:T(8,128)(2,1)S(1)}) custom-call(s32[8,8]{1,0:T(8,128)} %occ_mask_hbm.1, s32[8,8]{1,0:T(8,128)} %virt_mask_hbm.1, bf16[64,32,128]{2,1,0:T(8,128)(2,1)} %b_hbm.1, ...), custom_call_target="tpu_custom_call" | custom-call | tf_op jit(solution)/shard_map/pallas_call | solution.py:241
  1.9 0.5 %collective-permute-start = (bf16[64,1280]{1,0:T(8,128)(2,1)S(1)}, bf16[64,1280]{1,0:T(8,128)(2,1)S(1)}, u32[]{:S(2)}, u32[]{:S(2)}) collective-permute-start(bf16[64,1280]{1,0:T(8,128)(2,1)S(1)} %get-tuple-element.32.refs_1_), channel_id=1, source_target_pairs={{0,8},{1,9},{2,10},{3,11},{4,12},{5,13},{6,14},{7,15},{8,0},{9,1},... | collective-permute-start | bytes 491528 | tf_op jit(solution)/shard_map/ppermute | solution.py:234
  2.4 2.6 %collective-permute-start.1 = (bf16[64,1280]{1,0:T(8,128)(2,1)S(1)}, bf16[64,1280]{1,0:T(8,128)(2,1)S(1)}, u32[]{:S(2)}, u32[]{:S(2)}) collective-permute-start(bf16[64,1280]{1,0:T(8,128)(2,1)S(1)} %get-tuple-element.33.refs_2_), channel_id=1, source_target_pairs={{0,16},{1,17},{2,18},{3,19},{4,20},{5,21},{6,22},{7,23},{8,24},{9,... | collective-permute-start | bytes 491528 | tf_op jit(solution)/shard_map/ppermute | solution.py:234
  5.0 0.1 collective-permute-start.2
  5.1 2.8 %collective-permute-start.4 = (bf16[32,256]{1,0:T(8,128)(2,1)S(1)}, bf16[32,256]{1,0:T(8,128)(2,1)S(1)}, u32[]{:S(2)}, u32[]{:S(2)}) collective-permute-start(bf16[32,256]{1,0:T(8,128)(2,1)S(1)} %get-tuple-element.37.own_virt), channel_id=1, source_target_pairs={{0,4},{1,5},{2,6},{3,7},{4,0},{5,1},{6,2},{7,3},{8,13},{9,12},{10,... | collective-permute-start | bytes 49160 | tf_op jit(solution)/shard_map/ppermute | solution.py:238
  7.9 0.7 %collective-permute-start.3 = (bf16[32,256]{1,0:T(8,128)(2,1)S(1)}, bf16[32,256]{1,0:T(8,128)(2,1)S(1)}, u32[]{:S(2)}, u32[]{:S(2)}) collective-permute-start(bf16[32,256]{1,0:T(8,128)(2,1)S(1)} %get-tuple-element.37.own_virt), channel_id=1, source_target_pairs={{8,9},{9,8},{10,11},{11,10},{12,13},{13,12},{14,15},{15,14},{16,18... | collective-permute-start | bytes 49160 | tf_op jit(solution)/shard_map/ppermute | solution.py:238
  8.6 1.5 %collective-permute-done.1.refs_5_ = bf16[64,1280]{1,0:T(8,128)(2,1)S(1)} collective-permute-done((bf16[64,1280]{1,0:T(8,128)(2,1)S(1)}, bf16[64,1280]{1,0:T(8,128)(2,1)S(1)}, u32[]{:S(2)}, u32[]{:S(2)}) %collective-permute-start.1) | collective-permute-done | bytes 163872 | tf_op jit(solution)/shard_map/ppermute | solution.py:234
  10.0 3.0 %collective-permute-done.2.refs_6_ = bf16[64,1280]{1,0:T(8,128)(2,1)S(1)} collective-permute-done((bf16[64,1280]{1,0:T(8,128)(2,1)S(1)}, bf16[64,1280]{1,0:T(8,128)(2,1)S(1)}, u32[]{:S(2)}, u32[]{:S(2)}) %collective-permute-start.2) | collective-permute-done | bytes 163872 | tf_op jit(solution)/shard_map/ppermute | solution.py:234
  13.0 0.3 shard_map.56
  13.4 3.2 %collective-permute-start.7 = (bf16[64,2304]{1,0:T(8,128)(2,1)S(1)}, bf16[64,2304]{1,0:T(8,128)(2,1)S(1)}, u32[]{:S(2)}, u32[]{:S(2)}) collective-permute-start(bf16[64,2304]{1,0:T(8,128)(2,1)S(1)} %get-tuple-element.40), channel_id=1, source_target_pairs={{0,16},{1,17},{2,18},{3,19},{4,20},{5,21},{6,22},{7,23},{8,24},{9,... | collective-permute-start | bytes 884744 | tf_op jit(solution)/shard_map/ppermute | solution.py:234
  16.6 3.0 %collective-permute-start.5 = (bf16[32,1024]{1,0:T(8,128)(2,1)S(1)}, bf16[32,1024]{1,0:T(8,128)(2,1)S(1)}, u32[]{:S(2)}, u32[]{:S(2)}) collective-permute-start(bf16[32,1024]{1,0:T(8,128)(2,1)S(1)} %get-tuple-element.38), channel_id=1, source_target_pairs={{0,7},{1,6},{2,5},{3,4},{4,3},{5,2},{6,1},{7,0},{8,15},{9,14},{10,... | collective-permute-start | bytes 196616 | tf_op jit(solution)/shard_map/ppermute | solution.py:234
  19.6 1.8 %collective-permute-start.6 = (bf16[32,1024]{1,0:T(8,128)(2,1)S(1)}, bf16[32,1024]{1,0:T(8,128)(2,1)S(1)}, u32[]{:S(2)}, u32[]{:S(2)}) collective-permute-start(bf16[32,1024]{1,0:T(8,128)(2,1)S(1)} %get-tuple-element.39), channel_id=1, source_target_pairs={{0,6},{1,7},{2,4},{3,5},{4,2},{5,3},{6,0},{7,1},{8,14},{9,15},{10,... | collective-permute-start | bytes 196616 | tf_op jit(solution)/shard_map/ppermute | solution.py:234
  21.4 2.7 %collective-permute-done.5.refs_0_ = bf16[32,1024]{1,0:T(8,128)(2,1)S(1)} collective-permute-done((bf16[32,1024]{1,0:T(8,128)(2,1)S(1)}, bf16[32,1024]{1,0:T(8,128)(2,1)S(1)}, u32[]{:S(2)}, u32[]{:S(2)}) %collective-permute-start.5) | collective-permute-done | bytes 65568 | tf_op jit(solution)/shard_map/ppermute | solution.py:234
  24.1 1.5 %collective-permute-done.6.refs_1_ = bf16[32,1024]{1,0:T(8,128)(2,1)S(1)} collective-permute-done((bf16[32,1024]{1,0:T(8,128)(2,1)S(1)}, bf16[32,1024]{1,0:T(8,128)(2,1)S(1)}, u32[]{:S(2)}, u32[]{:S(2)}) %collective-permute-start.6) | collective-permute-done | bytes 65568 | tf_op jit(solution)/shard_map/ppermute | solution.py:234
  25.6 0.5 %collective-permute-start.8 = (bf16[64,2304]{1,0:T(8,128)(2,1)S(1)}, bf16[64,2304]{1,0:T(8,128)(2,1)S(1)}, u32[]{:S(2)}, u32[]{:S(2)}) collective-permute-start(bf16[64,2304]{1,0:T(8,128)(2,1)S(1)} %collective-permute-done.7.refs_7_), channel_id=1, source_target_pairs={{0,8},{1,9},{2,10},{3,11},{4,12},{5,13},{6,14},{7,15},{8,0},{9,1},... | collective-permute-start | bytes 884744 | tf_op jit(solution)/shard_map/ppermute | solution.py:234
  26.1 1.1 %collective-permute-start.10 = (bf16[32,1024]{1,0:T(8,128)(2,1)S(1)}, bf16[32,1024]{1,0:T(8,128)(2,1)S(1)}, u32[]{:S(2)}, u32[]{:S(2)}) collective-permute-start(bf16[32,1024]{1,0:T(8,128)(2,1)S(1)} %get-tuple-element.51), channel_id=1, source_target_pairs={{0,5},{1,4},{2,7},{3,6},{4,1},{5,0},{6,3},{7,2},{8,13},{9,12},{10,... | collective-permute-start | bytes 196616 | tf_op jit(solution)/shard_map/ppermute | solution.py:234
  27.2 1.8 %collective-permute-start.11 = (bf16[32,1024]{1,0:T(8,128)(2,1)S(1)}, bf16[32,1024]{1,0:T(8,128)(2,1)S(1)}, u32[]{:S(2)}, u32[]{:S(2)}) collective-permute-start(bf16[32,1024]{1,0:T(8,128)(2,1)S(1)} %get-tuple-element.52), channel_id=1, source_target_pairs={{0,4},{1,5},{2,6},{3,7},{4,0},{5,1},{6,2},{7,3},{8,12},{9,13},{10,... | collective-permute-start | bytes 196616 | tf_op jit(solution)/shard_map/ppermute | solution.py:234
  29.0 0.6 %collective-permute-start.12 = (bf16[32,1024]{1,0:T(8,128)(2,1)S(1)}, bf16[32,1024]{1,0:T(8,128)(2,1)S(1)}, u32[]{:S(2)}, u32[]{:S(2)}) collective-permute-start(bf16[32,1024]{1,0:T(8,128)(2,1)S(1)} %get-tuple-element.53), channel_id=1, source_target_pairs={{0,3},{1,2},{2,1},{3,0},{4,7},{5,6},{6,5},{7,4},{8,11},{9,10},{10,... | collective-permute-start | bytes 196616 | tf_op jit(solution)/shard_map/ppermute | solution.py:234
  29.7 2.3 %collective-permute-start.13 = (bf16[32,1024]{1,0:T(8,128)(2,1)S(1)}, bf16[32,1024]{1,0:T(8,128)(2,1)S(1)}, u32[]{:S(2)}, u32[]{:S(2)}) collective-permute-start(bf16[32,1024]{1,0:T(8,128)(2,1)S(1)} %get-tuple-element.54), channel_id=1, source_target_pairs={{0,2},{1,3},{2,0},{3,1},{4,6},{5,7},{6,4},{7,5},{8,10},{9,11},{10,... | collective-permute-start | bytes 196616 | tf_op jit(solution)/shard_map/ppermute | solution.py:234
  32.0 0.5 %collective-permute-start.14 = (bf16[32,1024]{1,0:T(8,128)(2,1)S(1)}, bf16[32,1024]{1,0:T(8,128)(2,1)S(1)}, u32[]{:S(2)}, u32[]{:S(2)}) collective-permute-start(bf16[32,1024]{1,0:T(8,128)(2,1)S(1)} %get-tuple-element.55), channel_id=1, source_target_pairs={{0,1},{1,0},{2,3},{3,2},{4,5},{5,4},{6,7},{7,6},{8,9},{9,8},{10,11... | collective-permute-start | bytes 196616 | tf_op jit(solution)/shard_map/ppermute | solution.py:234
  32.5 1.6 %shard_map.57.g_ref = bf16[32,256,128]{2,1,0:T(8,128)(2,1)S(1)} custom-call(bf16[64,1280]{1,0:T(8,128)(2,1)S(1)} %get-tuple-element.31.refs_0_, bf16[64,1280]{1,0:T(8,128)(2,1)S(1)} %get-tuple-element.32.refs_1_, bf16[64,1280]{1,0:T(8,128)(2,1)S(1)} %get-tuple-element.33.refs_2_, bf16[64,1280]{1,0:T(8,128)(2,1)S(1)} %get-tuple-element.34.refs_3_, ...), custom_call_target="tpu_custom_call" | custom-call | tf_op jit(solution)/shard_map/pallas_call | solution.py:294
  34.2 0.3 collective-permute-done.11.refs_3_
  34.5 1.8 %collective-permute-done.12.refs_4_ = bf16[32,1024]{1,0:T(8,128)(2,1)S(1)} collective-permute-done((bf16[32,1024]{1,0:T(8,128)(2,1)S(1)}, bf16[32,1024]{1,0:T(8,128)(2,1)S(1)}, u32[]{:S(2)}, u32[]{:S(2)}) %collective-permute-start.12) | collective-permute-done | bytes 65568 | tf_op jit(solution)/shard_map/ppermute | solution.py:234
  36.3 0.3 collective-permute-done.13.refs_5_
  36.6 0.7 %shard_map.58 = f32[32,128]{1,0:T(8,128)S(1)} custom-call(bf16[32,256,128]{2,1,0:T(8,128)(2,1)S(1)} %shard_map.57.g_ref, bf16[32,1024]{1,0:T(8,128)(2,1)S(1)} %collective-permute-done.5.refs_0_, bf16[32,1024]{1,0:T(8,128)(2,1)S(1)} %collective-permute-done.6.refs_1_, bf16[32,1024]{1,0:T(8,128)(2,1)S(1)} %collective-permute-done.10.refs_2_, ...), custom_call_target="tpu_custom_call" | custom-call | tf_op jit(solution)/shard_map/pallas_call | solution.py:303
  37.3 2.2 %collective-permute-start.16 = (f32[32,128]{1,0:T(8,128)S(1)}, f32[32,128]{1,0:T(8,128)S(1)}, u32[]{:S(2)}, u32[]{:S(2)}) collective-permute-start(f32[32,128]{1,0:T(8,128)S(1)} %shard_map.58), channel_id=1, source_target_pairs={{0,2},{1,3},{2,0},{3,1},{4,6},{5,7},{6,4},{7,5},{8,10},{9,11},{10,... | collective-permute-start | bytes 49160 | tf_op jit(solution)/shard_map/ppermute | solution.py:234
  39.6 1.3 %collective-permute-start.15 = (f32[32,128]{1,0:T(8,128)S(1)}, f32[32,128]{1,0:T(8,128)S(1)}, u32[]{:S(2)}, u32[]{:S(2)}) collective-permute-start(f32[32,128]{1,0:T(8,128)S(1)} %shard_map.58), channel_id=1, source_target_pairs={{0,1},{1,0},{2,3},{3,2},{4,5},{5,4},{6,7},{7,6},{8,9},{9,8},{10,11... | collective-permute-start | bytes 49160 | tf_op jit(solution)/shard_map/ppermute | solution.py:234
  40.8 1.1 %collective-permute-done.17 = f32[32,128]{1,0:T(8,128)S(1)} collective-permute-done((f32[32,128]{1,0:T(8,128)S(1)}, f32[32,128]{1,0:T(8,128)S(1)}, u32[]{:S(2)}, u32[]{:S(2)}) %collective-permute-start.17) | collective-permute-done | bytes 16416 | tf_op jit(solution)/shard_map/ppermute | solution.py:234
  42.0 1.3 %collective-permute-done.15 = f32[32,128]{1,0:T(8,128)S(1)} collective-permute-done((f32[32,128]{1,0:T(8,128)S(1)}, f32[32,128]{1,0:T(8,128)S(1)}, u32[]{:S(2)}, u32[]{:S(2)}) %collective-permute-start.15) | collective-permute-done | bytes 16416 | tf_op jit(solution)/shard_map/ppermute | solution.py:234
  43.3 1.0 %collective-permute-start.18 = (f32[32,128]{1,0:T(8,128)S(1)}, f32[32,128]{1,0:T(8,128)S(1)}, u32[]{:S(2)}, u32[]{:S(2)}) collective-permute-start(f32[32,128]{1,0:T(8,128)S(1)} %add_add_fusion), channel_id=1, source_target_pairs={{0,4},{1,5},{2,6},{3,7},{4,0},{5,1},{6,2},{7,3},{8,12},{9,13},{10,... | collective-permute-start | bytes 49160 | tf_op jit(solution)/shard_map/ppermute | solution.py:234
  44.3 3.6 %collective-permute-done.18 = f32[32,128]{1,0:T(8,128)S(1)} collective-permute-done((f32[32,128]{1,0:T(8,128)S(1)}, f32[32,128]{1,0:T(8,128)S(1)}, u32[]{:S(2)}, u32[]{:S(2)}) %collective-permute-start.18) | collective-permute-done | bytes 16416 | tf_op jit(solution)/shard_map/ppermute | solution.py:234
  47.9 0.6 %add.15 = f32[32,128]{1,0:T(8,128)} add(f32[32,128]{1,0:T(8,128)S(1)} %add_add_fusion, f32[32,128]{1,0:T(8,128)S(1)} %collective-permute-done.18) | non-fusion elementwise | flops 4096 | bytes 49152 | tf_op jit(solution)/shard_map/add | solution.py:313
  (12 shorter events, 0.1 us)
Async XLA Ops:
  1.9 3.2 %collective-permute-start = (bf16[64,1280]{1,0:T(8,128)(2,1)S(1)}, bf16[64,1280]{1,0:T(8,128)(2,1)S(1)}, u32[]{:S(2)}, u32[]{:S(2)}) collective-permute-start(bf16[64,1280]{1,0:T(8,128)(2,1)S(1)} %get-tuple-element.32.refs_1_), channel_id=1, source_target_pairs={{0,8},{1,9},{2,10},{3,11},{4,12},{5,13},{6,14},{7,15},{8,0},{9,1},... | collective-permute-start | bytes 491528 | tf_op jit(solution)/shard_map/ppermute | solution.py:234
  2.4 7.6 %collective-permute-start.1 = (bf16[64,1280]{1,0:T(8,128)(2,1)S(1)}, bf16[64,1280]{1,0:T(8,128)(2,1)S(1)}, u32[]{:S(2)}, u32[]{:S(2)}) collective-permute-start(bf16[64,1280]{1,0:T(8,128)(2,1)S(1)} %get-tuple-element.33.refs_2_), channel_id=1, source_target_pairs={{0,16},{1,17},{2,18},{3,19},{4,20},{5,21},{6,22},{7,23},{8,24},{9,... | collective-permute-start | bytes 491528 | tf_op jit(solution)/shard_map/ppermute | solution.py:234
  5.0 8.0 %collective-permute-start.2 = (bf16[64,1280]{1,0:T(8,128)(2,1)S(1)}, bf16[64,1280]{1,0:T(8,128)(2,1)S(1)}, u32[]{:S(2)}, u32[]{:S(2)}) collective-permute-start(bf16[64,1280]{1,0:T(8,128)(2,1)S(1)} %get-tuple-element.34.refs_3_), channel_id=1, source_target_pairs={{0,24},{1,25},{2,26},{3,27},{4,28},{5,29},{6,30},{7,31},{8,16},{9,... | collective-permute-start | bytes 491528 | tf_op jit(solution)/shard_map/ppermute | solution.py:234
  5.1 8.0 %collective-permute-start.4 = (bf16[32,256]{1,0:T(8,128)(2,1)S(1)}, bf16[32,256]{1,0:T(8,128)(2,1)S(1)}, u32[]{:S(2)}, u32[]{:S(2)}) collective-permute-start(bf16[32,256]{1,0:T(8,128)(2,1)S(1)} %get-tuple-element.37.own_virt), channel_id=1, source_target_pairs={{0,4},{1,5},{2,6},{3,7},{4,0},{5,1},{6,2},{7,3},{8,13},{9,12},{10,... | collective-permute-start | bytes 49160 | tf_op jit(solution)/shard_map/ppermute | solution.py:238
  7.9 5.1 %collective-permute-start.3 = (bf16[32,256]{1,0:T(8,128)(2,1)S(1)}, bf16[32,256]{1,0:T(8,128)(2,1)S(1)}, u32[]{:S(2)}, u32[]{:S(2)}) collective-permute-start(bf16[32,256]{1,0:T(8,128)(2,1)S(1)} %get-tuple-element.37.own_virt), channel_id=1, source_target_pairs={{8,9},{9,8},{10,11},{11,10},{12,13},{13,12},{14,15},{15,14},{16,18... | collective-permute-start | bytes 49160 | tf_op jit(solution)/shard_map/ppermute | solution.py:238
  13.4 12.3 %collective-permute-start.7 = (bf16[64,2304]{1,0:T(8,128)(2,1)S(1)}, bf16[64,2304]{1,0:T(8,128)(2,1)S(1)}, u32[]{:S(2)}, u32[]{:S(2)}) collective-permute-start(bf16[64,2304]{1,0:T(8,128)(2,1)S(1)} %get-tuple-element.40), channel_id=1, source_target_pairs={{0,16},{1,17},{2,18},{3,19},{4,20},{5,21},{6,22},{7,23},{8,24},{9,... | collective-permute-start | bytes 884744 | tf_op jit(solution)/shard_map/ppermute | solution.py:234
  16.6 7.5 %collective-permute-start.5 = (bf16[32,1024]{1,0:T(8,128)(2,1)S(1)}, bf16[32,1024]{1,0:T(8,128)(2,1)S(1)}, u32[]{:S(2)}, u32[]{:S(2)}) collective-permute-start(bf16[32,1024]{1,0:T(8,128)(2,1)S(1)} %get-tuple-element.38), channel_id=1, source_target_pairs={{0,7},{1,6},{2,5},{3,4},{4,3},{5,2},{6,1},{7,0},{8,15},{9,14},{10,... | collective-permute-start | bytes 196616 | tf_op jit(solution)/shard_map/ppermute | solution.py:234
  19.6 6.1 %collective-permute-start.6 = (bf16[32,1024]{1,0:T(8,128)(2,1)S(1)}, bf16[32,1024]{1,0:T(8,128)(2,1)S(1)}, u32[]{:S(2)}, u32[]{:S(2)}) collective-permute-start(bf16[32,1024]{1,0:T(8,128)(2,1)S(1)} %get-tuple-element.39), channel_id=1, source_target_pairs={{0,6},{1,7},{2,4},{3,5},{4,2},{5,3},{6,0},{7,1},{8,14},{9,15},{10,... | collective-permute-start | bytes 196616 | tf_op jit(solution)/shard_map/ppermute | solution.py:234
  25.6 6.4 %collective-permute-start.9 = (bf16[64,5376]{1,0:T(8,128)(2,1)S(1)}, bf16[64,5376]{1,0:T(8,128)(2,1)S(1)}, u32[]{:S(2)}, u32[]{:S(2)}) collective-permute-start(bf16[64,5376]{1,0:T(8,128)(2,1)S(1)} %get-tuple-element.48.refs_10_), channel_id=1, source_target_pairs={{0,8},{1,9},{2,10},{3,11},{4,12},{5,13},{6,14},{7,15},{8,0},{9,1},... | collective-permute-start | bytes 2064392 | tf_op jit(solution)/shard_map/ppermute | solution.py:234
  25.6 4.0 %collective-permute-start.8 = (bf16[64,2304]{1,0:T(8,128)(2,1)S(1)}, bf16[64,2304]{1,0:T(8,128)(2,1)S(1)}, u32[]{:S(2)}, u32[]{:S(2)}) collective-permute-start(bf16[64,2304]{1,0:T(8,128)(2,1)S(1)} %collective-permute-done.7.refs_7_), channel_id=1, source_target_pairs={{0,8},{1,9},{2,10},{3,11},{4,12},{5,13},{6,14},{7,15},{8,0},{9,1},... | collective-permute-start | bytes 884744 | tf_op jit(solution)/shard_map/ppermute | solution.py:234
  26.1 8.0 %collective-permute-start.10 = (bf16[32,1024]{1,0:T(8,128)(2,1)S(1)}, bf16[32,1024]{1,0:T(8,128)(2,1)S(1)}, u32[]{:S(2)}, u32[]{:S(2)}) collective-permute-start(bf16[32,1024]{1,0:T(8,128)(2,1)S(1)} %get-tuple-element.51), channel_id=1, source_target_pairs={{0,5},{1,4},{2,7},{3,6},{4,1},{5,0},{6,3},{7,2},{8,13},{9,12},{10,... | collective-permute-start | bytes 196616 | tf_op jit(solution)/shard_map/ppermute | solution.py:234
  27.2 7.3 %collective-permute-start.11 = (bf16[32,1024]{1,0:T(8,128)(2,1)S(1)}, bf16[32,1024]{1,0:T(8,128)(2,1)S(1)}, u32[]{:S(2)}, u32[]{:S(2)}) collective-permute-start(bf16[32,1024]{1,0:T(8,128)(2,1)S(1)} %get-tuple-element.52), channel_id=1, source_target_pairs={{0,4},{1,5},{2,6},{3,7},{4,0},{5,1},{6,2},{7,3},{8,12},{9,13},{10,... | collective-permute-start | bytes 196616 | tf_op jit(solution)/shard_map/ppermute | solution.py:234
  29.0 7.2 %collective-permute-start.12 = (bf16[32,1024]{1,0:T(8,128)(2,1)S(1)}, bf16[32,1024]{1,0:T(8,128)(2,1)S(1)}, u32[]{:S(2)}, u32[]{:S(2)}) collective-permute-start(bf16[32,1024]{1,0:T(8,128)(2,1)S(1)} %get-tuple-element.53), channel_id=1, source_target_pairs={{0,3},{1,2},{2,1},{3,0},{4,7},{5,6},{6,5},{7,4},{8,11},{9,10},{10,... | collective-permute-start | bytes 196616 | tf_op jit(solution)/shard_map/ppermute | solution.py:234
  29.7 6.9 %collective-permute-start.13 = (bf16[32,1024]{1,0:T(8,128)(2,1)S(1)}, bf16[32,1024]{1,0:T(8,128)(2,1)S(1)}, u32[]{:S(2)}, u32[]{:S(2)}) collective-permute-start(bf16[32,1024]{1,0:T(8,128)(2,1)S(1)} %get-tuple-element.54), channel_id=1, source_target_pairs={{0,2},{1,3},{2,0},{3,1},{4,6},{5,7},{6,4},{7,5},{8,10},{9,11},{10,... | collective-permute-start | bytes 196616 | tf_op jit(solution)/shard_map/ppermute | solution.py:234
  32.0 4.6 %collective-permute-start.14 = (bf16[32,1024]{1,0:T(8,128)(2,1)S(1)}, bf16[32,1024]{1,0:T(8,128)(2,1)S(1)}, u32[]{:S(2)}, u32[]{:S(2)}) collective-permute-start(bf16[32,1024]{1,0:T(8,128)(2,1)S(1)} %get-tuple-element.55), channel_id=1, source_target_pairs={{0,1},{1,0},{2,3},{3,2},{4,5},{5,4},{6,7},{7,6},{8,9},{9,8},{10,11... | collective-permute-start | bytes 196616 | tf_op jit(solution)/shard_map/ppermute | solution.py:234
  37.3 4.6 %collective-permute-start.17 = (f32[32,128]{1,0:T(8,128)S(1)}, f32[32,128]{1,0:T(8,128)S(1)}, u32[]{:S(2)}, u32[]{:S(2)}) collective-permute-start(f32[32,128]{1,0:T(8,128)S(1)} %shard_map.58), channel_id=1, source_target_pairs={{0,3},{1,2},{2,1},{3,0},{4,7},{5,6},{6,5},{7,4},{8,11},{9,10},{10,... | collective-permute-start | bytes 49160 | tf_op jit(solution)/shard_map/ppermute | solution.py:234
  37.3 4.6 %collective-permute-start.16 = (f32[32,128]{1,0:T(8,128)S(1)}, f32[32,128]{1,0:T(8,128)S(1)}, u32[]{:S(2)}, u32[]{:S(2)}) collective-permute-start(f32[32,128]{1,0:T(8,128)S(1)} %shard_map.58), channel_id=1, source_target_pairs={{0,2},{1,3},{2,0},{3,1},{4,6},{5,7},{6,4},{7,5},{8,10},{9,11},{10,... | collective-permute-start | bytes 49160 | tf_op jit(solution)/shard_map/ppermute | solution.py:234
  39.6 3.7 %collective-permute-start.15 = (f32[32,128]{1,0:T(8,128)S(1)}, f32[32,128]{1,0:T(8,128)S(1)}, u32[]{:S(2)}, u32[]{:S(2)}) collective-permute-start(f32[32,128]{1,0:T(8,128)S(1)} %shard_map.58), channel_id=1, source_target_pairs={{0,1},{1,0},{2,3},{3,2},{4,5},{5,4},{6,7},{7,6},{8,9},{9,8},{10,11... | collective-permute-start | bytes 49160 | tf_op jit(solution)/shard_map/ppermute | solution.py:234
  43.3 4.6 %collective-permute-start.18 = (f32[32,128]{1,0:T(8,128)S(1)}, f32[32,128]{1,0:T(8,128)S(1)}, u32[]{:S(2)}, u32[]{:S(2)}) collective-permute-start(f32[32,128]{1,0:T(8,128)S(1)} %add_add_fusion), channel_id=1, source_target_pairs={{0,4},{1,5},{2,6},{3,7},{4,0},{5,1},{6,2},{7,3},{8,12},{9,13},{10,... | collective-permute-start | bytes 49160 | tf_op jit(solution)/shard_map/ppermute | solution.py:234

commit v5 on v4

--- a/solution.py
+++ b/solution.py
@@ -95,6 +95,10 @@
             outs[m][:, l * naux:(l + 1) * naux] = tiles[m]
 
 
+def add_kernel(*refs):
+    refs[-1][...] = sum(r[...] for r in refs[:-1])
+
+
 def others(n_split, m):
     return [i for i in range(n_split) if i // 2 != m // 2]
 
@@ -122,7 +126,7 @@
 
 
 def first_kernel(n_split, n_tensor, width, own_virt, *refs):
-    own, got, rest = refs[:n_split], refs[n_split:2 * n_split - 1], refs[2 * n_split - 1:]
+    own, got, rest = refs[:n_split], refs[n_split:2 * n_split - 1][::-1], refs[2 * n_split - 1:]
     shares = n_tensor // n_split
     fetched, firsts, raws = rest[:shares], rest[shares:shares + n_tensor], rest[shares + n_tensor:]
     whole = jnp.concatenate([p[...] for p in (own[0], *got)], axis=0)
@@ -257,7 +261,6 @@
     received = [exchange(packed[m], split_bits=m) for m in range(1, n_split)]
 
     own = virt
-    virt, received[0] = lax.optimization_barrier((virt, received[0]))
     shares = n_tensor // n_split
     fetched = [fetch(virt, j) for j in range(shares)]
 
@@ -270,13 +273,13 @@
         in_specs=[vmem] * (2 * n_split + shares),
         out_specs=[vmem] * (n_tensor + len(widths)),
         compiler_params=params,
-    )(own, *packed, *received, *fetched)
+    )(own, *packed, *received[::-1], *fetched)
     firsts, raws = made[:n_tensor], made[n_tensor:]
 
     moved = {}
     moved.update({m: exchange(raws[m // 2 - 1], split_bits=m) for m in range(2, n_split, 2)})
     got = {0: firsts[0]}
-    ahead = [n_tensor - 1, n_tensor - 2]
+    ahead = [k for k in range(n_tensor - 1, 1, -1) if k != n_tensor // 2]
     got.update({k: exchange(firsts[k], tensor_bits=k) for k in ahead})
     later = [k for k in range(n_tensor - 1, 0, -1) if k not in ahead]
     evens = list(range(2, n_split, 2))
@@ -309,8 +312,16 @@
     )(g, *got[::-1])
     for near in stages(n_tensor):
         got = [exchange(total, tensor_bits=k) for k in near]
-        for x in got:
-            total = total + x
+        if near[-1] * 2 < n_tensor:
+            total = pl.pallas_call(
+                add_kernel,
+                out_shape=jax.ShapeDtypeStruct(total.shape, F32),
+                in_specs=[vmem] * (1 + len(got)),
+                out_specs=vmem,
+                compiler_params=params,
+            )(total, *got)
+        else:
+            total = sum(got, total)
     return total
 
 

time: 48.7 us -> 48.2 us (0.990)
  starting transfers between devices: 26 us -> 24.9 us
  waiting for transfers between devices: 17.4 us -> 18 us
    ppermute x2, waiting for transfers between devices: 0.01 us -> 1.16 us  [fetch(): lax.ppermute(x, ('split', 'tensor'), [(a, b) for a, b in pairs if a != b])]
    ppermute x17, starting transfers between devices: 22.5 us -> 21.4 us  [exchange(): lax.ppermute(x, ('split', 'tensor'), [(d, d ^ bits) for d in range(count)])]
    ppermute x17, waiting for transfers between devices: 17.4 us -> 16.8 us  [exchange(): lax.ppermute(x, ('split', 'tensor'), [(d, d ^ bits) for d in range(count)])]
  transfers between devices with their start and end apart: 19 -> 19, of which waited for: 10 -> 13; matrix products, arithmetic and copies ran while one was open for 0% -> 0% of each run, Pallas kernels for 3% -> 3%
where the time goes in v5:
time: 48.2 us; the launch traced here: 48.1 us
  starting transfers between devices  24.9 us (52%)
  waiting for transfers between devices  18 us (37%)
  Pallas kernels  4.55 us (9%)
  other arithmetic  0.61 us (1%)
    ppermute x17, starting transfers between devices, exchange(): lax.ppermute(x, ('split', 'tensor'), [(d, d ^ bits) for d in range(count)])  21.4 us
    ppermute x17, waiting for transfers between devices, exchange(): lax.ppermute(x, ('split', 'tensor'), [(d, d ^ bits) for d in range(count)])  16.8 us
    ppermute x2, starting transfers between devices, fetch(): lax.ppermute(x, ('split', 'tensor'), [(a, b) for a, b in pairs if a != b])  3.47 us
    pallas_call x1, Pallas kernels, local(): pl.pallas_call(functools.partial(pack_kernel, n_split), out_shape=[jax.Sh...  1.9 us
    pallas_call x1, Pallas kernels, local(): pl.pallas_call(functools.partial(g_kernel, n_split, n_tensor, packed_widt...  1.64 us
    ppermute x2, waiting for transfers between devices, fetch(): lax.ppermute(x, ('split', 'tensor'), [(a, b) for a, b in pairs if a != b])  1.16 us
  transfers between devices with their start and end apart: 19, of which 13 were waited for; matrix products, arithmetic and copies ran while one was open for 0% of the time, Pallas kernels for 3%

profile of v5, /device:TPU:0, one launch (start us, length us, event | category | flops | bytes accessed | tf_op | source)
XLA Modules:
  0.0 48.1 jit_solution(144236010461596806)
XLA Ops:
  0.0 1.9 %shard_map.55 = (bf16[32,256]{1,0:T(8,128)(2,1)S(1)}, bf16[64,1280]{1,0:T(8,128)(2,1)S(1)}, bf16[64,1280]{1,0:T(8,128)(2,1)S(1)}, bf16[64,1280]{1,0:T(8,128)(2,1)S(1)}, bf16[64,1280]{1,0:T(8,128)(2,1)S(1)}) custom-call(s32[8,8]{1,0:T(8,128)} %occ_mask_hbm.1, s32[8,8]{1,0:T(8,128)} %virt_mask_hbm.1, bf16[64,32,128]{2,1,0:T(8,128)(2,1)} %b_hbm.1, ...), custom_call_target="tpu_custom_call" | custom-call | tf_op jit(solution)/shard_map/pallas_call | solution.py:245
  1.9 0.5 %collective-permute-start = (bf16[64,1280]{1,0:T(8,128)(2,1)S(1)}, bf16[64,1280]{1,0:T(8,128)(2,1)S(1)}, u32[]{:S(2)}, u32[]{:S(2)}) collective-permute-start(bf16[64,1280]{1,0:T(8,128)(2,1)S(1)} %get-tuple-element.30.refs_1_), channel_id=1, source_target_pairs={{0,8},{1,9},{2,10},{3,11},{4,12},{5,13},{6,14},{7,15},{8,0},{9,1},... | collective-permute-start | bytes 491528 | tf_op jit(solution)/shard_map/ppermute | solution.py:238
  2.4 2.6 %collective-permute-start.1 = (bf16[64,1280]{1,0:T(8,128)(2,1)S(1)}, bf16[64,1280]{1,0:T(8,128)(2,1)S(1)}, u32[]{:S(2)}, u32[]{:S(2)}) collective-permute-start(bf16[64,1280]{1,0:T(8,128)(2,1)S(1)} %get-tuple-element.31.refs_2_), channel_id=1, source_target_pairs={{0,16},{1,17},{2,18},{3,19},{4,20},{5,21},{6,22},{7,23},{8,24},{9,... | collective-permute-start | bytes 491528 | tf_op jit(solution)/shard_map/ppermute | solution.py:238
  5.1 2.8 %collective-permute-start.4 = (bf16[32,256]{1,0:T(8,128)(2,1)S(1)}, bf16[32,256]{1,0:T(8,128)(2,1)S(1)}, u32[]{:S(2)}, u32[]{:S(2)}) collective-permute-start(bf16[32,256]{1,0:T(8,128)(2,1)S(1)} %get-tuple-element.33.own_virt), channel_id=1, source_target_pairs={{0,4},{1,5},{2,6},{3,7},{4,0},{5,1},{6,2},{7,3},{8,13},{9,12},{10,... | collective-permute-start | bytes 49160 | tf_op jit(solution)/shard_map/ppermute | solution.py:242
  7.9 0.7 %collective-permute-start.3 = (bf16[32,256]{1,0:T(8,128)(2,1)S(1)}, bf16[32,256]{1,0:T(8,128)(2,1)S(1)}, u32[]{:S(2)}, u32[]{:S(2)}) collective-permute-start(bf16[32,256]{1,0:T(8,128)(2,1)S(1)} %get-tuple-element.33.own_virt), channel_id=1, source_target_pairs={{8,9},{9,8},{10,11},{11,10},{12,13},{13,12},{14,15},{15,14},{16,18... | collective-permute-start | bytes 49160 | tf_op jit(solution)/shard_map/ppermute | solution.py:242
  8.5 1.2 %collective-permute-done.4.refs_8_ = bf16[32,256]{1,0:T(8,128)(2,1)S(1)} collective-permute-done((bf16[32,256]{1,0:T(8,128)(2,1)S(1)}, bf16[32,256]{1,0:T(8,128)(2,1)S(1)}, u32[]{:S(2)}, u32[]{:S(2)}) %collective-permute-start.4) | collective-permute-done | bytes 16416 | tf_op jit(solution)/shard_map/ppermute | solution.py:242
  9.7 0.3 collective-permute-done.1.refs_5_
  10.0 3.0 %collective-permute-done.2.refs_4_.refs_6_ = bf16[64,1280]{1,0:T(8,128)(2,1)S(1)} collective-permute-done((bf16[64,1280]{1,0:T(8,128)(2,1)S(1)}, bf16[64,1280]{1,0:T(8,128)(2,1)S(1)}, u32[]{:S(2)}, u32[]{:S(2)}) %collective-permute-start.2) | collective-permute-done | bytes 163872 | tf_op jit(solution)/shard_map/ppermute | solution.py:238
  13.0 0.3 shard_map.56
  13.4 3.2 %collective-permute-start.10 = (bf16[64,2304]{1,0:T(8,128)(2,1)S(1)}, bf16[64,2304]{1,0:T(8,128)(2,1)S(1)}, u32[]{:S(2)}, u32[]{:S(2)}) collective-permute-start(bf16[64,2304]{1,0:T(8,128)(2,1)S(1)} %get-tuple-element.39), channel_id=1, source_target_pairs={{0,16},{1,17},{2,18},{3,19},{4,20},{5,21},{6,22},{7,23},{8,24},{9,... | collective-permute-start | bytes 884744 | tf_op jit(solution)/shard_map/ppermute | solution.py:238
  16.6 3.0 %collective-permute-start.5 = (bf16[32,1024]{1,0:T(8,128)(2,1)S(1)}, bf16[32,1024]{1,0:T(8,128)(2,1)S(1)}, u32[]{:S(2)}, u32[]{:S(2)}) collective-permute-start(bf16[32,1024]{1,0:T(8,128)(2,1)S(1)} %get-tuple-element.34), channel_id=1, source_target_pairs={{0,7},{1,6},{2,5},{3,4},{4,3},{5,2},{6,1},{7,0},{8,15},{9,14},{10,... | collective-permute-start | bytes 196616 | tf_op jit(solution)/shard_map/ppermute | solution.py:238
  19.6 1.8 %collective-permute-start.6 = (bf16[32,1024]{1,0:T(8,128)(2,1)S(1)}, bf16[32,1024]{1,0:T(8,128)(2,1)S(1)}, u32[]{:S(2)}, u32[]{:S(2)}) collective-permute-start(bf16[32,1024]{1,0:T(8,128)(2,1)S(1)} %get-tuple-element.35), channel_id=1, source_target_pairs={{0,6},{1,7},{2,4},{3,5},{4,2},{5,3},{6,0},{7,1},{8,14},{9,15},{10,... | collective-permute-start | bytes 196616 | tf_op jit(solution)/shard_map/ppermute | solution.py:238
  21.4 3.5 %collective-permute-start.8 = (bf16[32,1024]{1,0:T(8,128)(2,1)S(1)}, bf16[32,1024]{1,0:T(8,128)(2,1)S(1)}, u32[]{:S(2)}, u32[]{:S(2)}) collective-permute-start(bf16[32,1024]{1,0:T(8,128)(2,1)S(1)} %get-tuple-element.37), channel_id=1, source_target_pairs={{0,3},{1,2},{2,1},{3,0},{4,7},{5,6},{6,5},{7,4},{8,11},{9,10},{10,... | collective-permute-start | bytes 196616 | tf_op jit(solution)/shard_map/ppermute | solution.py:238
  24.8 1.0 %collective-permute-done.6.refs_1_ = bf16[32,1024]{1,0:T(8,128)(2,1)S(1)} collective-permute-done((bf16[32,1024]{1,0:T(8,128)(2,1)S(1)}, bf16[32,1024]{1,0:T(8,128)(2,1)S(1)}, u32[]{:S(2)}, u32[]{:S(2)}) %collective-permute-start.6) | collective-permute-done | bytes 65568 | tf_op jit(solution)/shard_map/ppermute | solution.py:238
  25.9 2.6 %collective-permute-done.7.refs_2_ = bf16[32,1024]{1,0:T(8,128)(2,1)S(1)} collective-permute-done((bf16[32,1024]{1,0:T(8,128)(2,1)S(1)}, bf16[32,1024]{1,0:T(8,128)(2,1)S(1)}, u32[]{:S(2)}, u32[]{:S(2)}) %collective-permute-start.7) | collective-permute-done | bytes 65568 | tf_op jit(solution)/shard_map/ppermute | solution.py:238
  28.5 0.6 %collective-permute-done.8.refs_4_ = bf16[32,1024]{1,0:T(8,128)(2,1)S(1)} collective-permute-done((bf16[32,1024]{1,0:T(8,128)(2,1)S(1)}, bf16[32,1024]{1,0:T(8,128)(2,1)S(1)}, u32[]{:S(2)}, u32[]{:S(2)}) %collective-permute-start.8) | collective-permute-done | bytes 65568 | tf_op jit(solution)/shard_map/ppermute | solution.py:238
  29.1 0.3 collective-permute-done.9.refs_5_
  29.3 0.5 %collective-permute-start.11 = (bf16[64,2304]{1,0:T(8,128)(2,1)S(1)}, bf16[64,2304]{1,0:T(8,128)(2,1)S(1)}, u32[]{:S(2)}, u32[]{:S(2)}) collective-permute-start(bf16[64,2304]{1,0:T(8,128)(2,1)S(1)} %collective-permute-done.10.refs_7_), channel_id=1, source_target_pairs={{0,8},{1,9},{2,10},{3,11},{4,12},{5,13},{6,14},{7,15},{8,0},{9,1},... | collective-permute-start | bytes 884744 | tf_op jit(solution)/shard_map/ppermute | solution.py:238
  29.9 0.8 %collective-permute-start.13 = (bf16[32,1024]{1,0:T(8,128)(2,1)S(1)}, bf16[32,1024]{1,0:T(8,128)(2,1)S(1)}, u32[]{:S(2)}, u32[]{:S(2)}) collective-permute-start(bf16[32,1024]{1,0:T(8,128)(2,1)S(1)} %get-tuple-element.48), channel_id=1, source_target_pairs={{0,4},{1,5},{2,6},{3,7},{4,0},{5,1},{6,2},{7,3},{8,12},{9,13},{10,... | collective-permute-start | bytes 196616 | tf_op jit(solution)/shard_map/ppermute | solution.py:238
  30.7 0.8 %collective-permute-start.14 = (bf16[32,1024]{1,0:T(8,128)(2,1)S(1)}, bf16[32,1024]{1,0:T(8,128)(2,1)S(1)}, u32[]{:S(2)}, u32[]{:S(2)}) collective-permute-start(bf16[32,1024]{1,0:T(8,128)(2,1)S(1)} %get-tuple-element.51), channel_id=1, source_target_pairs={{0,1},{1,0},{2,3},{3,2},{4,5},{5,4},{6,7},{7,6},{8,9},{9,8},{10,11... | collective-permute-start | bytes 196616 | tf_op jit(solution)/shard_map/ppermute | solution.py:238
  31.5 0.5 collective-permute-done.11.refs_8_
  31.9 1.6 %shard_map.57.g_ref = bf16[32,256,128]{2,1,0:T(8,128)(2,1)S(1)} custom-call(bf16[64,1280]{1,0:T(8,128)(2,1)S(1)} %get-tuple-element.29.refs_0_, bf16[64,1280]{1,0:T(8,128)(2,1)S(1)} %get-tuple-element.30.refs_1_, bf16[64,1280]{1,0:T(8,128)(2,1)S(1)} %get-tuple-element.31.refs_2_, bf16[64,1280]{1,0:T(8,128)(2,1)S(1)} %get-tuple-element.32.refs_3_, ...), custom_call_target="tpu_custom_call" | custom-call | tf_op jit(solution)/shard_map/pallas_call | solution.py:297
  33.6 2.5 %collective-permute-done.13.refs_3_ = bf16[32,1024]{1,0:T(8,128)(2,1)S(1)} collective-permute-done((bf16[32,1024]{1,0:T(8,128)(2,1)S(1)}, bf16[32,1024]{1,0:T(8,128)(2,1)S(1)}, u32[]{:S(2)}, u32[]{:S(2)}) %collective-permute-start.13) | collective-permute-done | bytes 65568 | tf_op jit(solution)/shard_map/ppermute | solution.py:238
  36.1 0.7 %shard_map.58.refs_0_ = f32[32,128]{1,0:T(8,128)S(1)} custom-call(bf16[32,256,128]{2,1,0:T(8,128)(2,1)S(1)} %shard_map.57.g_ref, bf16[32,1024]{1,0:T(8,128)(2,1)S(1)} %collective-permute-done.5.refs_0_, bf16[32,1024]{1,0:T(8,128)(2,1)S(1)} %collective-permute-done.6.refs_1_, bf16[32,1024]{1,0:T(8,128)(2,1)S(1)} %collective-permute-done.7.refs_2_, ...), custom_call_target="tpu_custom_call" | custom-call | tf_op jit(solution)/shard_map/pallas_call | solution.py:306
  36.7 1.0 %collective-permute-start.17 = (f32[32,128]{1,0:T(8,128)S(1)}, f32[32,128]{1,0:T(8,128)S(1)}, u32[]{:S(2)}, u32[]{:S(2)}) collective-permute-start(f32[32,128]{1,0:T(8,128)S(1)} %shard_map.58.refs_0_), channel_id=1, source_target_pairs={{0,3},{1,2},{2,1},{3,0},{4,7},{5,6},{6,5},{7,4},{8,11},{9,10},{10,... | collective-permute-start | bytes 49160 | tf_op jit(solution)/shard_map/ppermute | solution.py:238
  37.7 1.3 %collective-permute-start.16 = (f32[32,128]{1,0:T(8,128)S(1)}, f32[32,128]{1,0:T(8,128)S(1)}, u32[]{:S(2)}, u32[]{:S(2)}) collective-permute-start(f32[32,128]{1,0:T(8,128)S(1)} %shard_map.58.refs_0_), channel_id=1, source_target_pairs={{0,2},{1,3},{2,0},{3,1},{4,6},{5,7},{6,4},{7,5},{8,10},{9,11},{10,... | collective-permute-start | bytes 49160 | tf_op jit(solution)/shard_map/ppermute | solution.py:238
  39.0 1.2 %collective-permute-start.15 = (f32[32,128]{1,0:T(8,128)S(1)}, f32[32,128]{1,0:T(8,128)S(1)}, u32[]{:S(2)}, u32[]{:S(2)}) collective-permute-start(f32[32,128]{1,0:T(8,128)S(1)} %shard_map.58.refs_0_), channel_id=1, source_target_pairs={{0,1},{1,0},{2,3},{3,2},{4,5},{5,4},{6,7},{7,6},{8,9},{9,8},{10,11... | collective-permute-start | bytes 49160 | tf_op jit(solution)/shard_map/ppermute | solution.py:238
  40.2 1.1 %collective-permute-done.17.refs_3_ = f32[32,128]{1,0:T(8,128)S(1)} collective-permute-done((f32[32,128]{1,0:T(8,128)S(1)}, f32[32,128]{1,0:T(8,128)S(1)}, u32[]{:S(2)}, u32[]{:S(2)}) %collective-permute-start.17) | collective-permute-done | bytes 16416 | tf_op jit(solution)/shard_map/ppermute | solution.py:238
  41.5 1.3 %collective-permute-done.15.refs_1_ = f32[32,128]{1,0:T(8,128)S(1)} collective-permute-done((f32[32,128]{1,0:T(8,128)S(1)}, f32[32,128]{1,0:T(8,128)S(1)}, u32[]{:S(2)}, u32[]{:S(2)}) %collective-permute-start.15) | collective-permute-done | bytes 16416 | tf_op jit(solution)/shard_map/ppermute | solution.py:238
  42.8 1.1 %collective-permute-start.18 = (f32[32,128]{1,0:T(8,128)S(1)}, f32[32,128]{1,0:T(8,128)S(1)}, u32[]{:S(2)}, u32[]{:S(2)}) collective-permute-start(f32[32,128]{1,0:T(8,128)S(1)} %shard_map.59), channel_id=1, source_target_pairs={{0,4},{1,5},{2,6},{3,7},{4,0},{5,1},{6,2},{7,3},{8,12},{9,13},{10,... | collective-permute-start | bytes 49160 | tf_op jit(solution)/shard_map/ppermute | solution.py:238
  43.9 3.5 %collective-permute-done.18 = f32[32,128]{1,0:T(8,128)S(1)} collective-permute-done((f32[32,128]{1,0:T(8,128)S(1)}, f32[32,128]{1,0:T(8,128)S(1)}, u32[]{:S(2)}, u32[]{:S(2)}) %collective-permute-start.18) | collective-permute-done | bytes 16416 | tf_op jit(solution)/shard_map/ppermute | solution.py:238
  47.4 0.6 %add.3 = f32[32,128]{1,0:T(8,128)} add(f32[32,128]{1,0:T(8,128)S(1)} %shard_map.59, f32[32,128]{1,0:T(8,128)S(1)} %collective-permute-done.18) | non-fusion elementwise | flops 4096 | bytes 49152 | tf_op jit(solution)/shard_map/add | solution.py:324
  (12 shorter events, 0.2 us)
Async XLA Ops:
  1.9 7.8 %collective-permute-start = (bf16[64,1280]{1,0:T(8,128)(2,1)S(1)}, bf16[64,1280]{1,0:T(8,128)(2,1)S(1)}, u32[]{:S(2)}, u32[]{:S(2)}) collective-permute-start(bf16[64,1280]{1,0:T(8,128)(2,1)S(1)} %get-tuple-element.30.refs_1_), channel_id=1, source_target_pairs={{0,8},{1,9},{2,10},{3,11},{4,12},{5,13},{6,14},{7,15},{8,0},{9,1},... | collective-permute-start | bytes 491528 | tf_op jit(solution)/shard_map/ppermute | solution.py:238
  2.4 7.6 %collective-permute-start.1 = (bf16[64,1280]{1,0:T(8,128)(2,1)S(1)}, bf16[64,1280]{1,0:T(8,128)(2,1)S(1)}, u32[]{:S(2)}, u32[]{:S(2)}) collective-permute-start(bf16[64,1280]{1,0:T(8,128)(2,1)S(1)} %get-tuple-element.31.refs_2_), channel_id=1, source_target_pairs={{0,16},{1,17},{2,18},{3,19},{4,20},{5,21},{6,22},{7,23},{8,24},{9,... | collective-permute-start | bytes 491528 | tf_op jit(solution)/shard_map/ppermute | solution.py:238
  5.0 8.0 %collective-permute-start.2 = (bf16[64,1280]{1,0:T(8,128)(2,1)S(1)}, bf16[64,1280]{1,0:T(8,128)(2,1)S(1)}, u32[]{:S(2)}, u32[]{:S(2)}) collective-permute-start(bf16[64,1280]{1,0:T(8,128)(2,1)S(1)} %get-tuple-element.32.refs_3_), channel_id=1, source_target_pairs={{0,24},{1,25},{2,26},{3,27},{4,28},{5,29},{6,30},{7,31},{8,16},{9,... | collective-permute-start | bytes 491528 | tf_op jit(solution)/shard_map/ppermute | solution.py:238
  5.1 4.6 %collective-permute-start.4 = (bf16[32,256]{1,0:T(8,128)(2,1)S(1)}, bf16[32,256]{1,0:T(8,128)(2,1)S(1)}, u32[]{:S(2)}, u32[]{:S(2)}) collective-permute-start(bf16[32,256]{1,0:T(8,128)(2,1)S(1)} %get-tuple-element.33.own_virt), channel_id=1, source_target_pairs={{0,4},{1,5},{2,6},{3,7},{4,0},{5,1},{6,2},{7,3},{8,13},{9,12},{10,... | collective-permute-start | bytes 49160 | tf_op jit(solution)/shard_map/ppermute | solution.py:242
  7.9 1.8 %collective-permute-start.3 = (bf16[32,256]{1,0:T(8,128)(2,1)S(1)}, bf16[32,256]{1,0:T(8,128)(2,1)S(1)}, u32[]{:S(2)}, u32[]{:S(2)}) collective-permute-start(bf16[32,256]{1,0:T(8,128)(2,1)S(1)} %get-tuple-element.33.own_virt), channel_id=1, source_target_pairs={{8,9},{9,8},{10,11},{11,10},{12,13},{13,12},{14,15},{15,14},{16,18... | collective-permute-start | bytes 49160 | tf_op jit(solution)/shard_map/ppermute | solution.py:242
  13.4 16.0 %collective-permute-start.10 = (bf16[64,2304]{1,0:T(8,128)(2,1)S(1)}, bf16[64,2304]{1,0:T(8,128)(2,1)S(1)}, u32[]{:S(2)}, u32[]{:S(2)}) collective-permute-start(bf16[64,2304]{1,0:T(8,128)(2,1)S(1)} %get-tuple-element.39), channel_id=1, source_target_pairs={{0,16},{1,17},{2,18},{3,19},{4,20},{5,21},{6,22},{7,23},{8,24},{9,... | collective-permute-start | bytes 884744 | tf_op jit(solution)/shard_map/ppermute | solution.py:238
  16.6 8.2 %collective-permute-start.5 = (bf16[32,1024]{1,0:T(8,128)(2,1)S(1)}, bf16[32,1024]{1,0:T(8,128)(2,1)S(1)}, u32[]{:S(2)}, u32[]{:S(2)}) collective-permute-start(bf16[32,1024]{1,0:T(8,128)(2,1)S(1)} %get-tuple-element.34), channel_id=1, source_target_pairs={{0,7},{1,6},{2,5},{3,4},{4,3},{5,2},{6,1},{7,0},{8,15},{9,14},{10,... | collective-permute-start | bytes 196616 | tf_op jit(solution)/shard_map/ppermute | solution.py:238
  19.6 6.3 %collective-permute-start.6 = (bf16[32,1024]{1,0:T(8,128)(2,1)S(1)}, bf16[32,1024]{1,0:T(8,128)(2,1)S(1)}, u32[]{:S(2)}, u32[]{:S(2)}) collective-permute-start(bf16[32,1024]{1,0:T(8,128)(2,1)S(1)} %get-tuple-element.35), channel_id=1, source_target_pairs={{0,6},{1,7},{2,4},{3,5},{4,2},{5,3},{6,0},{7,1},{8,14},{9,15},{10,... | collective-permute-start | bytes 196616 | tf_op jit(solution)/shard_map/ppermute | solution.py:238
  21.4 7.1 %collective-permute-start.7 = (bf16[32,1024]{1,0:T(8,128)(2,1)S(1)}, bf16[32,1024]{1,0:T(8,128)(2,1)S(1)}, u32[]{:S(2)}, u32[]{:S(2)}) collective-permute-start(bf16[32,1024]{1,0:T(8,128)(2,1)S(1)} %get-tuple-element.36), channel_id=1, source_target_pairs={{0,5},{1,4},{2,7},{3,6},{4,1},{5,0},{6,3},{7,2},{8,13},{9,12},{10,... | collective-permute-start | bytes 196616 | tf_op jit(solution)/shard_map/ppermute | solution.py:238
  21.4 7.7 %collective-permute-start.8 = (bf16[32,1024]{1,0:T(8,128)(2,1)S(1)}, bf16[32,1024]{1,0:T(8,128)(2,1)S(1)}, u32[]{:S(2)}, u32[]{:S(2)}) collective-permute-start(bf16[32,1024]{1,0:T(8,128)(2,1)S(1)} %get-tuple-element.37), channel_id=1, source_target_pairs={{0,3},{1,2},{2,1},{3,0},{4,7},{5,6},{6,5},{7,4},{8,11},{9,10},{10,... | collective-permute-start | bytes 196616 | tf_op jit(solution)/shard_map/ppermute | solution.py:238
  24.8 4.5 %collective-permute-start.9 = (bf16[32,1024]{1,0:T(8,128)(2,1)S(1)}, bf16[32,1024]{1,0:T(8,128)(2,1)S(1)}, u32[]{:S(2)}, u32[]{:S(2)}) collective-permute-start(bf16[32,1024]{1,0:T(8,128)(2,1)S(1)} %get-tuple-element.38), channel_id=1, source_target_pairs={{0,2},{1,3},{2,0},{3,1},{4,6},{5,7},{6,4},{7,5},{8,10},{9,11},{10,... | collective-permute-start | bytes 196616 | tf_op jit(solution)/shard_map/ppermute | solution.py:238
  29.3 2.6 %collective-permute-start.12 = (bf16[64,5376]{1,0:T(8,128)(2,1)S(1)}, bf16[64,5376]{1,0:T(8,128)(2,1)S(1)}, u32[]{:S(2)}, u32[]{:S(2)}) collective-permute-start(bf16[64,5376]{1,0:T(8,128)(2,1)S(1)} %get-tuple-element.44.refs_10_), channel_id=1, source_target_pairs={{0,8},{1,9},{2,10},{3,11},{4,12},{5,13},{6,14},{7,15},{8,0},{9,1},... | collective-permute-start | bytes 2064392 | tf_op jit(solution)/shard_map/ppermute | solution.py:238
  29.3 2.6 %collective-permute-start.11 = (bf16[64,2304]{1,0:T(8,128)(2,1)S(1)}, bf16[64,2304]{1,0:T(8,128)(2,1)S(1)}, u32[]{:S(2)}, u32[]{:S(2)}) collective-permute-start(bf16[64,2304]{1,0:T(8,128)(2,1)S(1)} %collective-permute-done.10.refs_7_), channel_id=1, source_target_pairs={{0,8},{1,9},{2,10},{3,11},{4,12},{5,13},{6,14},{7,15},{8,0},{9,1},... | collective-permute-start | bytes 884744 | tf_op jit(solution)/shard_map/ppermute | solution.py:238
  29.9 6.2 %collective-permute-start.13 = (bf16[32,1024]{1,0:T(8,128)(2,1)S(1)}, bf16[32,1024]{1,0:T(8,128)(2,1)S(1)}, u32[]{:S(2)}, u32[]{:S(2)}) collective-permute-start(bf16[32,1024]{1,0:T(8,128)(2,1)S(1)} %get-tuple-element.48), channel_id=1, source_target_pairs={{0,4},{1,5},{2,6},{3,7},{4,0},{5,1},{6,2},{7,3},{8,12},{9,13},{10,... | collective-permute-start | bytes 196616 | tf_op jit(solution)/shard_map/ppermute | solution.py:238
  30.7 5.4 %collective-permute-start.14 = (bf16[32,1024]{1,0:T(8,128)(2,1)S(1)}, bf16[32,1024]{1,0:T(8,128)(2,1)S(1)}, u32[]{:S(2)}, u32[]{:S(2)}) collective-permute-start(bf16[32,1024]{1,0:T(8,128)(2,1)S(1)} %get-tuple-element.51), channel_id=1, source_target_pairs={{0,1},{1,0},{2,3},{3,2},{4,5},{5,4},{6,7},{7,6},{8,9},{9,8},{10,11... | collective-permute-start | bytes 196616 | tf_op jit(solution)/shard_map/ppermute | solution.py:238
  36.7 4.6 %collective-permute-start.17 = (f32[32,128]{1,0:T(8,128)S(1)}, f32[32,128]{1,0:T(8,128)S(1)}, u32[]{:S(2)}, u32[]{:S(2)}) collective-permute-start(f32[32,128]{1,0:T(8,128)S(1)} %shard_map.58.refs_0_), channel_id=1, source_target_pairs={{0,3},{1,2},{2,1},{3,0},{4,7},{5,6},{6,5},{7,4},{8,11},{9,10},{10,... | collective-permute-start | bytes 49160 | tf_op jit(solution)/shard_map/ppermute | solution.py:238
  37.7 3.7 %collective-permute-start.16 = (f32[32,128]{1,0:T(8,128)S(1)}, f32[32,128]{1,0:T(8,128)S(1)}, u32[]{:S(2)}, u32[]{:S(2)}) collective-permute-start(f32[32,128]{1,0:T(8,128)S(1)} %shard_map.58.refs_0_), channel_id=1, source_target_pairs={{0,2},{1,3},{2,0},{3,1},{4,6},{5,7},{6,4},{7,5},{8,10},{9,11},{10,... | collective-permute-start | bytes 49160 | tf_op jit(solution)/shard_map/ppermute | solution.py:238
  39.0 3.7 %collective-permute-start.15 = (f32[32,128]{1,0:T(8,128)S(1)}, f32[32,128]{1,0:T(8,128)S(1)}, u32[]{:S(2)}, u32[]{:S(2)}) collective-permute-start(f32[32,128]{1,0:T(8,128)S(1)} %shard_map.58.refs_0_), channel_id=1, source_target_pairs={{0,1},{1,0},{2,3},{3,2},{4,5},{5,4},{6,7},{7,6},{8,9},{9,8},{10,11... | collective-permute-start | bytes 49160 | tf_op jit(solution)/shard_map/ppermute | solution.py:238
  42.8 4.6 %collective-permute-start.18 = (f32[32,128]{1,0:T(8,128)S(1)}, f32[32,128]{1,0:T(8,128)S(1)}, u32[]{:S(2)}, u32[]{:S(2)}) collective-permute-start(f32[32,128]{1,0:T(8,128)S(1)} %shard_map.59), channel_id=1, source_target_pairs={{0,4},{1,5},{2,6},{3,7},{4,0},{5,1},{6,2},{7,3},{8,12},{9,13},{10,... | collective-permute-start | bytes 49160 | tf_op jit(solution)/shard_map/ppermute | solution.py:238

commit v6 on v5

--- a/solution.py
+++ b/solution.py
@@ -64,6 +64,10 @@
         items = [jnp.where(flag, items[m ^ bit], items[m]) for m in range(len(items))]
         bit *= 2
     return items
+
+
+def near_place(n_split, i):
+    return [m for m in range(n_split) if m != 1].index(i)
 
 
 def pack_kernel(n_split, occ_mask_hbm, virt_mask_hbm, b_hbm, occ_hbm, virt_hbm, virt_ref, *rest):
@@ -84,8 +88,9 @@
     virt_ref[...] = virt.astype(BF16)
     occ = screened(occ_green[...], occ_mask, s * (rows // block), block)
     occ = xor_blocks(occ, cols, t).astype(BF16)
+    width = group * naux + occ.shape[1]
     for m in range(n_split):
-        outs[m][:, group * naux:] = occ
+        outs[m][:, group * naux:width] = occ
     copies[0].wait()
     basis = jnp.swapaxes(b[...], 0, 1)
     for l in range(group):
@@ -93,6 +98,9 @@
         tiles = xor_list(tiles, s)
         for m in range(n_split):
             outs[m][:, l * naux:(l + 1) * naux] = tiles[m]
+            if m != 1:
+                start = width + near_place(n_split, m) * group * naux + l * naux
+                outs[1][:, start:start + naux] = tiles[m]
 
 
 def add_kernel(*refs):
@@ -129,7 +137,7 @@
     own, got, rest = refs[:n_split], refs[n_split:2 * n_split - 1][::-1], refs[2 * n_split - 1:]
     shares = n_tensor // n_split
     fetched, firsts, raws = rest[:shares], rest[shares:shares + n_tensor], rest[shares + n_tensor:]
-    whole = jnp.concatenate([p[...] for p in (own[0], *got)], axis=0)
+    whole = jnp.concatenate([p[:, :own[0].shape[1]] for p in (own[0], *got)], axis=0)
     first = lax.dot_general(
         whole[:, width:], whole[:, :width], (((0,), (0,)), ((), ())), preferred_element_type=F32
     )
@@ -142,7 +150,7 @@
         for n, i in enumerate(others(n_split, 2 * p)):
             raws[p - 1][:, n * width:(n + 1) * width] = own[i][:, :width]
         write_rows(raws[p - 1], (n_split - 2) * width, blocks)
-    pieces = [own[i] for i in range(n_split) if i != 1] + list(got[1:])
+    pieces = list(got[1:])
     for n, piece in enumerate(pieces):
         raws[-1][:, n * width:(n + 1) * width] = piece[:, :width]
     write_rows(raws[-1], len(pieces) * width, blocks)
@@ -163,12 +171,12 @@
         if q == 0:
             return got[m - 1], 0
         if m == 1:
-            return core, [i for i in range(n_split) if i != 1].index(q ^ 1)
+            return got[0], own[0].shape[1] + near_place(n_split, q ^ 1) * width
         if q == 1:
-            return core, n_split - 1 + (m ^ 1) - 2
-        return raws[m - 2], others(n_split, m).index(m ^ q)
-
-    core_start = (2 * n_split - 3) * width
+            return core, ((m ^ 1) - 2) * width
+        return raws[m - 2], others(n_split, m).index(m ^ q) * width
+
+    core_start = (n_split - 2) * width
     found = [read_rows(own_core, core_start, shares, cols, nao), read_rows(core, core_start, shares, cols, nao)]
     found += [read_rows(r, (n_split - 2) * width, shares, cols, nao) for r in raws]
     blocks = [tile for i in range(shares) for tile in xor_list([f[i] for f in found], s)]
@@ -190,7 +198,7 @@
                 tiles = []
                 for m in range(n_split):
                     ref, n = piece(m, q)
-                    tiles.append(ref[:, n * width + l * naux:n * width + (l + 1) * naux])
+                    tiles.append(ref[:, n + l * naux:n + (l + 1) * naux])
                 right.append(jnp.concatenate(tiles, axis=0))
             made = jnp.dot(left, jnp.concatenate(right, axis=1), preferred_element_type=F32).astype(BF16)
             tiles = swap_lane_blocks([made[:, q * naux:(q + 1) * naux] for q in range(n_split)], naux // n_split)
@@ -218,8 +226,10 @@
 
 def stages(count):
     bit, found = 1, []
+    if (count.bit_length() - 1) % 2:
+        bit, found = 2, [[1]]
     while bit < count:
-        found.append([bit, 2 * bit, 3 * bit] if 2 * bit < count else [bit])
+        found.append([bit, 2 * bit, 3 * bit])
         bit *= 4
     return found
 
@@ -245,7 +255,10 @@
     virt, *packed = pl.pallas_call(
         functools.partial(pack_kernel, n_split),
         out_shape=[jax.ShapeDtypeStruct(green_virt.shape, BF16)]
-        + [jax.ShapeDtypeStruct((rows, packed_width + nao), BF16)] * n_split,
+        + [
+            jax.ShapeDtypeStruct((rows, packed_width + nao + (m == 1) * (n_split - 1) * packed_width), BF16)
+            for m in range(n_split)
+        ],
         in_specs=[hbm] * 5,
         out_specs=[vmem] * (n_split + 1),
         scratch_shapes=[
@@ -265,7 +278,7 @@
     fetched = [fetch(virt, j) for j in range(shares)]
 
     virt_width = shares * nao * cols // rows
-    widths = [(n_split - 2) * packed_width + virt_width] * (n_split // 2 - 1) + [(2 * n_split - 3) * packed_width + virt_width]
+    widths = [(n_split - 2) * packed_width + virt_width] * (n_split // 2 - 1) + [(n_split - 2) * packed_width + virt_width]
     made = pl.pallas_call(
         functools.partial(first_kernel, n_split, n_tensor, packed_width),
         out_shape=[jax.ShapeDtypeStruct((cols, packed_width), BF16)] * n_tensor
@@ -312,7 +325,7 @@
     )(g, *got[::-1])
     for near in stages(n_tensor):
         got = [exchange(total, tensor_bits=k) for k in near]
-        if near[-1] * 2 < n_tensor:
+        if near != stages(n_tensor)[-1]:
             total = pl.pallas_call(
                 add_kernel,
                 out_shape=jax.ShapeDtypeStruct(total.shape, F32),

time: 48.2 us -> 47.8 us (level)
  waiting for transfers between devices: 18 us -> 16.9 us
  starting transfers between devices: 24.9 us -> 25.4 us
    ppermute x17, waiting for transfers between devices: 16.8 us -> 15.8 us  [exchange(): lax.ppermute(x, ('split', 'tensor'), [(d, d ^ bits) for d in range(count)])]
    ppermute x17, starting transfers between devices: 21.4 us -> 22 us  [exchange(): lax.ppermute(x, ('split', 'tensor'), [(d, d ^ bits) for d in range(count)])]
  transfers between devices with their start and end apart: 19 -> 19, of which waited for: 13 -> 11; matrix products, arithmetic and copies ran while one was open for 0% -> 0% of each run, Pallas kernels for 3% -> 3%
where the time goes in v6:
time: 47.8 us; the launch traced here: 47.6 us
  starting transfers between devices  25.4 us (53%)
  waiting for transfers between devices  16.9 us (35%)
  Pallas kernels  4.56 us (10%)
  other arithmetic  0.61 us (1%)
    ppermute x17, starting transfers between devices, exchange(): lax.ppermute(x, ('split', 'tensor'), [(d, d ^ bits) for d in range(count)])  22 us
    ppermute x17, waiting for transfers between devices, exchange(): lax.ppermute(x, ('split', 'tensor'), [(d, d ^ bits) for d in range(count)])  15.8 us
    ppermute x2, starting transfers between devices, fetch(): lax.ppermute(x, ('split', 'tensor'), [(a, b) for a, b in pairs if a != b])  3.47 us
    pallas_call x1, Pallas kernels, local(): pl.pallas_call(functools.partial(pack_kernel, n_split), out_shape=[jax.Sh...  1.92 us
    pallas_call x1, Pallas kernels, local(): pl.pallas_call(functools.partial(g_kernel, n_split, n_tensor, packed_widt...  1.65 us
    ppermute x2, waiting for transfers between devices, fetch(): lax.ppermute(x, ('split', 'tensor'), [(a, b) for a, b in pairs if a != b])  1.16 us
  transfers between devices with their start and end apart: 19, of which 11 were waited for; matrix products, arithmetic and copies ran while one was open for 0% of the time, Pallas kernels for 3%

profile of v6, /device:TPU:0, one launch (start us, length us, event | category | flops | bytes accessed | tf_op | source)
XLA Modules:
  0.0 47.6 jit_solution(3441080847757514614)
XLA Ops:
  0.0 1.9 %shard_map.55 = (bf16[32,256]{1,0:T(8,128)(2,1)S(1)}, bf16[64,1280]{1,0:T(8,128)(2,1)S(1)}, bf16[64,4352]{1,0:T(8,128)(2,1)S(1)}, bf16[64,1280]{1,0:T(8,128)(2,1)S(1)}, bf16[64,1280]{1,0:T(8,128)(2,1)S(1)}) custom-call(s32[8,8]{1,0:T(8,128)} %occ_mask_hbm.1, s32[8,8]{1,0:T(8,128)} %virt_mask_hbm.1, bf16[64,32,128]{2,1,0:T(8,128)(2,1)} %b_hbm.1, ...), custom_call_target="tpu_custom_call" | custom-call | tf_op jit(solution)/shard_map/pallas_call | solution.py:255
  1.9 0.5 %collective-permute-start = (bf16[64,4352]{1,0:T(8,128)(2,1)S(1)}, bf16[64,4352]{1,0:T(8,128)(2,1)S(1)}, u32[]{:S(2)}, u32[]{:S(2)}) collective-permute-start(bf16[64,4352]{1,0:T(8,128)(2,1)S(1)} %get-tuple-element.30.refs_1_), channel_id=1, source_target_pairs={{0,8},{1,9},{2,10},{3,11},{4,12},{5,13},{6,14},{7,15},{8,0},{9,1},... | collective-permute-start | bytes 1671176 | tf_op jit(solution)/shard_map/ppermute | solution.py:248
  2.4 2.6 %collective-permute-start.1 = (bf16[64,1280]{1,0:T(8,128)(2,1)S(1)}, bf16[64,1280]{1,0:T(8,128)(2,1)S(1)}, u32[]{:S(2)}, u32[]{:S(2)}) collective-permute-start(bf16[64,1280]{1,0:T(8,128)(2,1)S(1)} %get-tuple-element.31.refs_2_), channel_id=1, source_target_pairs={{0,16},{1,17},{2,18},{3,19},{4,20},{5,21},{6,22},{7,23},{8,24},{9,... | collective-permute-start | bytes 491528 | tf_op jit(solution)/shard_map/ppermute | solution.py:248
  5.0 0.1 collective-permute-start.2
  5.1 2.8 %collective-permute-start.4 = (bf16[32,256]{1,0:T(8,128)(2,1)S(1)}, bf16[32,256]{1,0:T(8,128)(2,1)S(1)}, u32[]{:S(2)}, u32[]{:S(2)}) collective-permute-start(bf16[32,256]{1,0:T(8,128)(2,1)S(1)} %get-tuple-element.33.own_virt), channel_id=1, source_target_pairs={{0,4},{1,5},{2,6},{3,7},{4,0},{5,1},{6,2},{7,3},{8,13},{9,12},{10,... | collective-permute-start | bytes 49160 | tf_op jit(solution)/shard_map/ppermute | solution.py:252
  7.9 0.7 %collective-permute-start.3 = (bf16[32,256]{1,0:T(8,128)(2,1)S(1)}, bf16[32,256]{1,0:T(8,128)(2,1)S(1)}, u32[]{:S(2)}, u32[]{:S(2)}) collective-permute-start(bf16[32,256]{1,0:T(8,128)(2,1)S(1)} %get-tuple-element.33.own_virt), channel_id=1, source_target_pairs={{8,9},{9,8},{10,11},{11,10},{12,13},{13,12},{14,15},{15,14},{16,18... | collective-permute-start | bytes 49160 | tf_op jit(solution)/shard_map/ppermute | solution.py:252
  8.6 1.2 %collective-permute-done.4.refs_8_ = bf16[32,256]{1,0:T(8,128)(2,1)S(1)} collective-permute-done((bf16[32,256]{1,0:T(8,128)(2,1)S(1)}, bf16[32,256]{1,0:T(8,128)(2,1)S(1)}, u32[]{:S(2)}, u32[]{:S(2)}) %collective-permute-start.4) | collective-permute-done | bytes 16416 | tf_op jit(solution)/shard_map/ppermute | solution.py:252
  9.7 0.3 collective-permute-done.1.refs_5_
  10.1 3.0 %collective-permute-done.2.refs_4_.refs_6_ = bf16[64,1280]{1,0:T(8,128)(2,1)S(1)} collective-permute-done((bf16[64,1280]{1,0:T(8,128)(2,1)S(1)}, bf16[64,1280]{1,0:T(8,128)(2,1)S(1)}, u32[]{:S(2)}, u32[]{:S(2)}) %collective-permute-start.2) | collective-permute-done | bytes 163872 | tf_op jit(solution)/shard_map/ppermute | solution.py:248
  13.1 0.3 shard_map.56
  13.4 3.2 %collective-permute-start.10 = (bf16[64,2304]{1,0:T(8,128)(2,1)S(1)}, bf16[64,2304]{1,0:T(8,128)(2,1)S(1)}, u32[]{:S(2)}, u32[]{:S(2)}) collective-permute-start(bf16[64,2304]{1,0:T(8,128)(2,1)S(1)} %get-tuple-element.39), channel_id=1, source_target_pairs={{0,16},{1,17},{2,18},{3,19},{4,20},{5,21},{6,22},{7,23},{8,24},{9,... | collective-permute-start | bytes 884744 | tf_op jit(solution)/shard_map/ppermute | solution.py:248
  16.6 3.0 %collective-permute-start.5 = (bf16[32,1024]{1,0:T(8,128)(2,1)S(1)}, bf16[32,1024]{1,0:T(8,128)(2,1)S(1)}, u32[]{:S(2)}, u32[]{:S(2)}) collective-permute-start(bf16[32,1024]{1,0:T(8,128)(2,1)S(1)} %get-tuple-element.34), channel_id=1, source_target_pairs={{0,7},{1,6},{2,5},{3,4},{4,3},{5,2},{6,1},{7,0},{8,15},{9,14},{10,... | collective-permute-start | bytes 196616 | tf_op jit(solution)/shard_map/ppermute | solution.py:248
  19.6 1.8 %collective-permute-start.6 = (bf16[32,1024]{1,0:T(8,128)(2,1)S(1)}, bf16[32,1024]{1,0:T(8,128)(2,1)S(1)}, u32[]{:S(2)}, u32[]{:S(2)}) collective-permute-start(bf16[32,1024]{1,0:T(8,128)(2,1)S(1)} %get-tuple-element.35), channel_id=1, source_target_pairs={{0,6},{1,7},{2,4},{3,5},{4,2},{5,3},{6,0},{7,1},{8,14},{9,15},{10,... | collective-permute-start | bytes 196616 | tf_op jit(solution)/shard_map/ppermute | solution.py:248
  21.4 3.5 %collective-permute-start.8 = (bf16[32,1024]{1,0:T(8,128)(2,1)S(1)}, bf16[32,1024]{1,0:T(8,128)(2,1)S(1)}, u32[]{:S(2)}, u32[]{:S(2)}) collective-permute-start(bf16[32,1024]{1,0:T(8,128)(2,1)S(1)} %get-tuple-element.37), channel_id=1, source_target_pairs={{0,3},{1,2},{2,1},{3,0},{4,7},{5,6},{6,5},{7,4},{8,11},{9,10},{10,... | collective-permute-start | bytes 196616 | tf_op jit(solution)/shard_map/ppermute | solution.py:248
  24.9 1.0 %collective-permute-done.6.refs_1_ = bf16[32,1024]{1,0:T(8,128)(2,1)S(1)} collective-permute-done((bf16[32,1024]{1,0:T(8,128)(2,1)S(1)}, bf16[32,1024]{1,0:T(8,128)(2,1)S(1)}, u32[]{:S(2)}, u32[]{:S(2)}) %collective-permute-start.6) | collective-permute-done | bytes 65568 | tf_op jit(solution)/shard_map/ppermute | solution.py:248
  25.9 2.6 %collective-permute-done.7.refs_2_ = bf16[32,1024]{1,0:T(8,128)(2,1)S(1)} collective-permute-done((bf16[32,1024]{1,0:T(8,128)(2,1)S(1)}, bf16[32,1024]{1,0:T(8,128)(2,1)S(1)}, u32[]{:S(2)}, u32[]{:S(2)}) %collective-permute-start.7) | collective-permute-done | bytes 65568 | tf_op jit(solution)/shard_map/ppermute | solution.py:248
  28.5 0.6 %collective-permute-done.8.refs_4_ = bf16[32,1024]{1,0:T(8,128)(2,1)S(1)} collective-permute-done((bf16[32,1024]{1,0:T(8,128)(2,1)S(1)}, bf16[32,1024]{1,0:T(8,128)(2,1)S(1)}, u32[]{:S(2)}, u32[]{:S(2)}) %collective-permute-start.8) | collective-permute-done | bytes 65568 | tf_op jit(solution)/shard_map/ppermute | solution.py:248
  29.1 0.3 collective-permute-done.9.refs_5_
  29.4 0.5 %collective-permute-start.11 = (bf16[64,2304]{1,0:T(8,128)(2,1)S(1)}, bf16[64,2304]{1,0:T(8,128)(2,1)S(1)}, u32[]{:S(2)}, u32[]{:S(2)}) collective-permute-start(bf16[64,2304]{1,0:T(8,128)(2,1)S(1)} %collective-permute-done.10.refs_7_), channel_id=1, source_target_pairs={{0,8},{1,9},{2,10},{3,11},{4,12},{5,13},{6,14},{7,15},{8,0},{9,1},... | collective-permute-start | bytes 884744 | tf_op jit(solution)/shard_map/ppermute | solution.py:248
  29.9 0.8 %collective-permute-start.13 = (bf16[32,1024]{1,0:T(8,128)(2,1)S(1)}, bf16[32,1024]{1,0:T(8,128)(2,1)S(1)}, u32[]{:S(2)}, u32[]{:S(2)}) collective-permute-start(bf16[32,1024]{1,0:T(8,128)(2,1)S(1)} %get-tuple-element.48), channel_id=1, source_target_pairs={{0,4},{1,5},{2,6},{3,7},{4,0},{5,1},{6,2},{7,3},{8,12},{9,13},{10,... | collective-permute-start | bytes 196616 | tf_op jit(solution)/shard_map/ppermute | solution.py:248
  30.7 0.8 %collective-permute-start.14 = (bf16[32,1024]{1,0:T(8,128)(2,1)S(1)}, bf16[32,1024]{1,0:T(8,128)(2,1)S(1)}, u32[]{:S(2)}, u32[]{:S(2)}) collective-permute-start(bf16[32,1024]{1,0:T(8,128)(2,1)S(1)} %get-tuple-element.51), channel_id=1, source_target_pairs={{0,1},{1,0},{2,3},{3,2},{4,5},{5,4},{6,7},{7,6},{8,9},{9,8},{10,11... | collective-permute-start | bytes 196616 | tf_op jit(solution)/shard_map/ppermute | solution.py:248
  31.5 1.6 %shard_map.57.g_ref = bf16[32,256,128]{2,1,0:T(8,128)(2,1)S(1)} custom-call(bf16[64,1280]{1,0:T(8,128)(2,1)S(1)} %get-tuple-element.29.refs_0_, bf16[64,4352]{1,0:T(8,128)(2,1)S(1)} %get-tuple-element.30.refs_1_, bf16[64,1280]{1,0:T(8,128)(2,1)S(1)} %get-tuple-element.31.refs_2_, bf16[64,1280]{1,0:T(8,128)(2,1)S(1)} %get-tuple-element.32.refs_3_, ...), custom_call_target="tpu_custom_call" | custom-call | tf_op jit(solution)/shard_map/pallas_call | solution.py:310
  33.1 3.0 %collective-permute-done.13.refs_3_ = bf16[32,1024]{1,0:T(8,128)(2,1)S(1)} collective-permute-done((bf16[32,1024]{1,0:T(8,128)(2,1)S(1)}, bf16[32,1024]{1,0:T(8,128)(2,1)S(1)}, u32[]{:S(2)}, u32[]{:S(2)}) %collective-permute-start.13) | collective-permute-done | bytes 65568 | tf_op jit(solution)/shard_map/ppermute | solution.py:248
  36.1 0.7 %shard_map.58.refs_0_ = f32[32,128]{1,0:T(8,128)S(1)} custom-call(bf16[32,256,128]{2,1,0:T(8,128)(2,1)S(1)} %shard_map.57.g_ref, bf16[32,1024]{1,0:T(8,128)(2,1)S(1)} %collective-permute-done.5.refs_0_, bf16[32,1024]{1,0:T(8,128)(2,1)S(1)} %collective-permute-done.6.refs_1_, bf16[32,1024]{1,0:T(8,128)(2,1)S(1)} %collective-permute-done.7.refs_2_, ...), custom_call_target="tpu_custom_call" | custom-call | tf_op jit(solution)/shard_map/pallas_call | solution.py:319
  36.8 0.8 %collective-permute-start.15 = (f32[32,128]{1,0:T(8,128)S(1)}, f32[32,128]{1,0:T(8,128)S(1)}, u32[]{:S(2)}, u32[]{:S(2)}) collective-permute-start(f32[32,128]{1,0:T(8,128)S(1)} %shard_map.58.refs_0_), channel_id=1, source_target_pairs={{0,1},{1,0},{2,3},{3,2},{4,5},{5,4},{6,7},{7,6},{8,9},{9,8},{10,11... | collective-permute-start | bytes 49160 | tf_op jit(solution)/shard_map/ppermute | solution.py:248
  37.6 2.9 %collective-permute-done.15.refs_1_ = f32[32,128]{1,0:T(8,128)S(1)} collective-permute-done((f32[32,128]{1,0:T(8,128)S(1)}, f32[32,128]{1,0:T(8,128)S(1)}, u32[]{:S(2)}, u32[]{:S(2)}) %collective-permute-start.15) | collective-permute-done | bytes 16416 | tf_op jit(solution)/shard_map/ppermute | solution.py:248
  40.5 1.8 %collective-permute-start.18 = (f32[32,128]{1,0:T(8,128)S(1)}, f32[32,128]{1,0:T(8,128)S(1)}, u32[]{:S(2)}, u32[]{:S(2)}) collective-permute-start(f32[32,128]{1,0:T(8,128)S(1)} %shard_map.59), channel_id=1, source_target_pairs={{0,6},{1,7},{2,4},{3,5},{4,2},{5,3},{6,0},{7,1},{8,14},{9,15},{10,... | collective-permute-start | bytes 49160 | tf_op jit(solution)/shard_map/ppermute | solution.py:248
  42.3 0.2 collective-permute-start.17
  42.5 2.4 %collective-permute-start.16 = (f32[32,128]{1,0:T(8,128)S(1)}, f32[32,128]{1,0:T(8,128)S(1)}, u32[]{:S(2)}, u32[]{:S(2)}) collective-permute-start(f32[32,128]{1,0:T(8,128)S(1)} %shard_map.59), channel_id=1, source_target_pairs={{0,2},{1,3},{2,0},{3,1},{4,6},{5,7},{6,4},{7,5},{8,10},{9,11},{10,... | collective-permute-start | bytes 49160 | tf_op jit(solution)/shard_map/ppermute | solution.py:248
  44.9 1.1 %collective-permute-done.18 = f32[32,128]{1,0:T(8,128)S(1)} collective-permute-done((f32[32,128]{1,0:T(8,128)S(1)}, f32[32,128]{1,0:T(8,128)S(1)}, u32[]{:S(2)}, u32[]{:S(2)}) %collective-permute-start.18) | collective-permute-done | bytes 16416 | tf_op jit(solution)/shard_map/ppermute | solution.py:248
  46.0 0.9 %collective-permute-done.17 = f32[32,128]{1,0:T(8,128)S(1)} collective-permute-done((f32[32,128]{1,0:T(8,128)S(1)}, f32[32,128]{1,0:T(8,128)S(1)}, u32[]{:S(2)}, u32[]{:S(2)}) %collective-permute-start.17) | collective-permute-done | bytes 16416 | tf_op jit(solution)/shard_map/ppermute | solution.py:248
  47.0 0.6 %add_add_fusion = f32[32,128]{1,0:T(8,128)} fusion(f32[32,128]{1,0:T(8,128)S(1)} %collective-permute-done.18, f32[32,128]{1,0:T(8,128)S(1)} %collective-permute-done.17, f32[32,128]{1,0:T(8,128)S(1)} %shard_map.59, f32[32,128]{1,0:T(8,128)S(1)} %collective-permute-done.16), kind=kLoop, calls=%fused_computation | loop fusion | flops 12288 | bytes 81920 | tf_op jit(solution)/shard_map/add | solution.py:337
  (12 shorter events, 0.0 us)
Async XLA Ops:
  1.9 11.1 %collective-permute-start = (bf16[64,4352]{1,0:T(8,128)(2,1)S(1)}, bf16[64,4352]{1,0:T(8,128)(2,1)S(1)}, u32[]{:S(2)}, u32[]{:S(2)}) collective-permute-start(bf16[64,4352]{1,0:T(8,128)(2,1)S(1)} %get-tuple-element.30.refs_1_), channel_id=1, source_target_pairs={{0,8},{1,9},{2,10},{3,11},{4,12},{5,13},{6,14},{7,15},{8,0},{9,1},... | collective-permute-start | bytes 1671176 | tf_op jit(solution)/shard_map/ppermute | solution.py:248
  2.4 7.6 %collective-permute-start.1 = (bf16[64,1280]{1,0:T(8,128)(2,1)S(1)}, bf16[64,1280]{1,0:T(8,128)(2,1)S(1)}, u32[]{:S(2)}, u32[]{:S(2)}) collective-permute-start(bf16[64,1280]{1,0:T(8,128)(2,1)S(1)} %get-tuple-element.31.refs_2_), channel_id=1, source_target_pairs={{0,16},{1,17},{2,18},{3,19},{4,20},{5,21},{6,22},{7,23},{8,24},{9,... | collective-permute-start | bytes 491528 | tf_op jit(solution)/shard_map/ppermute | solution.py:248
  5.0 8.0 %collective-permute-start.2 = (bf16[64,1280]{1,0:T(8,128)(2,1)S(1)}, bf16[64,1280]{1,0:T(8,128)(2,1)S(1)}, u32[]{:S(2)}, u32[]{:S(2)}) collective-permute-start(bf16[64,1280]{1,0:T(8,128)(2,1)S(1)} %get-tuple-element.32.refs_3_), channel_id=1, source_target_pairs={{0,24},{1,25},{2,26},{3,27},{4,28},{5,29},{6,30},{7,31},{8,16},{9,... | collective-permute-start | bytes 491528 | tf_op jit(solution)/shard_map/ppermute | solution.py:248
  5.1 4.6 %collective-permute-start.4 = (bf16[32,256]{1,0:T(8,128)(2,1)S(1)}, bf16[32,256]{1,0:T(8,128)(2,1)S(1)}, u32[]{:S(2)}, u32[]{:S(2)}) collective-permute-start(bf16[32,256]{1,0:T(8,128)(2,1)S(1)} %get-tuple-element.33.own_virt), channel_id=1, source_target_pairs={{0,4},{1,5},{2,6},{3,7},{4,0},{5,1},{6,2},{7,3},{8,13},{9,12},{10,... | collective-permute-start | bytes 49160 | tf_op jit(solution)/shard_map/ppermute | solution.py:252
  7.9 1.8 %collective-permute-start.3 = (bf16[32,256]{1,0:T(8,128)(2,1)S(1)}, bf16[32,256]{1,0:T(8,128)(2,1)S(1)}, u32[]{:S(2)}, u32[]{:S(2)}) collective-permute-start(bf16[32,256]{1,0:T(8,128)(2,1)S(1)} %get-tuple-element.33.own_virt), channel_id=1, source_target_pairs={{8,9},{9,8},{10,11},{11,10},{12,13},{13,12},{14,15},{15,14},{16,18... | collective-permute-start | bytes 49160 | tf_op jit(solution)/shard_map/ppermute | solution.py:252
  13.4 16.0 %collective-permute-start.10 = (bf16[64,2304]{1,0:T(8,128)(2,1)S(1)}, bf16[64,2304]{1,0:T(8,128)(2,1)S(1)}, u32[]{:S(2)}, u32[]{:S(2)}) collective-permute-start(bf16[64,2304]{1,0:T(8,128)(2,1)S(1)} %get-tuple-element.39), channel_id=1, source_target_pairs={{0,16},{1,17},{2,18},{3,19},{4,20},{5,21},{6,22},{7,23},{8,24},{9,... | collective-permute-start | bytes 884744 | tf_op jit(solution)/shard_map/ppermute | solution.py:248
  16.6 8.3 %collective-permute-start.5 = (bf16[32,1024]{1,0:T(8,128)(2,1)S(1)}, bf16[32,1024]{1,0:T(8,128)(2,1)S(1)}, u32[]{:S(2)}, u32[]{:S(2)}) collective-permute-start(bf16[32,1024]{1,0:T(8,128)(2,1)S(1)} %get-tuple-element.34), channel_id=1, source_target_pairs={{0,7},{1,6},{2,5},{3,4},{4,3},{5,2},{6,1},{7,0},{8,15},{9,14},{10,... | collective-permute-start | bytes 196616 | tf_op jit(solution)/shard_map/ppermute | solution.py:248
  19.6 6.3 %collective-permute-start.6 = (bf16[32,1024]{1,0:T(8,128)(2,1)S(1)}, bf16[32,1024]{1,0:T(8,128)(2,1)S(1)}, u32[]{:S(2)}, u32[]{:S(2)}) collective-permute-start(bf16[32,1024]{1,0:T(8,128)(2,1)S(1)} %get-tuple-element.35), channel_id=1, source_target_pairs={{0,6},{1,7},{2,4},{3,5},{4,2},{5,3},{6,0},{7,1},{8,14},{9,15},{10,... | collective-permute-start | bytes 196616 | tf_op jit(solution)/shard_map/ppermute | solution.py:248
  21.4 7.1 %collective-permute-start.7 = (bf16[32,1024]{1,0:T(8,128)(2,1)S(1)}, bf16[32,1024]{1,0:T(8,128)(2,1)S(1)}, u32[]{:S(2)}, u32[]{:S(2)}) collective-permute-start(bf16[32,1024]{1,0:T(8,128)(2,1)S(1)} %get-tuple-element.36), channel_id=1, source_target_pairs={{0,5},{1,4},{2,7},{3,6},{4,1},{5,0},{6,3},{7,2},{8,13},{9,12},{10,... | collective-permute-start | bytes 196616 | tf_op jit(solution)/shard_map/ppermute | solution.py:248
  21.4 7.7 %collective-permute-start.8 = (bf16[32,1024]{1,0:T(8,128)(2,1)S(1)}, bf16[32,1024]{1,0:T(8,128)(2,1)S(1)}, u32[]{:S(2)}, u32[]{:S(2)}) collective-permute-start(bf16[32,1024]{1,0:T(8,128)(2,1)S(1)} %get-tuple-element.37), channel_id=1, source_target_pairs={{0,3},{1,2},{2,1},{3,0},{4,7},{5,6},{6,5},{7,4},{8,11},{9,10},{10,... | collective-permute-start | bytes 196616 | tf_op jit(solution)/shard_map/ppermute | solution.py:248
  24.9 4.5 %collective-permute-start.9 = (bf16[32,1024]{1,0:T(8,128)(2,1)S(1)}, bf16[32,1024]{1,0:T(8,128)(2,1)S(1)}, u32[]{:S(2)}, u32[]{:S(2)}) collective-permute-start(bf16[32,1024]{1,0:T(8,128)(2,1)S(1)} %get-tuple-element.38), channel_id=1, source_target_pairs={{0,2},{1,3},{2,0},{3,1},{4,6},{5,7},{6,4},{7,5},{8,10},{9,11},{10,... | collective-permute-start | bytes 196616 | tf_op jit(solution)/shard_map/ppermute | solution.py:248
  29.4 2.1 %collective-permute-start.12 = (bf16[64,2304]{1,0:T(8,128)(2,1)S(1)}, bf16[64,2304]{1,0:T(8,128)(2,1)S(1)}, u32[]{:S(2)}, u32[]{:S(2)}) collective-permute-start(bf16[64,2304]{1,0:T(8,128)(2,1)S(1)} %get-tuple-element.44.refs_10_), channel_id=1, source_target_pairs={{0,8},{1,9},{2,10},{3,11},{4,12},{5,13},{6,14},{7,15},{8,0},{9,1},... | collective-permute-start | bytes 884744 | tf_op jit(solution)/shard_map/ppermute | solution.py:248
  29.4 2.1 %collective-permute-start.11 = (bf16[64,2304]{1,0:T(8,128)(2,1)S(1)}, bf16[64,2304]{1,0:T(8,128)(2,1)S(1)}, u32[]{:S(2)}, u32[]{:S(2)}) collective-permute-start(bf16[64,2304]{1,0:T(8,128)(2,1)S(1)} %collective-permute-done.10.refs_7_), channel_id=1, source_target_pairs={{0,8},{1,9},{2,10},{3,11},{4,12},{5,13},{6,14},{7,15},{8,0},{9,1},... | collective-permute-start | bytes 884744 | tf_op jit(solution)/shard_map/ppermute | solution.py:248
  29.9 6.2 %collective-permute-start.13 = (bf16[32,1024]{1,0:T(8,128)(2,1)S(1)}, bf16[32,1024]{1,0:T(8,128)(2,1)S(1)}, u32[]{:S(2)}, u32[]{:S(2)}) collective-permute-start(bf16[32,1024]{1,0:T(8,128)(2,1)S(1)} %get-tuple-element.48), channel_id=1, source_target_pairs={{0,4},{1,5},{2,6},{3,7},{4,0},{5,1},{6,2},{7,3},{8,12},{9,13},{10,... | collective-permute-start | bytes 196616 | tf_op jit(solution)/shard_map/ppermute | solution.py:248
  30.7 5.4 %collective-permute-start.14 = (bf16[32,1024]{1,0:T(8,128)(2,1)S(1)}, bf16[32,1024]{1,0:T(8,128)(2,1)S(1)}, u32[]{:S(2)}, u32[]{:S(2)}) collective-permute-start(bf16[32,1024]{1,0:T(8,128)(2,1)S(1)} %get-tuple-element.51), channel_id=1, source_target_pairs={{0,1},{1,0},{2,3},{3,2},{4,5},{5,4},{6,7},{7,6},{8,9},{9,8},{10,11... | collective-permute-start | bytes 196616 | tf_op jit(solution)/shard_map/ppermute | solution.py:248
  36.8 3.8 %collective-permute-start.15 = (f32[32,128]{1,0:T(8,128)S(1)}, f32[32,128]{1,0:T(8,128)S(1)}, u32[]{:S(2)}, u32[]{:S(2)}) collective-permute-start(f32[32,128]{1,0:T(8,128)S(1)} %shard_map.58.refs_0_), channel_id=1, source_target_pairs={{0,1},{1,0},{2,3},{3,2},{4,5},{5,4},{6,7},{7,6},{8,9},{9,8},{10,11... | collective-permute-start | bytes 49160 | tf_op jit(solution)/shard_map/ppermute | solution.py:248
  40.5 5.5 %collective-permute-start.18 = (f32[32,128]{1,0:T(8,128)S(1)}, f32[32,128]{1,0:T(8,128)S(1)}, u32[]{:S(2)}, u32[]{:S(2)}) collective-permute-start(f32[32,128]{1,0:T(8,128)S(1)} %shard_map.59), channel_id=1, source_target_pairs={{0,6},{1,7},{2,4},{3,5},{4,2},{5,3},{6,0},{7,1},{8,14},{9,15},{10,... | collective-permute-start | bytes 49160 | tf_op jit(solution)/shard_map/ppermute | solution.py:248
  42.3 4.6 %collective-permute-start.17 = (f32[32,128]{1,0:T(8,128)S(1)}, f32[32,128]{1,0:T(8,128)S(1)}, u32[]{:S(2)}, u32[]{:S(2)}) collective-permute-start(f32[32,128]{1,0:T(8,128)S(1)} %shard_map.59), channel_id=1, source_target_pairs={{0,4},{1,5},{2,6},{3,7},{4,0},{5,1},{6,2},{7,3},{8,12},{9,13},{10,... | collective-permute-start | bytes 49160 | tf_op jit(solution)/shard_map/ppermute | solution.py:248
  42.5 4.4 %collective-permute-start.16 = (f32[32,128]{1,0:T(8,128)S(1)}, f32[32,128]{1,0:T(8,128)S(1)}, u32[]{:S(2)}, u32[]{:S(2)}) collective-permute-start(f32[32,128]{1,0:T(8,128)S(1)} %shard_map.59), channel_id=1, source_target_pairs={{0,2},{1,3},{2,0},{3,1},{4,6},{5,7},{6,4},{7,5},{8,10},{9,11},{10,... | collective-permute-start | bytes 49160 | tf_op jit(solution)/shard_map/ppermute | solution.py:248

commit v7 on v6

--- a/solution.py
+++ b/solution.py
@@ -248,8 +248,11 @@
         return lax.ppermute(x, ("split", "tensor"), [(d, d ^ bits) for d in range(count)])
 
     def fetch(x, j):
-        pairs = [(s * n_tensor + t, s * n_tensor + (t ^ (j * n_split + s))) for s in range(n_split) for t in range(n_tensor)]
-        return lax.ppermute(x, ("split", "tensor"), [(a, b) for a, b in pairs if a != b])
+        pairs = []
+        for s in range(n_split):
+            k = j * n_split + s
+            pairs += [(s * n_tensor + t, s * n_tensor + (t ^ max(k, 1))) for t in range(n_tensor)]
+        return lax.ppermute(x, ("split", "tensor"), pairs)
 
     arguments = [occ_mask, virt_mask, three_centre, green_occ, green_virt]
     virt, *packed = pl.pallas_call(
@@ -292,7 +295,8 @@
     moved = {}
     moved.update({m: exchange(raws[m // 2 - 1], split_bits=m) for m in range(2, n_split, 2)})
     got = {0: firsts[0]}
-    ahead = [k for k in range(n_tensor - 1, 1, -1) if k != n_tensor // 2]
+    far = range(n_tensor - 1, n_tensor // 2, -1)
+    ahead = [k for k in far if k % 2] + [k for k in far if k % 2 == 0] + list(range(n_tensor // 2 - 1, 2, -1))
     got.update({k: exchange(firsts[k], tensor_bits=k) for k in ahead})
     later = [k for k in range(n_tensor - 1, 0, -1) if k not in ahead]
     evens = list(range(2, n_split, 2))

time: 47.8 us -> 47.2 us (0.987)
  waiting for transfers between devices: 16.9 us -> 13.8 us
  starting transfers between devices: 25.4 us -> 28.1 us
    ppermute x17, waiting for transfers between devices: 15.8 us -> 11.4 us  [exchange(): lax.ppermute(x, ('split', 'tensor'), [(d, d ^ bits) for d in range(count)])]
    ppermute x17, starting transfers between devices: 22 us -> 23.7 us  [exchange(): lax.ppermute(x, ('split', 'tensor'), [(d, d ^ bits) for d in range(count)])]
    ppermute x2, waiting for transfers between devices: 1.16 us -> 2.34 us  [fetch(): return lax.ppermute(x, ('split', 'tensor'), pairs)]
    ppermute x2, starting transfers between devices: 3.47 us -> 4.34 us  [fetch(): return lax.ppermute(x, ('split', 'tensor'), pairs)]
where the time goes in v7:
time: 47.2 us; the launch traced here: 47.1 us
  starting transfers between devices  28.1 us (60%)
  waiting for transfers between devices  13.8 us (29%)
  Pallas kernels  4.56 us (10%)
  other arithmetic  0.61 us (1%)
    ppermute x17, starting transfers between devices, exchange(): lax.ppermute(x, ('split', 'tensor'), [(d, d ^ bits) for d in range(count)])  23.7 us
    ppermute x17, waiting for transfers between devices, exchange(): lax.ppermute(x, ('split', 'tensor'), [(d, d ^ bits) for d in range(count)])  11.4 us
    ppermute x2, starting transfers between devices, fetch(): return lax.ppermute(x, ('split', 'tensor'), pairs)  4.34 us
    ppermute x2, waiting for transfers between devices, fetch(): return lax.ppermute(x, ('split', 'tensor'), pairs)  2.34 us
    pallas_call x1, Pallas kernels, local(): pl.pallas_call(functools.partial(pack_kernel, n_split), out_shape=[jax.Sh...  1.92 us
    pallas_call x1, Pallas kernels, local(): pl.pallas_call(functools.partial(g_kernel, n_split, n_tensor, packed_widt...  1.65 us
  transfers between devices with their start and end apart: 19, of which 11 were waited for; matrix products, arithmetic and copies ran while one was open for 0% of the time, Pallas kernels for 3%

profile of v7, /device:TPU:0, one launch (start us, length us, event | category | flops | bytes accessed | tf_op | source)
XLA Modules:
  0.0 47.1 jit_solution(4230853343769216409)
XLA Ops:
  0.0 1.9 %shard_map.55 = (bf16[32,256]{1,0:T(8,128)(2,1)S(1)}, bf16[64,1280]{1,0:T(8,128)(2,1)S(1)}, bf16[64,4352]{1,0:T(8,128)(2,1)S(1)}, bf16[64,1280]{1,0:T(8,128)(2,1)S(1)}, bf16[64,1280]{1,0:T(8,128)(2,1)S(1)}) custom-call(s32[8,8]{1,0:T(8,128)} %occ_mask_hbm.1, s32[8,8]{1,0:T(8,128)} %virt_mask_hbm.1, bf16[64,32,128]{2,1,0:T(8,128)(2,1)} %b_hbm.1, ...), custom_call_target="tpu_custom_call" | custom-call | tf_op jit(solution)/shard_map/pallas_call | solution.py:258
  1.9 0.5 %collective-permute-start = (bf16[64,4352]{1,0:T(8,128)(2,1)S(1)}, bf16[64,4352]{1,0:T(8,128)(2,1)S(1)}, u32[]{:S(2)}, u32[]{:S(2)}) collective-permute-start(bf16[64,4352]{1,0:T(8,128)(2,1)S(1)} %get-tuple-element.30.refs_1_), channel_id=1, source_target_pairs={{0,8},{1,9},{2,10},{3,11},{4,12},{5,13},{6,14},{7,15},{8,0},{9,1},... | collective-permute-start | bytes 1671176 | tf_op jit(solution)/shard_map/ppermute | solution.py:248
  2.4 2.6 %collective-permute-start.1 = (bf16[64,1280]{1,0:T(8,128)(2,1)S(1)}, bf16[64,1280]{1,0:T(8,128)(2,1)S(1)}, u32[]{:S(2)}, u32[]{:S(2)}) collective-permute-start(bf16[64,1280]{1,0:T(8,128)(2,1)S(1)} %get-tuple-element.31.refs_2_), channel_id=1, source_target_pairs={{0,16},{1,17},{2,18},{3,19},{4,20},{5,21},{6,22},{7,23},{8,24},{9,... | collective-permute-start | bytes 491528 | tf_op jit(solution)/shard_map/ppermute | solution.py:248
  5.1 2.8 %collective-permute-start.4 = (bf16[32,256]{1,0:T(8,128)(2,1)S(1)}, bf16[32,256]{1,0:T(8,128)(2,1)S(1)}, u32[]{:S(2)}, u32[]{:S(2)}) collective-permute-start(bf16[32,256]{1,0:T(8,128)(2,1)S(1)} %get-tuple-element.33.own_virt), channel_id=1, source_target_pairs={{0,4},{1,5},{2,6},{3,7},{4,0},{5,1},{6,2},{7,3},{8,13},{9,12},{10,... | collective-permute-start | bytes 49160 | tf_op jit(solution)/shard_map/ppermute | solution.py:255
  7.9 1.5 %collective-permute-start.3 = (bf16[32,256]{1,0:T(8,128)(2,1)S(1)}, bf16[32,256]{1,0:T(8,128)(2,1)S(1)}, u32[]{:S(2)}, u32[]{:S(2)}) collective-permute-start(bf16[32,256]{1,0:T(8,128)(2,1)S(1)} %get-tuple-element.33.own_virt), channel_id=1, source_target_pairs={{0,1},{1,0},{2,3},{3,2},{4,5},{5,4},{6,7},{7,6},{8,9},{9,8},{10,11... | collective-permute-start | bytes 49160 | tf_op jit(solution)/shard_map/ppermute | solution.py:255
  9.4 0.3 collective-permute-done.4.refs_8_
  9.7 2.0 %collective-permute-done.3.refs_7_ = bf16[32,256]{1,0:T(8,128)(2,1)S(1)} collective-permute-done((bf16[32,256]{1,0:T(8,128)(2,1)S(1)}, bf16[32,256]{1,0:T(8,128)(2,1)S(1)}, u32[]{:S(2)}, u32[]{:S(2)}) %collective-permute-start.3) | collective-permute-done | bytes 16416 | tf_op jit(solution)/shard_map/ppermute | solution.py:255
  11.8 1.3 %collective-permute-done.2.refs_4_.refs_6_ = bf16[64,1280]{1,0:T(8,128)(2,1)S(1)} collective-permute-done((bf16[64,1280]{1,0:T(8,128)(2,1)S(1)}, bf16[64,1280]{1,0:T(8,128)(2,1)S(1)}, u32[]{:S(2)}, u32[]{:S(2)}) %collective-permute-start.2) | collective-permute-done | bytes 163872 | tf_op jit(solution)/shard_map/ppermute | solution.py:248
  13.1 0.3 shard_map.56
  13.4 1.6 %collective-permute-start.9 = (bf16[64,2304]{1,0:T(8,128)(2,1)S(1)}, bf16[64,2304]{1,0:T(8,128)(2,1)S(1)}, u32[]{:S(2)}, u32[]{:S(2)}) collective-permute-start(bf16[64,2304]{1,0:T(8,128)(2,1)S(1)} %get-tuple-element.38), channel_id=1, source_target_pairs={{0,16},{1,17},{2,18},{3,19},{4,20},{5,21},{6,22},{7,23},{8,24},{9,... | collective-permute-start | bytes 884744 | tf_op jit(solution)/shard_map/ppermute | solution.py:248
  15.0 4.6 %collective-permute-start.5 = (bf16[32,1024]{1,0:T(8,128)(2,1)S(1)}, bf16[32,1024]{1,0:T(8,128)(2,1)S(1)}, u32[]{:S(2)}, u32[]{:S(2)}) collective-permute-start(bf16[32,1024]{1,0:T(8,128)(2,1)S(1)} %get-tuple-element.34), channel_id=1, source_target_pairs={{0,7},{1,6},{2,5},{3,4},{4,3},{5,2},{6,1},{7,0},{8,15},{9,14},{10,... | collective-permute-start | bytes 196616 | tf_op jit(solution)/shard_map/ppermute | solution.py:248
  19.6 1.9 %collective-permute-start.7 = (bf16[32,1024]{1,0:T(8,128)(2,1)S(1)}, bf16[32,1024]{1,0:T(8,128)(2,1)S(1)}, u32[]{:S(2)}, u32[]{:S(2)}) collective-permute-start(bf16[32,1024]{1,0:T(8,128)(2,1)S(1)} %get-tuple-element.36), channel_id=1, source_target_pairs={{0,6},{1,7},{2,4},{3,5},{4,2},{5,3},{6,0},{7,1},{8,14},{9,15},{10,... | collective-permute-start | bytes 196616 | tf_op jit(solution)/shard_map/ppermute | solution.py:248
  21.4 2.5 %collective-permute-start.8 = (bf16[32,1024]{1,0:T(8,128)(2,1)S(1)}, bf16[32,1024]{1,0:T(8,128)(2,1)S(1)}, u32[]{:S(2)}, u32[]{:S(2)}) collective-permute-start(bf16[32,1024]{1,0:T(8,128)(2,1)S(1)} %get-tuple-element.37), channel_id=1, source_target_pairs={{0,3},{1,2},{2,1},{3,0},{4,7},{5,6},{6,5},{7,4},{8,11},{9,10},{10,... | collective-permute-start | bytes 196616 | tf_op jit(solution)/shard_map/ppermute | solution.py:248
  24.0 3.4 %collective-permute-done.6.refs_2_ = bf16[32,1024]{1,0:T(8,128)(2,1)S(1)} collective-permute-done((bf16[32,1024]{1,0:T(8,128)(2,1)S(1)}, bf16[32,1024]{1,0:T(8,128)(2,1)S(1)}, u32[]{:S(2)}, u32[]{:S(2)}) %collective-permute-start.6) | collective-permute-done | bytes 65568 | tf_op jit(solution)/shard_map/ppermute | solution.py:248
  27.3 0.6 %collective-permute-done.8.refs_4_ = bf16[32,1024]{1,0:T(8,128)(2,1)S(1)} collective-permute-done((bf16[32,1024]{1,0:T(8,128)(2,1)S(1)}, bf16[32,1024]{1,0:T(8,128)(2,1)S(1)}, u32[]{:S(2)}, u32[]{:S(2)}) %collective-permute-start.8) | collective-permute-done | bytes 65568 | tf_op jit(solution)/shard_map/ppermute | solution.py:248
  27.9 0.5 %collective-permute-start.10 = (bf16[64,2304]{1,0:T(8,128)(2,1)S(1)}, bf16[64,2304]{1,0:T(8,128)(2,1)S(1)}, u32[]{:S(2)}, u32[]{:S(2)}) collective-permute-start(bf16[64,2304]{1,0:T(8,128)(2,1)S(1)} %collective-permute-done.9.refs_7_), channel_id=1, source_target_pairs={{0,8},{1,9},{2,10},{3,11},{4,12},{5,13},{6,14},{7,15},{8,0},{9,1},... | collective-permute-start | bytes 884744 | tf_op jit(solution)/shard_map/ppermute | solution.py:248
  28.4 1.9 %collective-permute-start.12 = (bf16[32,1024]{1,0:T(8,128)(2,1)S(1)}, bf16[32,1024]{1,0:T(8,128)(2,1)S(1)}, u32[]{:S(2)}, u32[]{:S(2)}) collective-permute-start(bf16[32,1024]{1,0:T(8,128)(2,1)S(1)} %get-tuple-element.48), channel_id=1, source_target_pairs={{0,4},{1,5},{2,6},{3,7},{4,0},{5,1},{6,2},{7,3},{8,12},{9,13},{10,... | collective-permute-start | bytes 196616 | tf_op jit(solution)/shard_map/ppermute | solution.py:248
  30.4 1.1 %collective-permute-start.13 = (bf16[32,1024]{1,0:T(8,128)(2,1)S(1)}, bf16[32,1024]{1,0:T(8,128)(2,1)S(1)}, u32[]{:S(2)}, u32[]{:S(2)}) collective-permute-start(bf16[32,1024]{1,0:T(8,128)(2,1)S(1)} %get-tuple-element.50), channel_id=1, source_target_pairs={{0,2},{1,3},{2,0},{3,1},{4,6},{5,7},{6,4},{7,5},{8,10},{9,11},{10,... | collective-permute-start | bytes 196616 | tf_op jit(solution)/shard_map/ppermute | solution.py:248
  31.5 1.0 %collective-permute-start.14 = (bf16[32,1024]{1,0:T(8,128)(2,1)S(1)}, bf16[32,1024]{1,0:T(8,128)(2,1)S(1)}, u32[]{:S(2)}, u32[]{:S(2)}) collective-permute-start(bf16[32,1024]{1,0:T(8,128)(2,1)S(1)} %get-tuple-element.51), channel_id=1, source_target_pairs={{0,1},{1,0},{2,3},{3,2},{4,5},{5,4},{6,7},{7,6},{8,9},{9,8},{10,11... | collective-permute-start | bytes 196616 | tf_op jit(solution)/shard_map/ppermute | solution.py:248
  32.5 1.6 %shard_map.57.g_ref = bf16[32,256,128]{2,1,0:T(8,128)(2,1)S(1)} custom-call(bf16[64,1280]{1,0:T(8,128)(2,1)S(1)} %get-tuple-element.29.refs_0_, bf16[64,4352]{1,0:T(8,128)(2,1)S(1)} %get-tuple-element.30.refs_1_, bf16[64,1280]{1,0:T(8,128)(2,1)S(1)} %get-tuple-element.31.refs_2_, bf16[64,1280]{1,0:T(8,128)(2,1)S(1)} %get-tuple-element.32.refs_3_, ...), custom_call_target="tpu_custom_call" | custom-call | tf_op jit(solution)/shard_map/pallas_call | solution.py:314
  34.2 0.6 %collective-permute-done.12.refs_3_ = bf16[32,1024]{1,0:T(8,128)(2,1)S(1)} collective-permute-done((bf16[32,1024]{1,0:T(8,128)(2,1)S(1)}, bf16[32,1024]{1,0:T(8,128)(2,1)S(1)}, u32[]{:S(2)}, u32[]{:S(2)}) %collective-permute-start.12) | collective-permute-done | bytes 65568 | tf_op jit(solution)/shard_map/ppermute | solution.py:248
  34.8 0.4 collective-permute-done.13.refs_5_
  35.2 0.5 %collective-permute-done.14.refs_6_ = bf16[32,1024]{1,0:T(8,128)(2,1)S(1)} collective-permute-done((bf16[32,1024]{1,0:T(8,128)(2,1)S(1)}, bf16[32,1024]{1,0:T(8,128)(2,1)S(1)}, u32[]{:S(2)}, u32[]{:S(2)}) %collective-permute-start.14) | collective-permute-done | bytes 65568 | tf_op jit(solution)/shard_map/ppermute | solution.py:248
  35.8 0.7 %shard_map.58.refs_0_ = f32[32,128]{1,0:T(8,128)S(1)} custom-call(bf16[32,256,128]{2,1,0:T(8,128)(2,1)S(1)} %shard_map.57.g_ref, bf16[32,1024]{1,0:T(8,128)(2,1)S(1)} %collective-permute-done.5.refs_0_, bf16[32,1024]{1,0:T(8,128)(2,1)S(1)} %collective-permute-done.7.refs_1_, bf16[32,1024]{1,0:T(8,128)(2,1)S(1)} %collective-permute-done.6.refs_2_, ...), custom_call_target="tpu_custom_call" | custom-call | tf_op jit(solution)/shard_map/pallas_call | solution.py:323
  36.4 1.0 %collective-permute-start.15 = (f32[32,128]{1,0:T(8,128)S(1)}, f32[32,128]{1,0:T(8,128)S(1)}, u32[]{:S(2)}, u32[]{:S(2)}) collective-permute-start(f32[32,128]{1,0:T(8,128)S(1)} %shard_map.58.refs_0_), channel_id=1, source_target_pairs={{0,1},{1,0},{2,3},{3,2},{4,5},{5,4},{6,7},{7,6},{8,9},{9,8},{10,11... | collective-permute-start | bytes 49160 | tf_op jit(solution)/shard_map/ppermute | solution.py:248
  37.5 2.7 %collective-permute-done.15.refs_1_ = f32[32,128]{1,0:T(8,128)S(1)} collective-permute-done((f32[32,128]{1,0:T(8,128)S(1)}, f32[32,128]{1,0:T(8,128)S(1)}, u32[]{:S(2)}, u32[]{:S(2)}) %collective-permute-start.15) | collective-permute-done | bytes 16416 | tf_op jit(solution)/shard_map/ppermute | solution.py:248
  40.2 1.5 %collective-permute-start.18 = (f32[32,128]{1,0:T(8,128)S(1)}, f32[32,128]{1,0:T(8,128)S(1)}, u32[]{:S(2)}, u32[]{:S(2)}) collective-permute-start(f32[32,128]{1,0:T(8,128)S(1)} %shard_map.59), channel_id=1, source_target_pairs={{0,6},{1,7},{2,4},{3,5},{4,2},{5,3},{6,0},{7,1},{8,14},{9,15},{10,... | collective-permute-start | bytes 49160 | tf_op jit(solution)/shard_map/ppermute | solution.py:248
  41.7 0.9 %collective-permute-start.17 = (f32[32,128]{1,0:T(8,128)S(1)}, f32[32,128]{1,0:T(8,128)S(1)}, u32[]{:S(2)}, u32[]{:S(2)}) collective-permute-start(f32[32,128]{1,0:T(8,128)S(1)} %shard_map.59), channel_id=1, source_target_pairs={{0,4},{1,5},{2,6},{3,7},{4,0},{5,1},{6,2},{7,3},{8,12},{9,13},{10,... | collective-permute-start | bytes 49160 | tf_op jit(solution)/shard_map/ppermute | solution.py:248
  42.5 2.0 %collective-permute-start.16 = (f32[32,128]{1,0:T(8,128)S(1)}, f32[32,128]{1,0:T(8,128)S(1)}, u32[]{:S(2)}, u32[]{:S(2)}) collective-permute-start(f32[32,128]{1,0:T(8,128)S(1)} %shard_map.59), channel_id=1, source_target_pairs={{0,2},{1,3},{2,0},{3,1},{4,6},{5,7},{6,4},{7,5},{8,10},{9,11},{10,... | collective-permute-start | bytes 49160 | tf_op jit(solution)/shard_map/ppermute | solution.py:248
  44.6 1.1 %collective-permute-done.18 = f32[32,128]{1,0:T(8,128)S(1)} collective-permute-done((f32[32,128]{1,0:T(8,128)S(1)}, f32[32,128]{1,0:T(8,128)S(1)}, u32[]{:S(2)}, u32[]{:S(2)}) %collective-permute-start.18) | collective-permute-done | bytes 16416 | tf_op jit(solution)/shard_map/ppermute | solution.py:248
  45.7 0.7 %collective-permute-done.17 = f32[32,128]{1,0:T(8,128)S(1)} collective-permute-done((f32[32,128]{1,0:T(8,128)S(1)}, f32[32,128]{1,0:T(8,128)S(1)}, u32[]{:S(2)}, u32[]{:S(2)}) %collective-permute-start.17) | collective-permute-done | bytes 16416 | tf_op jit(solution)/shard_map/ppermute | solution.py:248
  46.5 0.6 %add_add_fusion = f32[32,128]{1,0:T(8,128)} fusion(f32[32,128]{1,0:T(8,128)S(1)} %collective-permute-done.18, f32[32,128]{1,0:T(8,128)S(1)} %collective-permute-done.17, f32[32,128]{1,0:T(8,128)S(1)} %shard_map.59, f32[32,128]{1,0:T(8,128)S(1)} %collective-permute-done.16), kind=kLoop, calls=%fused_computation | loop fusion | flops 12288 | bytes 81920 | tf_op jit(solution)/shard_map/add | solution.py:341
  (12 shorter events, 0.1 us)
Async XLA Ops:
  1.9 11.1 %collective-permute-start = (bf16[64,4352]{1,0:T(8,128)(2,1)S(1)}, bf16[64,4352]{1,0:T(8,128)(2,1)S(1)}, u32[]{:S(2)}, u32[]{:S(2)}) collective-permute-start(bf16[64,4352]{1,0:T(8,128)(2,1)S(1)} %get-tuple-element.30.refs_1_), channel_id=1, source_target_pairs={{0,8},{1,9},{2,10},{3,11},{4,12},{5,13},{6,14},{7,15},{8,0},{9,1},... | collective-permute-start | bytes 1671176 | tf_op jit(solution)/shard_map/ppermute | solution.py:248
  2.4 9.3 %collective-permute-start.1 = (bf16[64,1280]{1,0:T(8,128)(2,1)S(1)}, bf16[64,1280]{1,0:T(8,128)(2,1)S(1)}, u32[]{:S(2)}, u32[]{:S(2)}) collective-permute-start(bf16[64,1280]{1,0:T(8,128)(2,1)S(1)} %get-tuple-element.31.refs_2_), channel_id=1, source_target_pairs={{0,16},{1,17},{2,18},{3,19},{4,20},{5,21},{6,22},{7,23},{8,24},{9,... | collective-permute-start | bytes 491528 | tf_op jit(solution)/shard_map/ppermute | solution.py:248
  5.0 8.0 %collective-permute-start.2 = (bf16[64,1280]{1,0:T(8,128)(2,1)S(1)}, bf16[64,1280]{1,0:T(8,128)(2,1)S(1)}, u32[]{:S(2)}, u32[]{:S(2)}) collective-permute-start(bf16[64,1280]{1,0:T(8,128)(2,1)S(1)} %get-tuple-element.32.refs_3_), channel_id=1, source_target_pairs={{0,24},{1,25},{2,26},{3,27},{4,28},{5,29},{6,30},{7,31},{8,16},{9,... | collective-permute-start | bytes 491528 | tf_op jit(solution)/shard_map/ppermute | solution.py:248
  5.1 4.6 %collective-permute-start.4 = (bf16[32,256]{1,0:T(8,128)(2,1)S(1)}, bf16[32,256]{1,0:T(8,128)(2,1)S(1)}, u32[]{:S(2)}, u32[]{:S(2)}) collective-permute-start(bf16[32,256]{1,0:T(8,128)(2,1)S(1)} %get-tuple-element.33.own_virt), channel_id=1, source_target_pairs={{0,4},{1,5},{2,6},{3,7},{4,0},{5,1},{6,2},{7,3},{8,13},{9,12},{10,... | collective-permute-start | bytes 49160 | tf_op jit(solution)/shard_map/ppermute | solution.py:255
  7.9 3.9 %collective-permute-start.3 = (bf16[32,256]{1,0:T(8,128)(2,1)S(1)}, bf16[32,256]{1,0:T(8,128)(2,1)S(1)}, u32[]{:S(2)}, u32[]{:S(2)}) collective-permute-start(bf16[32,256]{1,0:T(8,128)(2,1)S(1)} %get-tuple-element.33.own_virt), channel_id=1, source_target_pairs={{0,1},{1,0},{2,3},{3,2},{4,5},{5,4},{6,7},{7,6},{8,9},{9,8},{10,11... | collective-permute-start | bytes 49160 | tf_op jit(solution)/shard_map/ppermute | solution.py:255
  13.4 14.5 %collective-permute-start.9 = (bf16[64,2304]{1,0:T(8,128)(2,1)S(1)}, bf16[64,2304]{1,0:T(8,128)(2,1)S(1)}, u32[]{:S(2)}, u32[]{:S(2)}) collective-permute-start(bf16[64,2304]{1,0:T(8,128)(2,1)S(1)} %get-tuple-element.38), channel_id=1, source_target_pairs={{0,16},{1,17},{2,18},{3,19},{4,20},{5,21},{6,22},{7,23},{8,24},{9,... | collective-permute-start | bytes 884744 | tf_op jit(solution)/shard_map/ppermute | solution.py:248
  15.0 8.9 %collective-permute-start.5 = (bf16[32,1024]{1,0:T(8,128)(2,1)S(1)}, bf16[32,1024]{1,0:T(8,128)(2,1)S(1)}, u32[]{:S(2)}, u32[]{:S(2)}) collective-permute-start(bf16[32,1024]{1,0:T(8,128)(2,1)S(1)} %get-tuple-element.34), channel_id=1, source_target_pairs={{0,7},{1,6},{2,5},{3,4},{4,3},{5,2},{6,1},{7,0},{8,15},{9,14},{10,... | collective-permute-start | bytes 196616 | tf_op jit(solution)/shard_map/ppermute | solution.py:248
  19.6 7.8 %collective-permute-start.6 = (bf16[32,1024]{1,0:T(8,128)(2,1)S(1)}, bf16[32,1024]{1,0:T(8,128)(2,1)S(1)}, u32[]{:S(2)}, u32[]{:S(2)}) collective-permute-start(bf16[32,1024]{1,0:T(8,128)(2,1)S(1)} %get-tuple-element.35), channel_id=1, source_target_pairs={{0,5},{1,4},{2,7},{3,6},{4,1},{5,0},{6,3},{7,2},{8,13},{9,12},{10,... | collective-permute-start | bytes 196616 | tf_op jit(solution)/shard_map/ppermute | solution.py:248
  19.6 7.8 %collective-permute-start.7 = (bf16[32,1024]{1,0:T(8,128)(2,1)S(1)}, bf16[32,1024]{1,0:T(8,128)(2,1)S(1)}, u32[]{:S(2)}, u32[]{:S(2)}) collective-permute-start(bf16[32,1024]{1,0:T(8,128)(2,1)S(1)} %get-tuple-element.36), channel_id=1, source_target_pairs={{0,6},{1,7},{2,4},{3,5},{4,2},{5,3},{6,0},{7,1},{8,14},{9,15},{10,... | collective-permute-start | bytes 196616 | tf_op jit(solution)/shard_map/ppermute | solution.py:248
  21.4 6.5 %collective-permute-start.8 = (bf16[32,1024]{1,0:T(8,128)(2,1)S(1)}, bf16[32,1024]{1,0:T(8,128)(2,1)S(1)}, u32[]{:S(2)}, u32[]{:S(2)}) collective-permute-start(bf16[32,1024]{1,0:T(8,128)(2,1)S(1)} %get-tuple-element.37), channel_id=1, source_target_pairs={{0,3},{1,2},{2,1},{3,0},{4,7},{5,6},{6,5},{7,4},{8,11},{9,10},{10,... | collective-permute-start | bytes 196616 | tf_op jit(solution)/shard_map/ppermute | solution.py:248
  27.9 4.6 %collective-permute-start.11 = (bf16[64,2304]{1,0:T(8,128)(2,1)S(1)}, bf16[64,2304]{1,0:T(8,128)(2,1)S(1)}, u32[]{:S(2)}, u32[]{:S(2)}) collective-permute-start(bf16[64,2304]{1,0:T(8,128)(2,1)S(1)} %get-tuple-element.44.refs_10_), channel_id=1, source_target_pairs={{0,8},{1,9},{2,10},{3,11},{4,12},{5,13},{6,14},{7,15},{8,0},{9,1},... | collective-permute-start | bytes 884744 | tf_op jit(solution)/shard_map/ppermute | solution.py:248
  27.9 4.6 %collective-permute-start.10 = (bf16[64,2304]{1,0:T(8,128)(2,1)S(1)}, bf16[64,2304]{1,0:T(8,128)(2,1)S(1)}, u32[]{:S(2)}, u32[]{:S(2)}) collective-permute-start(bf16[64,2304]{1,0:T(8,128)(2,1)S(1)} %collective-permute-done.9.refs_7_), channel_id=1, source_target_pairs={{0,8},{1,9},{2,10},{3,11},{4,12},{5,13},{6,14},{7,15},{8,0},{9,1},... | collective-permute-start | bytes 884744 | tf_op jit(solution)/shard_map/ppermute | solution.py:248
  28.4 6.3 %collective-permute-start.12 = (bf16[32,1024]{1,0:T(8,128)(2,1)S(1)}, bf16[32,1024]{1,0:T(8,128)(2,1)S(1)}, u32[]{:S(2)}, u32[]{:S(2)}) collective-permute-start(bf16[32,1024]{1,0:T(8,128)(2,1)S(1)} %get-tuple-element.48), channel_id=1, source_target_pairs={{0,4},{1,5},{2,6},{3,7},{4,0},{5,1},{6,2},{7,3},{8,12},{9,13},{10,... | collective-permute-start | bytes 196616 | tf_op jit(solution)/shard_map/ppermute | solution.py:248
  30.4 4.9 %collective-permute-start.13 = (bf16[32,1024]{1,0:T(8,128)(2,1)S(1)}, bf16[32,1024]{1,0:T(8,128)(2,1)S(1)}, u32[]{:S(2)}, u32[]{:S(2)}) collective-permute-start(bf16[32,1024]{1,0:T(8,128)(2,1)S(1)} %get-tuple-element.50), channel_id=1, source_target_pairs={{0,2},{1,3},{2,0},{3,1},{4,6},{5,7},{6,4},{7,5},{8,10},{9,11},{10,... | collective-permute-start | bytes 196616 | tf_op jit(solution)/shard_map/ppermute | solution.py:248
  31.5 4.3 %collective-permute-start.14 = (bf16[32,1024]{1,0:T(8,128)(2,1)S(1)}, bf16[32,1024]{1,0:T(8,128)(2,1)S(1)}, u32[]{:S(2)}, u32[]{:S(2)}) collective-permute-start(bf16[32,1024]{1,0:T(8,128)(2,1)S(1)} %get-tuple-element.51), channel_id=1, source_target_pairs={{0,1},{1,0},{2,3},{3,2},{4,5},{5,4},{6,7},{7,6},{8,9},{9,8},{10,11... | collective-permute-start | bytes 196616 | tf_op jit(solution)/shard_map/ppermute | solution.py:248
  36.4 3.8 %collective-permute-start.15 = (f32[32,128]{1,0:T(8,128)S(1)}, f32[32,128]{1,0:T(8,128)S(1)}, u32[]{:S(2)}, u32[]{:S(2)}) collective-permute-start(f32[32,128]{1,0:T(8,128)S(1)} %shard_map.58.refs_0_), channel_id=1, source_target_pairs={{0,1},{1,0},{2,3},{3,2},{4,5},{5,4},{6,7},{7,6},{8,9},{9,8},{10,11... | collective-permute-start | bytes 49160 | tf_op jit(solution)/shard_map/ppermute | solution.py:248
  40.2 5.5 %collective-permute-start.18 = (f32[32,128]{1,0:T(8,128)S(1)}, f32[32,128]{1,0:T(8,128)S(1)}, u32[]{:S(2)}, u32[]{:S(2)}) collective-permute-start(f32[32,128]{1,0:T(8,128)S(1)} %shard_map.59), channel_id=1, source_target_pairs={{0,6},{1,7},{2,4},{3,5},{4,2},{5,3},{6,0},{7,1},{8,14},{9,15},{10,... | collective-permute-start | bytes 49160 | tf_op jit(solution)/shard_map/ppermute | solution.py:248
  41.7 4.7 %collective-permute-start.17 = (f32[32,128]{1,0:T(8,128)S(1)}, f32[32,128]{1,0:T(8,128)S(1)}, u32[]{:S(2)}, u32[]{:S(2)}) collective-permute-start(f32[32,128]{1,0:T(8,128)S(1)} %shard_map.59), channel_id=1, source_target_pairs={{0,4},{1,5},{2,6},{3,7},{4,0},{5,1},{6,2},{7,3},{8,12},{9,13},{10,... | collective-permute-start | bytes 49160 | tf_op jit(solution)/shard_map/ppermute | solution.py:248
  42.5 3.9 %collective-permute-start.16 = (f32[32,128]{1,0:T(8,128)S(1)}, f32[32,128]{1,0:T(8,128)S(1)}, u32[]{:S(2)}, u32[]{:S(2)}) collective-permute-start(f32[32,128]{1,0:T(8,128)S(1)} %shard_map.59), channel_id=1, source_target_pairs={{0,2},{1,3},{2,0},{3,1},{4,6},{5,7},{6,4},{7,5},{8,10},{9,11},{10,... | collective-permute-start | bytes 49160 | tf_op jit(solution)/shard_map/ppermute | solution.py:248

commit v8 on v7

--- a/solution.py
+++ b/solution.py
@@ -8,6 +8,7 @@
 from jax.sharding import PartitionSpec as P
 
 VMEM_LIMIT = 40 * 1024 * 1024
+CHUNKS, HALVES = 2, 2
 BF16 = jnp.bfloat16
 F32 = jnp.float32
 
@@ -72,9 +73,10 @@
 
 def pack_kernel(n_split, occ_mask_hbm, virt_mask_hbm, b_hbm, occ_hbm, virt_hbm, virt_ref, *rest):
     outs, (occ_mask, virt_mask, b, occ_green, virt_green, sems) = rest[:n_split], rest[n_split:]
-    pairs = (
-        (b_hbm, b), (occ_hbm, occ_green), (virt_hbm, virt_green), (occ_mask_hbm, occ_mask), (virt_mask_hbm, virt_mask)
-    )
+    step = b.shape[0] // CHUNKS
+    bands = [slice(i * step, (i + 1) * step) for i in range(CHUNKS)]
+    pairs = [(occ_hbm, occ_green), (virt_hbm, virt_green), (occ_mask_hbm, occ_mask), (virt_mask_hbm, virt_mask)]
+    pairs += [(b_hbm.at[band], b.at[band]) for band in bands]
     copies = [pltpu.make_async_copy(src, dst, sems.at[i]) for i, (src, dst) in enumerate(pairs)]
     for copy in copies:
         copy.start()
@@ -82,7 +84,7 @@
     rows, cols, naux = b.shape
     group = cols // n_split
     block = occ_green.shape[1] // occ_mask.shape[0]
-    for copy in copies[1:]:
+    for copy in copies[:4]:
         copy.wait()
     virt = screened(virt_green[...], virt_mask, t * (cols // block), block)
     virt_ref[...] = virt.astype(BF16)
@@ -91,16 +93,21 @@
     width = group * naux + occ.shape[1]
     for m in range(n_split):
         outs[m][:, group * naux:width] = occ
-    copies[0].wait()
-    basis = jnp.swapaxes(b[...], 0, 1)
-    for l in range(group):
-        tiles = swap_lane_blocks([basis[j * group + l] for j in range(n_split)], naux // n_split)
-        tiles = xor_list(tiles, s)
-        for m in range(n_split):
-            outs[m][:, l * naux:(l + 1) * naux] = tiles[m]
-            if m != 1:
-                start = width + near_place(n_split, m) * group * naux + l * naux
-                outs[1][:, start:start + naux] = tiles[m]
+    half = rows // HALVES
+    for first in range(0, rows, half):
+        for i, copy in enumerate(copies[4:]):
+            if first <= i * step < first + half:
+                copy.wait()
+        band = slice(first, first + half)
+        basis = jnp.swapaxes(b[band], 0, 1)
+        for l in range(group):
+            tiles = swap_lane_blocks([basis[j * group + l] for j in range(n_split)], naux // n_split)
+            tiles = xor_list(tiles, s)
+            for m in range(n_split):
+                outs[m][band, l * naux:(l + 1) * naux] = tiles[m]
+                if m != 1:
+                    start = width + near_place(n_split, m) * group * naux + l * naux
+                    outs[1][band, start:start + naux] = tiles[m]
 
 
 def add_kernel(*refs):
@@ -270,7 +277,7 @@
             pltpu.VMEM(three_centre.shape, BF16),
             pltpu.VMEM(green_occ.shape, BF16),
             pltpu.VMEM(green_virt.shape, BF16),
-            pltpu.SemaphoreType.DMA((5,)),
+            pltpu.SemaphoreType.DMA((4 + CHUNKS,)),
         ],
         compiler_params=params,
     )(*[pltpu.with_memory_space_constraint(x, pltpu.HBM) for x in arguments])

time: 47.2 us -> 47.1 us (level)
  transfers between devices with their start and end apart: 19 -> 19, of which waited for: 11 -> 11; matrix products, arithmetic and copies ran while one was open for 0% -> 0% of each run, Pallas kernels for 3% -> 4%
where the time goes in v8:
time: 47.1 us; the launch traced here: 47 us
  starting transfers between devices  28.1 us (60%)
  waiting for transfers between devices  13.8 us (29%)
  Pallas kernels  4.42 us (9%)
  other arithmetic  0.61 us (1%)
    ppermute x17, starting transfers between devices, exchange(): lax.ppermute(x, ('split', 'tensor'), [(d, d ^ bits) for d in range(count)])  23.7 us
    ppermute x17, waiting for transfers between devices, exchange(): lax.ppermute(x, ('split', 'tensor'), [(d, d ^ bits) for d in range(count)])  11.5 us
    ppermute x2, starting transfers between devices, fetch(): return lax.ppermute(x, ('split', 'tensor'), pairs)  4.34 us
    ppermute x2, waiting for transfers between devices, fetch(): return lax.ppermute(x, ('split', 'tensor'), pairs)  2.34 us
    pallas_call x1, Pallas kernels, local(): pl.pallas_call(functools.partial(pack_kernel, n_split), out_shape=[jax.Sh...  1.77 us
    pallas_call x1, Pallas kernels, local(): pl.pallas_call(functools.partial(g_kernel, n_split, n_tensor, packed_widt...  1.65 us
  transfers between devices with their start and end apart: 19, of which 11 were waited for; matrix products, arithmetic and copies ran while one was open for 0% of the time, Pallas kernels for 4%

profile of v8, /device:TPU:0, one launch (start us, length us, event | category | flops | bytes accessed | tf_op | source)
XLA Modules:
  0.0 47.0 jit_solution(7318619630836911468)
XLA Ops:
  0.0 1.8 %shard_map.55 = (bf16[32,256]{1,0:T(8,128)(2,1)S(1)}, bf16[64,1280]{1,0:T(8,128)(2,1)S(1)}, bf16[64,4352]{1,0:T(8,128)(2,1)S(1)}, bf16[64,1280]{1,0:T(8,128)(2,1)S(1)}, bf16[64,1280]{1,0:T(8,128)(2,1)S(1)}) custom-call(s32[8,8]{1,0:T(8,128)} %occ_mask_hbm.1, s32[8,8]{1,0:T(8,128)} %virt_mask_hbm.1, bf16[64,32,128]{2,1,0:T(8,128)(2,1)} %b_hbm.1, ...), custom_call_target="tpu_custom_call" | custom-call | tf_op jit(solution)/shard_map/pallas_call | solution.py:265
  1.8 0.5 %collective-permute-start = (bf16[64,4352]{1,0:T(8,128)(2,1)S(1)}, bf16[64,4352]{1,0:T(8,128)(2,1)S(1)}, u32[]{:S(2)}, u32[]{:S(2)}) collective-permute-start(bf16[64,4352]{1,0:T(8,128)(2,1)S(1)} %get-tuple-element.30.refs_1_), channel_id=1, source_target_pairs={{0,8},{1,9},{2,10},{3,11},{4,12},{5,13},{6,14},{7,15},{8,0},{9,1},... | collective-permute-start | bytes 1671176 | tf_op jit(solution)/shard_map/ppermute | solution.py:255
  2.3 2.6 %collective-permute-start.1 = (bf16[64,1280]{1,0:T(8,128)(2,1)S(1)}, bf16[64,1280]{1,0:T(8,128)(2,1)S(1)}, u32[]{:S(2)}, u32[]{:S(2)}) collective-permute-start(bf16[64,1280]{1,0:T(8,128)(2,1)S(1)} %get-tuple-element.31.refs_2_), channel_id=1, source_target_pairs={{0,16},{1,17},{2,18},{3,19},{4,20},{5,21},{6,22},{7,23},{8,24},{9,... | collective-permute-start | bytes 491528 | tf_op jit(solution)/shard_map/ppermute | solution.py:255
  4.9 2.8 %collective-permute-start.4 = (bf16[32,256]{1,0:T(8,128)(2,1)S(1)}, bf16[32,256]{1,0:T(8,128)(2,1)S(1)}, u32[]{:S(2)}, u32[]{:S(2)}) collective-permute-start(bf16[32,256]{1,0:T(8,128)(2,1)S(1)} %get-tuple-element.33.own_virt), channel_id=1, source_target_pairs={{0,4},{1,5},{2,6},{3,7},{4,0},{5,1},{6,2},{7,3},{8,13},{9,12},{10,... | collective-permute-start | bytes 49160 | tf_op jit(solution)/shard_map/ppermute | solution.py:262
  7.8 1.5 %collective-permute-start.3 = (bf16[32,256]{1,0:T(8,128)(2,1)S(1)}, bf16[32,256]{1,0:T(8,128)(2,1)S(1)}, u32[]{:S(2)}, u32[]{:S(2)}) collective-permute-start(bf16[32,256]{1,0:T(8,128)(2,1)S(1)} %get-tuple-element.33.own_virt), channel_id=1, source_target_pairs={{0,1},{1,0},{2,3},{3,2},{4,5},{5,4},{6,7},{7,6},{8,9},{9,8},{10,11... | collective-permute-start | bytes 49160 | tf_op jit(solution)/shard_map/ppermute | solution.py:262
  9.3 0.3 collective-permute-done.4.refs_8_
  9.6 2.0 %collective-permute-done.3.refs_7_ = bf16[32,256]{1,0:T(8,128)(2,1)S(1)} collective-permute-done((bf16[32,256]{1,0:T(8,128)(2,1)S(1)}, bf16[32,256]{1,0:T(8,128)(2,1)S(1)}, u32[]{:S(2)}, u32[]{:S(2)}) %collective-permute-start.3) | collective-permute-done | bytes 16416 | tf_op jit(solution)/shard_map/ppermute | solution.py:262
  11.6 1.3 %collective-permute-done.2.refs_4_.refs_6_ = bf16[64,1280]{1,0:T(8,128)(2,1)S(1)} collective-permute-done((bf16[64,1280]{1,0:T(8,128)(2,1)S(1)}, bf16[64,1280]{1,0:T(8,128)(2,1)S(1)}, u32[]{:S(2)}, u32[]{:S(2)}) %collective-permute-start.2) | collective-permute-done | bytes 163872 | tf_op jit(solution)/shard_map/ppermute | solution.py:255
  12.9 0.3 shard_map.56
  13.2 1.6 %collective-permute-start.9 = (bf16[64,2304]{1,0:T(8,128)(2,1)S(1)}, bf16[64,2304]{1,0:T(8,128)(2,1)S(1)}, u32[]{:S(2)}, u32[]{:S(2)}) collective-permute-start(bf16[64,2304]{1,0:T(8,128)(2,1)S(1)} %get-tuple-element.38), channel_id=1, source_target_pairs={{0,16},{1,17},{2,18},{3,19},{4,20},{5,21},{6,22},{7,23},{8,24},{9,... | collective-permute-start | bytes 884744 | tf_op jit(solution)/shard_map/ppermute | solution.py:255
  14.9 4.6 %collective-permute-start.5 = (bf16[32,1024]{1,0:T(8,128)(2,1)S(1)}, bf16[32,1024]{1,0:T(8,128)(2,1)S(1)}, u32[]{:S(2)}, u32[]{:S(2)}) collective-permute-start(bf16[32,1024]{1,0:T(8,128)(2,1)S(1)} %get-tuple-element.34), channel_id=1, source_target_pairs={{0,7},{1,6},{2,5},{3,4},{4,3},{5,2},{6,1},{7,0},{8,15},{9,14},{10,... | collective-permute-start | bytes 196616 | tf_op jit(solution)/shard_map/ppermute | solution.py:255
  19.4 1.9 %collective-permute-start.7 = (bf16[32,1024]{1,0:T(8,128)(2,1)S(1)}, bf16[32,1024]{1,0:T(8,128)(2,1)S(1)}, u32[]{:S(2)}, u32[]{:S(2)}) collective-permute-start(bf16[32,1024]{1,0:T(8,128)(2,1)S(1)} %get-tuple-element.36), channel_id=1, source_target_pairs={{0,6},{1,7},{2,4},{3,5},{4,2},{5,3},{6,0},{7,1},{8,14},{9,15},{10,... | collective-permute-start | bytes 196616 | tf_op jit(solution)/shard_map/ppermute | solution.py:255
  21.3 2.5 %collective-permute-start.8 = (bf16[32,1024]{1,0:T(8,128)(2,1)S(1)}, bf16[32,1024]{1,0:T(8,128)(2,1)S(1)}, u32[]{:S(2)}, u32[]{:S(2)}) collective-permute-start(bf16[32,1024]{1,0:T(8,128)(2,1)S(1)} %get-tuple-element.37), channel_id=1, source_target_pairs={{0,3},{1,2},{2,1},{3,0},{4,7},{5,6},{6,5},{7,4},{8,11},{9,10},{10,... | collective-permute-start | bytes 196616 | tf_op jit(solution)/shard_map/ppermute | solution.py:255
  23.8 3.4 %collective-permute-done.6.refs_2_ = bf16[32,1024]{1,0:T(8,128)(2,1)S(1)} collective-permute-done((bf16[32,1024]{1,0:T(8,128)(2,1)S(1)}, bf16[32,1024]{1,0:T(8,128)(2,1)S(1)}, u32[]{:S(2)}, u32[]{:S(2)}) %collective-permute-start.6) | collective-permute-done | bytes 65568 | tf_op jit(solution)/shard_map/ppermute | solution.py:255
  27.2 0.6 %collective-permute-done.8.refs_4_ = bf16[32,1024]{1,0:T(8,128)(2,1)S(1)} collective-permute-done((bf16[32,1024]{1,0:T(8,128)(2,1)S(1)}, bf16[32,1024]{1,0:T(8,128)(2,1)S(1)}, u32[]{:S(2)}, u32[]{:S(2)}) %collective-permute-start.8) | collective-permute-done | bytes 65568 | tf_op jit(solution)/shard_map/ppermute | solution.py:255
  27.8 0.5 %collective-permute-start.10 = (bf16[64,2304]{1,0:T(8,128)(2,1)S(1)}, bf16[64,2304]{1,0:T(8,128)(2,1)S(1)}, u32[]{:S(2)}, u32[]{:S(2)}) collective-permute-start(bf16[64,2304]{1,0:T(8,128)(2,1)S(1)} %collective-permute-done.9.refs_7_), channel_id=1, source_target_pairs={{0,8},{1,9},{2,10},{3,11},{4,12},{5,13},{6,14},{7,15},{8,0},{9,1},... | collective-permute-start | bytes 884744 | tf_op jit(solution)/shard_map/ppermute | solution.py:255
  28.3 1.9 %collective-permute-start.12 = (bf16[32,1024]{1,0:T(8,128)(2,1)S(1)}, bf16[32,1024]{1,0:T(8,128)(2,1)S(1)}, u32[]{:S(2)}, u32[]{:S(2)}) collective-permute-start(bf16[32,1024]{1,0:T(8,128)(2,1)S(1)} %get-tuple-element.48), channel_id=1, source_target_pairs={{0,4},{1,5},{2,6},{3,7},{4,0},{5,1},{6,2},{7,3},{8,12},{9,13},{10,... | collective-permute-start | bytes 196616 | tf_op jit(solution)/shard_map/ppermute | solution.py:255
  30.2 1.1 %collective-permute-start.13 = (bf16[32,1024]{1,0:T(8,128)(2,1)S(1)}, bf16[32,1024]{1,0:T(8,128)(2,1)S(1)}, u32[]{:S(2)}, u32[]{:S(2)}) collective-permute-start(bf16[32,1024]{1,0:T(8,128)(2,1)S(1)} %get-tuple-element.50), channel_id=1, source_target_pairs={{0,2},{1,3},{2,0},{3,1},{4,6},{5,7},{6,4},{7,5},{8,10},{9,11},{10,... | collective-permute-start | bytes 196616 | tf_op jit(solution)/shard_map/ppermute | solution.py:255
  31.4 1.0 %collective-permute-start.14 = (bf16[32,1024]{1,0:T(8,128)(2,1)S(1)}, bf16[32,1024]{1,0:T(8,128)(2,1)S(1)}, u32[]{:S(2)}, u32[]{:S(2)}) collective-permute-start(bf16[32,1024]{1,0:T(8,128)(2,1)S(1)} %get-tuple-element.51), channel_id=1, source_target_pairs={{0,1},{1,0},{2,3},{3,2},{4,5},{5,4},{6,7},{7,6},{8,9},{9,8},{10,11... | collective-permute-start | bytes 196616 | tf_op jit(solution)/shard_map/ppermute | solution.py:255
  32.4 1.6 %shard_map.57.g_ref = bf16[32,256,128]{2,1,0:T(8,128)(2,1)S(1)} custom-call(bf16[64,1280]{1,0:T(8,128)(2,1)S(1)} %get-tuple-element.29.refs_0_, bf16[64,4352]{1,0:T(8,128)(2,1)S(1)} %get-tuple-element.30.refs_1_, bf16[64,1280]{1,0:T(8,128)(2,1)S(1)} %get-tuple-element.31.refs_2_, bf16[64,1280]{1,0:T(8,128)(2,1)S(1)} %get-tuple-element.32.refs_3_, ...), custom_call_target="tpu_custom_call" | custom-call | tf_op jit(solution)/shard_map/pallas_call | solution.py:321
  34.0 0.6 %collective-permute-done.12.refs_3_ = bf16[32,1024]{1,0:T(8,128)(2,1)S(1)} collective-permute-done((bf16[32,1024]{1,0:T(8,128)(2,1)S(1)}, bf16[32,1024]{1,0:T(8,128)(2,1)S(1)}, u32[]{:S(2)}, u32[]{:S(2)}) %collective-permute-start.12) | collective-permute-done | bytes 65568 | tf_op jit(solution)/shard_map/ppermute | solution.py:255
  34.6 0.4 collective-permute-done.13.refs_5_
  35.1 0.6 %collective-permute-done.14.refs_6_ = bf16[32,1024]{1,0:T(8,128)(2,1)S(1)} collective-permute-done((bf16[32,1024]{1,0:T(8,128)(2,1)S(1)}, bf16[32,1024]{1,0:T(8,128)(2,1)S(1)}, u32[]{:S(2)}, u32[]{:S(2)}) %collective-permute-start.14) | collective-permute-done | bytes 65568 | tf_op jit(solution)/shard_map/ppermute | solution.py:255
  35.6 0.7 %shard_map.58.refs_0_ = f32[32,128]{1,0:T(8,128)S(1)} custom-call(bf16[32,256,128]{2,1,0:T(8,128)(2,1)S(1)} %shard_map.57.g_ref, bf16[32,1024]{1,0:T(8,128)(2,1)S(1)} %collective-permute-done.5.refs_0_, bf16[32,1024]{1,0:T(8,128)(2,1)S(1)} %collective-permute-done.7.refs_1_, bf16[32,1024]{1,0:T(8,128)(2,1)S(1)} %collective-permute-done.6.refs_2_, ...), custom_call_target="tpu_custom_call" | custom-call | tf_op jit(solution)/shard_map/pallas_call | solution.py:330
  36.3 1.0 %collective-permute-start.15 = (f32[32,128]{1,0:T(8,128)S(1)}, f32[32,128]{1,0:T(8,128)S(1)}, u32[]{:S(2)}, u32[]{:S(2)}) collective-permute-start(f32[32,128]{1,0:T(8,128)S(1)} %shard_map.58.refs_0_), channel_id=1, source_target_pairs={{0,1},{1,0},{2,3},{3,2},{4,5},{5,4},{6,7},{7,6},{8,9},{9,8},{10,11... | collective-permute-start | bytes 49160 | tf_op jit(solution)/shard_map/ppermute | solution.py:255
  37.3 2.7 %collective-permute-done.15.refs_1_ = f32[32,128]{1,0:T(8,128)S(1)} collective-permute-done((f32[32,128]{1,0:T(8,128)S(1)}, f32[32,128]{1,0:T(8,128)S(1)}, u32[]{:S(2)}, u32[]{:S(2)}) %collective-permute-start.15) | collective-permute-done | bytes 16416 | tf_op jit(solution)/shard_map/ppermute | solution.py:255
  40.1 1.5 %collective-permute-start.18 = (f32[32,128]{1,0:T(8,128)S(1)}, f32[32,128]{1,0:T(8,128)S(1)}, u32[]{:S(2)}, u32[]{:S(2)}) collective-permute-start(f32[32,128]{1,0:T(8,128)S(1)} %shard_map.59), channel_id=1, source_target_pairs={{0,6},{1,7},{2,4},{3,5},{4,2},{5,3},{6,0},{7,1},{8,14},{9,15},{10,... | collective-permute-start | bytes 49160 | tf_op jit(solution)/shard_map/ppermute | solution.py:255
  41.5 0.8 %collective-permute-start.17 = (f32[32,128]{1,0:T(8,128)S(1)}, f32[32,128]{1,0:T(8,128)S(1)}, u32[]{:S(2)}, u32[]{:S(2)}) collective-permute-start(f32[32,128]{1,0:T(8,128)S(1)} %shard_map.59), channel_id=1, source_target_pairs={{0,4},{1,5},{2,6},{3,7},{4,0},{5,1},{6,2},{7,3},{8,12},{9,13},{10,... | collective-permute-start | bytes 49160 | tf_op jit(solution)/shard_map/ppermute | solution.py:255
  42.4 2.1 %collective-permute-start.16 = (f32[32,128]{1,0:T(8,128)S(1)}, f32[32,128]{1,0:T(8,128)S(1)}, u32[]{:S(2)}, u32[]{:S(2)}) collective-permute-start(f32[32,128]{1,0:T(8,128)S(1)} %shard_map.59), channel_id=1, source_target_pairs={{0,2},{1,3},{2,0},{3,1},{4,6},{5,7},{6,4},{7,5},{8,10},{9,11},{10,... | collective-permute-start | bytes 49160 | tf_op jit(solution)/shard_map/ppermute | solution.py:255
  44.4 1.1 %collective-permute-done.18 = f32[32,128]{1,0:T(8,128)S(1)} collective-permute-done((f32[32,128]{1,0:T(8,128)S(1)}, f32[32,128]{1,0:T(8,128)S(1)}, u32[]{:S(2)}, u32[]{:S(2)}) %collective-permute-start.18) | collective-permute-done | bytes 16416 | tf_op jit(solution)/shard_map/ppermute | solution.py:255
  45.6 0.7 %collective-permute-done.17 = f32[32,128]{1,0:T(8,128)S(1)} collective-permute-done((f32[32,128]{1,0:T(8,128)S(1)}, f32[32,128]{1,0:T(8,128)S(1)}, u32[]{:S(2)}, u32[]{:S(2)}) %collective-permute-start.17) | collective-permute-done | bytes 16416 | tf_op jit(solution)/shard_map/ppermute | solution.py:255
  46.3 0.6 %add_add_fusion = f32[32,128]{1,0:T(8,128)} fusion(f32[32,128]{1,0:T(8,128)S(1)} %collective-permute-done.18, f32[32,128]{1,0:T(8,128)S(1)} %collective-permute-done.17, f32[32,128]{1,0:T(8,128)S(1)} %shard_map.59, f32[32,128]{1,0:T(8,128)S(1)} %collective-permute-done.16), kind=kLoop, calls=%fused_computation | loop fusion | flops 12288 | bytes 81920 | tf_op jit(solution)/shard_map/add | solution.py:348
  (12 shorter events, 0.1 us)
Async XLA Ops:
  1.8 11.1 %collective-permute-start = (bf16[64,4352]{1,0:T(8,128)(2,1)S(1)}, bf16[64,4352]{1,0:T(8,128)(2,1)S(1)}, u32[]{:S(2)}, u32[]{:S(2)}) collective-permute-start(bf16[64,4352]{1,0:T(8,128)(2,1)S(1)} %get-tuple-element.30.refs_1_), channel_id=1, source_target_pairs={{0,8},{1,9},{2,10},{3,11},{4,12},{5,13},{6,14},{7,15},{8,0},{9,1},... | collective-permute-start | bytes 1671176 | tf_op jit(solution)/shard_map/ppermute | solution.py:255
  2.3 9.3 %collective-permute-start.1 = (bf16[64,1280]{1,0:T(8,128)(2,1)S(1)}, bf16[64,1280]{1,0:T(8,128)(2,1)S(1)}, u32[]{:S(2)}, u32[]{:S(2)}) collective-permute-start(bf16[64,1280]{1,0:T(8,128)(2,1)S(1)} %get-tuple-element.31.refs_2_), channel_id=1, source_target_pairs={{0,16},{1,17},{2,18},{3,19},{4,20},{5,21},{6,22},{7,23},{8,24},{9,... | collective-permute-start | bytes 491528 | tf_op jit(solution)/shard_map/ppermute | solution.py:255
  4.9 8.0 %collective-permute-start.2 = (bf16[64,1280]{1,0:T(8,128)(2,1)S(1)}, bf16[64,1280]{1,0:T(8,128)(2,1)S(1)}, u32[]{:S(2)}, u32[]{:S(2)}) collective-permute-start(bf16[64,1280]{1,0:T(8,128)(2,1)S(1)} %get-tuple-element.32.refs_3_), channel_id=1, source_target_pairs={{0,24},{1,25},{2,26},{3,27},{4,28},{5,29},{6,30},{7,31},{8,16},{9,... | collective-permute-start | bytes 491528 | tf_op jit(solution)/shard_map/ppermute | solution.py:255
  4.9 4.6 %collective-permute-start.4 = (bf16[32,256]{1,0:T(8,128)(2,1)S(1)}, bf16[32,256]{1,0:T(8,128)(2,1)S(1)}, u32[]{:S(2)}, u32[]{:S(2)}) collective-permute-start(bf16[32,256]{1,0:T(8,128)(2,1)S(1)} %get-tuple-element.33.own_virt), channel_id=1, source_target_pairs={{0,4},{1,5},{2,6},{3,7},{4,0},{5,1},{6,2},{7,3},{8,13},{9,12},{10,... | collective-permute-start | bytes 49160 | tf_op jit(solution)/shard_map/ppermute | solution.py:262
  7.8 3.9 %collective-permute-start.3 = (bf16[32,256]{1,0:T(8,128)(2,1)S(1)}, bf16[32,256]{1,0:T(8,128)(2,1)S(1)}, u32[]{:S(2)}, u32[]{:S(2)}) collective-permute-start(bf16[32,256]{1,0:T(8,128)(2,1)S(1)} %get-tuple-element.33.own_virt), channel_id=1, source_target_pairs={{0,1},{1,0},{2,3},{3,2},{4,5},{5,4},{6,7},{7,6},{8,9},{9,8},{10,11... | collective-permute-start | bytes 49160 | tf_op jit(solution)/shard_map/ppermute | solution.py:262
  13.2 14.5 %collective-permute-start.9 = (bf16[64,2304]{1,0:T(8,128)(2,1)S(1)}, bf16[64,2304]{1,0:T(8,128)(2,1)S(1)}, u32[]{:S(2)}, u32[]{:S(2)}) collective-permute-start(bf16[64,2304]{1,0:T(8,128)(2,1)S(1)} %get-tuple-element.38), channel_id=1, source_target_pairs={{0,16},{1,17},{2,18},{3,19},{4,20},{5,21},{6,22},{7,23},{8,24},{9,... | collective-permute-start | bytes 884744 | tf_op jit(solution)/shard_map/ppermute | solution.py:255
  14.9 8.9 %collective-permute-start.5 = (bf16[32,1024]{1,0:T(8,128)(2,1)S(1)}, bf16[32,1024]{1,0:T(8,128)(2,1)S(1)}, u32[]{:S(2)}, u32[]{:S(2)}) collective-permute-start(bf16[32,1024]{1,0:T(8,128)(2,1)S(1)} %get-tuple-element.34), channel_id=1, source_target_pairs={{0,7},{1,6},{2,5},{3,4},{4,3},{5,2},{6,1},{7,0},{8,15},{9,14},{10,... | collective-permute-start | bytes 196616 | tf_op jit(solution)/shard_map/ppermute | solution.py:255
  19.4 7.8 %collective-permute-start.6 = (bf16[32,1024]{1,0:T(8,128)(2,1)S(1)}, bf16[32,1024]{1,0:T(8,128)(2,1)S(1)}, u32[]{:S(2)}, u32[]{:S(2)}) collective-permute-start(bf16[32,1024]{1,0:T(8,128)(2,1)S(1)} %get-tuple-element.35), channel_id=1, source_target_pairs={{0,5},{1,4},{2,7},{3,6},{4,1},{5,0},{6,3},{7,2},{8,13},{9,12},{10,... | collective-permute-start | bytes 196616 | tf_op jit(solution)/shard_map/ppermute | solution.py:255
  19.4 7.8 %collective-permute-start.7 = (bf16[32,1024]{1,0:T(8,128)(2,1)S(1)}, bf16[32,1024]{1,0:T(8,128)(2,1)S(1)}, u32[]{:S(2)}, u32[]{:S(2)}) collective-permute-start(bf16[32,1024]{1,0:T(8,128)(2,1)S(1)} %get-tuple-element.36), channel_id=1, source_target_pairs={{0,6},{1,7},{2,4},{3,5},{4,2},{5,3},{6,0},{7,1},{8,14},{9,15},{10,... | collective-permute-start | bytes 196616 | tf_op jit(solution)/shard_map/ppermute | solution.py:255
  21.3 6.5 %collective-permute-start.8 = (bf16[32,1024]{1,0:T(8,128)(2,1)S(1)}, bf16[32,1024]{1,0:T(8,128)(2,1)S(1)}, u32[]{:S(2)}, u32[]{:S(2)}) collective-permute-start(bf16[32,1024]{1,0:T(8,128)(2,1)S(1)} %get-tuple-element.37), channel_id=1, source_target_pairs={{0,3},{1,2},{2,1},{3,0},{4,7},{5,6},{6,5},{7,4},{8,11},{9,10},{10,... | collective-permute-start | bytes 196616 | tf_op jit(solution)/shard_map/ppermute | solution.py:255
  27.8 4.6 %collective-permute-start.11 = (bf16[64,2304]{1,0:T(8,128)(2,1)S(1)}, bf16[64,2304]{1,0:T(8,128)(2,1)S(1)}, u32[]{:S(2)}, u32[]{:S(2)}) collective-permute-start(bf16[64,2304]{1,0:T(8,128)(2,1)S(1)} %get-tuple-element.44.refs_10_), channel_id=1, source_target_pairs={{0,8},{1,9},{2,10},{3,11},{4,12},{5,13},{6,14},{7,15},{8,0},{9,1},... | collective-permute-start | bytes 884744 | tf_op jit(solution)/shard_map/ppermute | solution.py:255
  27.8 4.6 %collective-permute-start.10 = (bf16[64,2304]{1,0:T(8,128)(2,1)S(1)}, bf16[64,2304]{1,0:T(8,128)(2,1)S(1)}, u32[]{:S(2)}, u32[]{:S(2)}) collective-permute-start(bf16[64,2304]{1,0:T(8,128)(2,1)S(1)} %collective-permute-done.9.refs_7_), channel_id=1, source_target_pairs={{0,8},{1,9},{2,10},{3,11},{4,12},{5,13},{6,14},{7,15},{8,0},{9,1},... | collective-permute-start | bytes 884744 | tf_op jit(solution)/shard_map/ppermute | solution.py:255
  28.3 6.3 %collective-permute-start.12 = (bf16[32,1024]{1,0:T(8,128)(2,1)S(1)}, bf16[32,1024]{1,0:T(8,128)(2,1)S(1)}, u32[]{:S(2)}, u32[]{:S(2)}) collective-permute-start(bf16[32,1024]{1,0:T(8,128)(2,1)S(1)} %get-tuple-element.48), channel_id=1, source_target_pairs={{0,4},{1,5},{2,6},{3,7},{4,0},{5,1},{6,2},{7,3},{8,12},{9,13},{10,... | collective-permute-start | bytes 196616 | tf_op jit(solution)/shard_map/ppermute | solution.py:255
  30.2 4.9 %collective-permute-start.13 = (bf16[32,1024]{1,0:T(8,128)(2,1)S(1)}, bf16[32,1024]{1,0:T(8,128)(2,1)S(1)}, u32[]{:S(2)}, u32[]{:S(2)}) collective-permute-start(bf16[32,1024]{1,0:T(8,128)(2,1)S(1)} %get-tuple-element.50), channel_id=1, source_target_pairs={{0,2},{1,3},{2,0},{3,1},{4,6},{5,7},{6,4},{7,5},{8,10},{9,11},{10,... | collective-permute-start | bytes 196616 | tf_op jit(solution)/shard_map/ppermute | solution.py:255
  31.4 4.3 %collective-permute-start.14 = (bf16[32,1024]{1,0:T(8,128)(2,1)S(1)}, bf16[32,1024]{1,0:T(8,128)(2,1)S(1)}, u32[]{:S(2)}, u32[]{:S(2)}) collective-permute-start(bf16[32,1024]{1,0:T(8,128)(2,1)S(1)} %get-tuple-element.51), channel_id=1, source_target_pairs={{0,1},{1,0},{2,3},{3,2},{4,5},{5,4},{6,7},{7,6},{8,9},{9,8},{10,11... | collective-permute-start | bytes 196616 | tf_op jit(solution)/shard_map/ppermute | solution.py:255
  36.3 3.8 %collective-permute-start.15 = (f32[32,128]{1,0:T(8,128)S(1)}, f32[32,128]{1,0:T(8,128)S(1)}, u32[]{:S(2)}, u32[]{:S(2)}) collective-permute-start(f32[32,128]{1,0:T(8,128)S(1)} %shard_map.58.refs_0_), channel_id=1, source_target_pairs={{0,1},{1,0},{2,3},{3,2},{4,5},{5,4},{6,7},{7,6},{8,9},{9,8},{10,11... | collective-permute-start | bytes 49160 | tf_op jit(solution)/shard_map/ppermute | solution.py:255
  40.1 5.5 %collective-permute-start.18 = (f32[32,128]{1,0:T(8,128)S(1)}, f32[32,128]{1,0:T(8,128)S(1)}, u32[]{:S(2)}, u32[]{:S(2)}) collective-permute-start(f32[32,128]{1,0:T(8,128)S(1)} %shard_map.59), channel_id=1, source_target_pairs={{0,6},{1,7},{2,4},{3,5},{4,2},{5,3},{6,0},{7,1},{8,14},{9,15},{10,... | collective-permute-start | bytes 49160 | tf_op jit(solution)/shard_map/ppermute | solution.py:255
  41.5 4.7 %collective-permute-start.17 = (f32[32,128]{1,0:T(8,128)S(1)}, f32[32,128]{1,0:T(8,128)S(1)}, u32[]{:S(2)}, u32[]{:S(2)}) collective-permute-start(f32[32,128]{1,0:T(8,128)S(1)} %shard_map.59), channel_id=1, source_target_pairs={{0,4},{1,5},{2,6},{3,7},{4,0},{5,1},{6,2},{7,3},{8,12},{9,13},{10,... | collective-permute-start | bytes 49160 | tf_op jit(solution)/shard_map/ppermute | solution.py:255
  42.4 3.9 %collective-permute-start.16 = (f32[32,128]{1,0:T(8,128)S(1)}, f32[32,128]{1,0:T(8,128)S(1)}, u32[]{:S(2)}, u32[]{:S(2)}) collective-permute-start(f32[32,128]{1,0:T(8,128)S(1)} %shard_map.59), channel_id=1, source_target_pairs={{0,2},{1,3},{2,0},{3,1},{4,6},{5,7},{6,4},{7,5},{8,10},{9,11},{10,... | collective-permute-start | bytes 49160 | tf_op jit(solution)/shard_map/ppermute | solution.py:255

commit v9 on v8

--- a/solution.py
+++ b/solution.py
@@ -236,7 +236,7 @@
     if (count.bit_length() - 1) % 2:
         bit, found = 2, [[1]]
     while bit < count:
-        found.append([bit, 2 * bit, 3 * bit])
+        found.append([2 * bit, bit, 3 * bit])
         bit *= 4
     return found
 

time: 47.1 us -> 46.9 us (level)
  no operation moved by 1% of the time
where the time goes in v9:
time: 46.9 us; the launch traced here: 46.8 us
  starting transfers between devices  28.1 us (60%)
  waiting for transfers between devices  13.7 us (29%)
  Pallas kernels  4.42 us (9%)
  other arithmetic  0.61 us (1%)
    ppermute x17, starting transfers between devices, exchange(): lax.ppermute(x, ('split', 'tensor'), [(d, d ^ bits) for d in range(count)])  23.7 us
    ppermute x17, waiting for transfers between devices, exchange(): lax.ppermute(x, ('split', 'tensor'), [(d, d ^ bits) for d in range(count)])  11.3 us
    ppermute x2, starting transfers between devices, fetch(): return lax.ppermute(x, ('split', 'tensor'), pairs)  4.34 us
    ppermute x2, waiting for transfers between devices, fetch(): return lax.ppermute(x, ('split', 'tensor'), pairs)  2.34 us
    pallas_call x1, Pallas kernels, local(): pl.pallas_call(functools.partial(pack_kernel, n_split), out_shape=[jax.Sh...  1.77 us
    pallas_call x1, Pallas kernels, local(): pl.pallas_call(functools.partial(g_kernel, n_split, n_tensor, packed_widt...  1.65 us
  transfers between devices with their start and end apart: 19, of which 11 were waited for; matrix products, arithmetic and copies ran while one was open for 0% of the time, Pallas kernels for 4%

profile of v9, /device:TPU:0, one launch (start us, length us, event | category | flops | bytes accessed | tf_op | source)
XLA Modules:
  0.0 46.8 jit_solution(11604307864233649746)
XLA Ops:
  0.0 1.8 %shard_map.55 = (bf16[32,256]{1,0:T(8,128)(2,1)S(1)}, bf16[64,1280]{1,0:T(8,128)(2,1)S(1)}, bf16[64,4352]{1,0:T(8,128)(2,1)S(1)}, bf16[64,1280]{1,0:T(8,128)(2,1)S(1)}, bf16[64,1280]{1,0:T(8,128)(2,1)S(1)}) custom-call(s32[8,8]{1,0:T(8,128)} %occ_mask_hbm.1, s32[8,8]{1,0:T(8,128)} %virt_mask_hbm.1, bf16[64,32,128]{2,1,0:T(8,128)(2,1)} %b_hbm.1, ...), custom_call_target="tpu_custom_call" | custom-call | tf_op jit(solution)/shard_map/pallas_call | solution.py:265
  1.8 0.5 %collective-permute-start = (bf16[64,4352]{1,0:T(8,128)(2,1)S(1)}, bf16[64,4352]{1,0:T(8,128)(2,1)S(1)}, u32[]{:S(2)}, u32[]{:S(2)}) collective-permute-start(bf16[64,4352]{1,0:T(8,128)(2,1)S(1)} %get-tuple-element.30.refs_1_), channel_id=1, source_target_pairs={{0,8},{1,9},{2,10},{3,11},{4,12},{5,13},{6,14},{7,15},{8,0},{9,1},... | collective-permute-start | bytes 1671176 | tf_op jit(solution)/shard_map/ppermute | solution.py:255
  2.3 2.6 %collective-permute-start.1 = (bf16[64,1280]{1,0:T(8,128)(2,1)S(1)}, bf16[64,1280]{1,0:T(8,128)(2,1)S(1)}, u32[]{:S(2)}, u32[]{:S(2)}) collective-permute-start(bf16[64,1280]{1,0:T(8,128)(2,1)S(1)} %get-tuple-element.31.refs_2_), channel_id=1, source_target_pairs={{0,16},{1,17},{2,18},{3,19},{4,20},{5,21},{6,22},{7,23},{8,24},{9,... | collective-permute-start | bytes 491528 | tf_op jit(solution)/shard_map/ppermute | solution.py:255
  4.9 0.1 collective-permute-start.2
  4.9 2.8 %collective-permute-start.4 = (bf16[32,256]{1,0:T(8,128)(2,1)S(1)}, bf16[32,256]{1,0:T(8,128)(2,1)S(1)}, u32[]{:S(2)}, u32[]{:S(2)}) collective-permute-start(bf16[32,256]{1,0:T(8,128)(2,1)S(1)} %get-tuple-element.33.own_virt), channel_id=1, source_target_pairs={{0,4},{1,5},{2,6},{3,7},{4,0},{5,1},{6,2},{7,3},{8,13},{9,12},{10,... | collective-permute-start | bytes 49160 | tf_op jit(solution)/shard_map/ppermute | solution.py:262
  7.8 1.5 %collective-permute-start.3 = (bf16[32,256]{1,0:T(8,128)(2,1)S(1)}, bf16[32,256]{1,0:T(8,128)(2,1)S(1)}, u32[]{:S(2)}, u32[]{:S(2)}) collective-permute-start(bf16[32,256]{1,0:T(8,128)(2,1)S(1)} %get-tuple-element.33.own_virt), channel_id=1, source_target_pairs={{0,1},{1,0},{2,3},{3,2},{4,5},{5,4},{6,7},{7,6},{8,9},{9,8},{10,11... | collective-permute-start | bytes 49160 | tf_op jit(solution)/shard_map/ppermute | solution.py:262
  9.3 0.3 collective-permute-done.4.refs_8_
  9.6 2.0 %collective-permute-done.3.refs_7_ = bf16[32,256]{1,0:T(8,128)(2,1)S(1)} collective-permute-done((bf16[32,256]{1,0:T(8,128)(2,1)S(1)}, bf16[32,256]{1,0:T(8,128)(2,1)S(1)}, u32[]{:S(2)}, u32[]{:S(2)}) %collective-permute-start.3) | collective-permute-done | bytes 16416 | tf_op jit(solution)/shard_map/ppermute | solution.py:262
  11.6 1.3 %collective-permute-done.2.refs_4_.refs_6_ = bf16[64,1280]{1,0:T(8,128)(2,1)S(1)} collective-permute-done((bf16[64,1280]{1,0:T(8,128)(2,1)S(1)}, bf16[64,1280]{1,0:T(8,128)(2,1)S(1)}, u32[]{:S(2)}, u32[]{:S(2)}) %collective-permute-start.2) | collective-permute-done | bytes 163872 | tf_op jit(solution)/shard_map/ppermute | solution.py:255
  12.9 0.3 shard_map.56
  13.2 1.6 %collective-permute-start.9 = (bf16[64,2304]{1,0:T(8,128)(2,1)S(1)}, bf16[64,2304]{1,0:T(8,128)(2,1)S(1)}, u32[]{:S(2)}, u32[]{:S(2)}) collective-permute-start(bf16[64,2304]{1,0:T(8,128)(2,1)S(1)} %get-tuple-element.38), channel_id=1, source_target_pairs={{0,16},{1,17},{2,18},{3,19},{4,20},{5,21},{6,22},{7,23},{8,24},{9,... | collective-permute-start | bytes 884744 | tf_op jit(solution)/shard_map/ppermute | solution.py:255
  14.9 4.6 %collective-permute-start.5 = (bf16[32,1024]{1,0:T(8,128)(2,1)S(1)}, bf16[32,1024]{1,0:T(8,128)(2,1)S(1)}, u32[]{:S(2)}, u32[]{:S(2)}) collective-permute-start(bf16[32,1024]{1,0:T(8,128)(2,1)S(1)} %get-tuple-element.34), channel_id=1, source_target_pairs={{0,7},{1,6},{2,5},{3,4},{4,3},{5,2},{6,1},{7,0},{8,15},{9,14},{10,... | collective-permute-start | bytes 196616 | tf_op jit(solution)/shard_map/ppermute | solution.py:255
  19.4 1.9 %collective-permute-start.7 = (bf16[32,1024]{1,0:T(8,128)(2,1)S(1)}, bf16[32,1024]{1,0:T(8,128)(2,1)S(1)}, u32[]{:S(2)}, u32[]{:S(2)}) collective-permute-start(bf16[32,1024]{1,0:T(8,128)(2,1)S(1)} %get-tuple-element.36), channel_id=1, source_target_pairs={{0,6},{1,7},{2,4},{3,5},{4,2},{5,3},{6,0},{7,1},{8,14},{9,15},{10,... | collective-permute-start | bytes 196616 | tf_op jit(solution)/shard_map/ppermute | solution.py:255
  21.3 2.5 %collective-permute-start.8 = (bf16[32,1024]{1,0:T(8,128)(2,1)S(1)}, bf16[32,1024]{1,0:T(8,128)(2,1)S(1)}, u32[]{:S(2)}, u32[]{:S(2)}) collective-permute-start(bf16[32,1024]{1,0:T(8,128)(2,1)S(1)} %get-tuple-element.37), channel_id=1, source_target_pairs={{0,3},{1,2},{2,1},{3,0},{4,7},{5,6},{6,5},{7,4},{8,11},{9,10},{10,... | collective-permute-start | bytes 196616 | tf_op jit(solution)/shard_map/ppermute | solution.py:255
  23.8 3.4 %collective-permute-done.6.refs_2_ = bf16[32,1024]{1,0:T(8,128)(2,1)S(1)} collective-permute-done((bf16[32,1024]{1,0:T(8,128)(2,1)S(1)}, bf16[32,1024]{1,0:T(8,128)(2,1)S(1)}, u32[]{:S(2)}, u32[]{:S(2)}) %collective-permute-start.6) | collective-permute-done | bytes 65568 | tf_op jit(solution)/shard_map/ppermute | solution.py:255
  27.2 0.6 %collective-permute-done.8.refs_4_ = bf16[32,1024]{1,0:T(8,128)(2,1)S(1)} collective-permute-done((bf16[32,1024]{1,0:T(8,128)(2,1)S(1)}, bf16[32,1024]{1,0:T(8,128)(2,1)S(1)}, u32[]{:S(2)}, u32[]{:S(2)}) %collective-permute-start.8) | collective-permute-done | bytes 65568 | tf_op jit(solution)/shard_map/ppermute | solution.py:255
  27.8 0.5 %collective-permute-start.10 = (bf16[64,2304]{1,0:T(8,128)(2,1)S(1)}, bf16[64,2304]{1,0:T(8,128)(2,1)S(1)}, u32[]{:S(2)}, u32[]{:S(2)}) collective-permute-start(bf16[64,2304]{1,0:T(8,128)(2,1)S(1)} %collective-permute-done.9.refs_7_), channel_id=1, source_target_pairs={{0,8},{1,9},{2,10},{3,11},{4,12},{5,13},{6,14},{7,15},{8,0},{9,1},... | collective-permute-start | bytes 884744 | tf_op jit(solution)/shard_map/ppermute | solution.py:255
  28.3 1.9 %collective-permute-start.12 = (bf16[32,1024]{1,0:T(8,128)(2,1)S(1)}, bf16[32,1024]{1,0:T(8,128)(2,1)S(1)}, u32[]{:S(2)}, u32[]{:S(2)}) collective-permute-start(bf16[32,1024]{1,0:T(8,128)(2,1)S(1)} %get-tuple-element.48), channel_id=1, source_target_pairs={{0,4},{1,5},{2,6},{3,7},{4,0},{5,1},{6,2},{7,3},{8,12},{9,13},{10,... | collective-permute-start | bytes 196616 | tf_op jit(solution)/shard_map/ppermute | solution.py:255
  30.2 1.1 %collective-permute-start.13 = (bf16[32,1024]{1,0:T(8,128)(2,1)S(1)}, bf16[32,1024]{1,0:T(8,128)(2,1)S(1)}, u32[]{:S(2)}, u32[]{:S(2)}) collective-permute-start(bf16[32,1024]{1,0:T(8,128)(2,1)S(1)} %get-tuple-element.50), channel_id=1, source_target_pairs={{0,2},{1,3},{2,0},{3,1},{4,6},{5,7},{6,4},{7,5},{8,10},{9,11},{10,... | collective-permute-start | bytes 196616 | tf_op jit(solution)/shard_map/ppermute | solution.py:255
  31.4 1.0 %collective-permute-start.14 = (bf16[32,1024]{1,0:T(8,128)(2,1)S(1)}, bf16[32,1024]{1,0:T(8,128)(2,1)S(1)}, u32[]{:S(2)}, u32[]{:S(2)}) collective-permute-start(bf16[32,1024]{1,0:T(8,128)(2,1)S(1)} %get-tuple-element.51), channel_id=1, source_target_pairs={{0,1},{1,0},{2,3},{3,2},{4,5},{5,4},{6,7},{7,6},{8,9},{9,8},{10,11... | collective-permute-start | bytes 196616 | tf_op jit(solution)/shard_map/ppermute | solution.py:255
  32.4 1.6 %shard_map.57.g_ref = bf16[32,256,128]{2,1,0:T(8,128)(2,1)S(1)} custom-call(bf16[64,1280]{1,0:T(8,128)(2,1)S(1)} %get-tuple-element.29.refs_0_, bf16[64,4352]{1,0:T(8,128)(2,1)S(1)} %get-tuple-element.30.refs_1_, bf16[64,1280]{1,0:T(8,128)(2,1)S(1)} %get-tuple-element.31.refs_2_, bf16[64,1280]{1,0:T(8,128)(2,1)S(1)} %get-tuple-element.32.refs_3_, ...), custom_call_target="tpu_custom_call" | custom-call | tf_op jit(solution)/shard_map/pallas_call | solution.py:321
  34.0 0.6 %collective-permute-done.12.refs_3_ = bf16[32,1024]{1,0:T(8,128)(2,1)S(1)} collective-permute-done((bf16[32,1024]{1,0:T(8,128)(2,1)S(1)}, bf16[32,1024]{1,0:T(8,128)(2,1)S(1)}, u32[]{:S(2)}, u32[]{:S(2)}) %collective-permute-start.12) | collective-permute-done | bytes 65568 | tf_op jit(solution)/shard_map/ppermute | solution.py:255
  34.6 0.4 collective-permute-done.13.refs_5_
  35.1 0.6 %collective-permute-done.14.refs_6_ = bf16[32,1024]{1,0:T(8,128)(2,1)S(1)} collective-permute-done((bf16[32,1024]{1,0:T(8,128)(2,1)S(1)}, bf16[32,1024]{1,0:T(8,128)(2,1)S(1)}, u32[]{:S(2)}, u32[]{:S(2)}) %collective-permute-start.14) | collective-permute-done | bytes 65568 | tf_op jit(solution)/shard_map/ppermute | solution.py:255
  35.6 0.7 %shard_map.58.refs_0_ = f32[32,128]{1,0:T(8,128)S(1)} custom-call(bf16[32,256,128]{2,1,0:T(8,128)(2,1)S(1)} %shard_map.57.g_ref, bf16[32,1024]{1,0:T(8,128)(2,1)S(1)} %collective-permute-done.5.refs_0_, bf16[32,1024]{1,0:T(8,128)(2,1)S(1)} %collective-permute-done.7.refs_1_, bf16[32,1024]{1,0:T(8,128)(2,1)S(1)} %collective-permute-done.6.refs_2_, ...), custom_call_target="tpu_custom_call" | custom-call | tf_op jit(solution)/shard_map/pallas_call | solution.py:330
  36.3 1.0 %collective-permute-start.15 = (f32[32,128]{1,0:T(8,128)S(1)}, f32[32,128]{1,0:T(8,128)S(1)}, u32[]{:S(2)}, u32[]{:S(2)}) collective-permute-start(f32[32,128]{1,0:T(8,128)S(1)} %shard_map.58.refs_0_), channel_id=1, source_target_pairs={{0,1},{1,0},{2,3},{3,2},{4,5},{5,4},{6,7},{7,6},{8,9},{9,8},{10,11... | collective-permute-start | bytes 49160 | tf_op jit(solution)/shard_map/ppermute | solution.py:255
  37.3 2.7 %collective-permute-done.15.refs_1_ = f32[32,128]{1,0:T(8,128)S(1)} collective-permute-done((f32[32,128]{1,0:T(8,128)S(1)}, f32[32,128]{1,0:T(8,128)S(1)}, u32[]{:S(2)}, u32[]{:S(2)}) %collective-permute-start.15) | collective-permute-done | bytes 16416 | tf_op jit(solution)/shard_map/ppermute | solution.py:255
  40.1 1.5 %collective-permute-start.18 = (f32[32,128]{1,0:T(8,128)S(1)}, f32[32,128]{1,0:T(8,128)S(1)}, u32[]{:S(2)}, u32[]{:S(2)}) collective-permute-start(f32[32,128]{1,0:T(8,128)S(1)} %shard_map.59), channel_id=1, source_target_pairs={{0,6},{1,7},{2,4},{3,5},{4,2},{5,3},{6,0},{7,1},{8,14},{9,15},{10,... | collective-permute-start | bytes 49160 | tf_op jit(solution)/shard_map/ppermute | solution.py:255
  41.5 2.9 %collective-permute-start.16 = (f32[32,128]{1,0:T(8,128)S(1)}, f32[32,128]{1,0:T(8,128)S(1)}, u32[]{:S(2)}, u32[]{:S(2)}) collective-permute-start(f32[32,128]{1,0:T(8,128)S(1)} %shard_map.59), channel_id=1, source_target_pairs={{0,4},{1,5},{2,6},{3,7},{4,0},{5,1},{6,2},{7,3},{8,12},{9,13},{10,... | collective-permute-start | bytes 49160 | tf_op jit(solution)/shard_map/ppermute | solution.py:255
  44.4 1.1 %collective-permute-done.18 = f32[32,128]{1,0:T(8,128)S(1)} collective-permute-done((f32[32,128]{1,0:T(8,128)S(1)}, f32[32,128]{1,0:T(8,128)S(1)}, u32[]{:S(2)}, u32[]{:S(2)}) %collective-permute-start.18) | collective-permute-done | bytes 16416 | tf_op jit(solution)/shard_map/ppermute | solution.py:255
  45.6 0.6 %collective-permute-done.16 = f32[32,128]{1,0:T(8,128)S(1)} collective-permute-done((f32[32,128]{1,0:T(8,128)S(1)}, f32[32,128]{1,0:T(8,128)S(1)}, u32[]{:S(2)}, u32[]{:S(2)}) %collective-permute-start.16) | collective-permute-done | bytes 16416 | tf_op jit(solution)/shard_map/ppermute | solution.py:255
  46.2 0.6 %add_add_fusion = f32[32,128]{1,0:T(8,128)} fusion(f32[32,128]{1,0:T(8,128)S(1)} %collective-permute-done.18, f32[32,128]{1,0:T(8,128)S(1)} %collective-permute-done.17, f32[32,128]{1,0:T(8,128)S(1)} %shard_map.59, f32[32,128]{1,0:T(8,128)S(1)} %collective-permute-done.16), kind=kLoop, calls=%fused_computation | loop fusion | flops 12288 | bytes 81920 | tf_op jit(solution)/shard_map/add | solution.py:348
  (12 shorter events, 0.0 us)
Async XLA Ops:
  1.8 11.1 %collective-permute-start = (bf16[64,4352]{1,0:T(8,128)(2,1)S(1)}, bf16[64,4352]{1,0:T(8,128)(2,1)S(1)}, u32[]{:S(2)}, u32[]{:S(2)}) collective-permute-start(bf16[64,4352]{1,0:T(8,128)(2,1)S(1)} %get-tuple-element.30.refs_1_), channel_id=1, source_target_pairs={{0,8},{1,9},{2,10},{3,11},{4,12},{5,13},{6,14},{7,15},{8,0},{9,1},... | collective-permute-start | bytes 1671176 | tf_op jit(solution)/shard_map/ppermute | solution.py:255
  2.3 9.3 %collective-permute-start.1 = (bf16[64,1280]{1,0:T(8,128)(2,1)S(1)}, bf16[64,1280]{1,0:T(8,128)(2,1)S(1)}, u32[]{:S(2)}, u32[]{:S(2)}) collective-permute-start(bf16[64,1280]{1,0:T(8,128)(2,1)S(1)} %get-tuple-element.31.refs_2_), channel_id=1, source_target_pairs={{0,16},{1,17},{2,18},{3,19},{4,20},{5,21},{6,22},{7,23},{8,24},{9,... | collective-permute-start | bytes 491528 | tf_op jit(solution)/shard_map/ppermute | solution.py:255
  4.9 8.0 %collective-permute-start.2 = (bf16[64,1280]{1,0:T(8,128)(2,1)S(1)}, bf16[64,1280]{1,0:T(8,128)(2,1)S(1)}, u32[]{:S(2)}, u32[]{:S(2)}) collective-permute-start(bf16[64,1280]{1,0:T(8,128)(2,1)S(1)} %get-tuple-element.32.refs_3_), channel_id=1, source_target_pairs={{0,24},{1,25},{2,26},{3,27},{4,28},{5,29},{6,30},{7,31},{8,16},{9,... | collective-permute-start | bytes 491528 | tf_op jit(solution)/shard_map/ppermute | solution.py:255
  4.9 4.6 %collective-permute-start.4 = (bf16[32,256]{1,0:T(8,128)(2,1)S(1)}, bf16[32,256]{1,0:T(8,128)(2,1)S(1)}, u32[]{:S(2)}, u32[]{:S(2)}) collective-permute-start(bf16[32,256]{1,0:T(8,128)(2,1)S(1)} %get-tuple-element.33.own_virt), channel_id=1, source_target_pairs={{0,4},{1,5},{2,6},{3,7},{4,0},{5,1},{6,2},{7,3},{8,13},{9,12},{10,... | collective-permute-start | bytes 49160 | tf_op jit(solution)/shard_map/ppermute | solution.py:262
  7.8 3.9 %collective-permute-start.3 = (bf16[32,256]{1,0:T(8,128)(2,1)S(1)}, bf16[32,256]{1,0:T(8,128)(2,1)S(1)}, u32[]{:S(2)}, u32[]{:S(2)}) collective-permute-start(bf16[32,256]{1,0:T(8,128)(2,1)S(1)} %get-tuple-element.33.own_virt), channel_id=1, source_target_pairs={{0,1},{1,0},{2,3},{3,2},{4,5},{5,4},{6,7},{7,6},{8,9},{9,8},{10,11... | collective-permute-start | bytes 49160 | tf_op jit(solution)/shard_map/ppermute | solution.py:262
  13.2 14.5 %collective-permute-start.9 = (bf16[64,2304]{1,0:T(8,128)(2,1)S(1)}, bf16[64,2304]{1,0:T(8,128)(2,1)S(1)}, u32[]{:S(2)}, u32[]{:S(2)}) collective-permute-start(bf16[64,2304]{1,0:T(8,128)(2,1)S(1)} %get-tuple-element.38), channel_id=1, source_target_pairs={{0,16},{1,17},{2,18},{3,19},{4,20},{5,21},{6,22},{7,23},{8,24},{9,... | collective-permute-start | bytes 884744 | tf_op jit(solution)/shard_map/ppermute | solution.py:255
  14.9 8.9 %collective-permute-start.5 = (bf16[32,1024]{1,0:T(8,128)(2,1)S(1)}, bf16[32,1024]{1,0:T(8,128)(2,1)S(1)}, u32[]{:S(2)}, u32[]{:S(2)}) collective-permute-start(bf16[32,1024]{1,0:T(8,128)(2,1)S(1)} %get-tuple-element.34), channel_id=1, source_target_pairs={{0,7},{1,6},{2,5},{3,4},{4,3},{5,2},{6,1},{7,0},{8,15},{9,14},{10,... | collective-permute-start | bytes 196616 | tf_op jit(solution)/shard_map/ppermute | solution.py:255
  19.4 7.8 %collective-permute-start.6 = (bf16[32,1024]{1,0:T(8,128)(2,1)S(1)}, bf16[32,1024]{1,0:T(8,128)(2,1)S(1)}, u32[]{:S(2)}, u32[]{:S(2)}) collective-permute-start(bf16[32,1024]{1,0:T(8,128)(2,1)S(1)} %get-tuple-element.35), channel_id=1, source_target_pairs={{0,5},{1,4},{2,7},{3,6},{4,1},{5,0},{6,3},{7,2},{8,13},{9,12},{10,... | collective-permute-start | bytes 196616 | tf_op jit(solution)/shard_map/ppermute | solution.py:255
  19.4 7.8 %collective-permute-start.7 = (bf16[32,1024]{1,0:T(8,128)(2,1)S(1)}, bf16[32,1024]{1,0:T(8,128)(2,1)S(1)}, u32[]{:S(2)}, u32[]{:S(2)}) collective-permute-start(bf16[32,1024]{1,0:T(8,128)(2,1)S(1)} %get-tuple-element.36), channel_id=1, source_target_pairs={{0,6},{1,7},{2,4},{3,5},{4,2},{5,3},{6,0},{7,1},{8,14},{9,15},{10,... | collective-permute-start | bytes 196616 | tf_op jit(solution)/shard_map/ppermute | solution.py:255
  21.3 6.5 %collective-permute-start.8 = (bf16[32,1024]{1,0:T(8,128)(2,1)S(1)}, bf16[32,1024]{1,0:T(8,128)(2,1)S(1)}, u32[]{:S(2)}, u32[]{:S(2)}) collective-permute-start(bf16[32,1024]{1,0:T(8,128)(2,1)S(1)} %get-tuple-element.37), channel_id=1, source_target_pairs={{0,3},{1,2},{2,1},{3,0},{4,7},{5,6},{6,5},{7,4},{8,11},{9,10},{10,... | collective-permute-start | bytes 196616 | tf_op jit(solution)/shard_map/ppermute | solution.py:255
  27.8 4.6 %collective-permute-start.11 = (bf16[64,2304]{1,0:T(8,128)(2,1)S(1)}, bf16[64,2304]{1,0:T(8,128)(2,1)S(1)}, u32[]{:S(2)}, u32[]{:S(2)}) collective-permute-start(bf16[64,2304]{1,0:T(8,128)(2,1)S(1)} %get-tuple-element.44.refs_10_), channel_id=1, source_target_pairs={{0,8},{1,9},{2,10},{3,11},{4,12},{5,13},{6,14},{7,15},{8,0},{9,1},... | collective-permute-start | bytes 884744 | tf_op jit(solution)/shard_map/ppermute | solution.py:255
  27.8 4.6 %collective-permute-start.10 = (bf16[64,2304]{1,0:T(8,128)(2,1)S(1)}, bf16[64,2304]{1,0:T(8,128)(2,1)S(1)}, u32[]{:S(2)}, u32[]{:S(2)}) collective-permute-start(bf16[64,2304]{1,0:T(8,128)(2,1)S(1)} %collective-permute-done.9.refs_7_), channel_id=1, source_target_pairs={{0,8},{1,9},{2,10},{3,11},{4,12},{5,13},{6,14},{7,15},{8,0},{9,1},... | collective-permute-start | bytes 884744 | tf_op jit(solution)/shard_map/ppermute | solution.py:255
  28.3 6.3 %collective-permute-start.12 = (bf16[32,1024]{1,0:T(8,128)(2,1)S(1)}, bf16[32,1024]{1,0:T(8,128)(2,1)S(1)}, u32[]{:S(2)}, u32[]{:S(2)}) collective-permute-start(bf16[32,1024]{1,0:T(8,128)(2,1)S(1)} %get-tuple-element.48), channel_id=1, source_target_pairs={{0,4},{1,5},{2,6},{3,7},{4,0},{5,1},{6,2},{7,3},{8,12},{9,13},{10,... | collective-permute-start | bytes 196616 | tf_op jit(solution)/shard_map/ppermute | solution.py:255
  30.2 4.9 %collective-permute-start.13 = (bf16[32,1024]{1,0:T(8,128)(2,1)S(1)}, bf16[32,1024]{1,0:T(8,128)(2,1)S(1)}, u32[]{:S(2)}, u32[]{:S(2)}) collective-permute-start(bf16[32,1024]{1,0:T(8,128)(2,1)S(1)} %get-tuple-element.50), channel_id=1, source_target_pairs={{0,2},{1,3},{2,0},{3,1},{4,6},{5,7},{6,4},{7,5},{8,10},{9,11},{10,... | collective-permute-start | bytes 196616 | tf_op jit(solution)/shard_map/ppermute | solution.py:255
  31.4 4.3 %collective-permute-start.14 = (bf16[32,1024]{1,0:T(8,128)(2,1)S(1)}, bf16[32,1024]{1,0:T(8,128)(2,1)S(1)}, u32[]{:S(2)}, u32[]{:S(2)}) collective-permute-start(bf16[32,1024]{1,0:T(8,128)(2,1)S(1)} %get-tuple-element.51), channel_id=1, source_target_pairs={{0,1},{1,0},{2,3},{3,2},{4,5},{5,4},{6,7},{7,6},{8,9},{9,8},{10,11... | collective-permute-start | bytes 196616 | tf_op jit(solution)/shard_map/ppermute | solution.py:255
  36.3 3.8 %collective-permute-start.15 = (f32[32,128]{1,0:T(8,128)S(1)}, f32[32,128]{1,0:T(8,128)S(1)}, u32[]{:S(2)}, u32[]{:S(2)}) collective-permute-start(f32[32,128]{1,0:T(8,128)S(1)} %shard_map.58.refs_0_), channel_id=1, source_target_pairs={{0,1},{1,0},{2,3},{3,2},{4,5},{5,4},{6,7},{7,6},{8,9},{9,8},{10,11... | collective-permute-start | bytes 49160 | tf_op jit(solution)/shard_map/ppermute | solution.py:255
  40.1 5.5 %collective-permute-start.18 = (f32[32,128]{1,0:T(8,128)S(1)}, f32[32,128]{1,0:T(8,128)S(1)}, u32[]{:S(2)}, u32[]{:S(2)}) collective-permute-start(f32[32,128]{1,0:T(8,128)S(1)} %shard_map.59), channel_id=1, source_target_pairs={{0,6},{1,7},{2,4},{3,5},{4,2},{5,3},{6,0},{7,1},{8,14},{9,15},{10,... | collective-permute-start | bytes 49160 | tf_op jit(solution)/shard_map/ppermute | solution.py:255
  41.5 4.1 %collective-permute-start.17 = (f32[32,128]{1,0:T(8,128)S(1)}, f32[32,128]{1,0:T(8,128)S(1)}, u32[]{:S(2)}, u32[]{:S(2)}) collective-permute-start(f32[32,128]{1,0:T(8,128)S(1)} %shard_map.59), channel_id=1, source_target_pairs={{0,2},{1,3},{2,0},{3,1},{4,6},{5,7},{6,4},{7,5},{8,10},{9,11},{10,... | collective-permute-start | bytes 49160 | tf_op jit(solution)/shard_map/ppermute | solution.py:255
  41.5 4.6 %collective-permute-start.16 = (f32[32,128]{1,0:T(8,128)S(1)}, f32[32,128]{1,0:T(8,128)S(1)}, u32[]{:S(2)}, u32[]{:S(2)}) collective-permute-start(f32[32,128]{1,0:T(8,128)S(1)} %shard_map.59), channel_id=1, source_target_pairs={{0,4},{1,5},{2,6},{3,7},{4,0},{5,1},{6,2},{7,3},{8,12},{9,13},{10,... | collective-permute-start | bytes 49160 | tf_op jit(solution)/shard_map/ppermute | solution.py:255
